TPU v7x, 512 devices: a whole 4x4x16 slice. The times are simulated.
512 devices in a mesh: grp: 16 (over z), ty: 8 (over x, core), tx: 4 (over y).
Axes of the slice: x: 4, y: 4, z: 16, core: 2. Of those that a mesh axis runs over, the one named last changes fastest.
Arguments:
- images: float32 [4, 3, 8192, 512], P(None, None, ('grp', 'ty'), 'tx'), parts along dimension 2, may hold values from -16 to 16
- gains: float32 [4, 3], replicated, may hold values from 0.5 to 2
- labels: int32 [8192, 512], P(('grp', 'ty'), 'tx'), parts along dimension 0, may hold values from 0 to 3, as said below
Outputs:
- blended: float32 [3, 8192, 512], P(None, ('grp', 'ty'), 'tx'), parts along dimension 1
There are 16 independent parts, one for each index of `grp`. A program takes and returns all parts, laid end to end along the dimension named above; an argument that names none is the same for every part. Nothing has to cross between parts.
Inputs may be any that keep to these rules, and one draw needn't show every extreme that they name: labels are constant on aligned 8 x 8 blocks of pixels.
All inputs are finite; a program needn't handle non-finite values.
Results may differ from a plain program's by a relative error of at most 0.0001.
Values sent between devices are 32-bit elements; how exact they have to be, the bound alone decides.
No kernel may reach another device: no remote copies, remote signals or barrier semaphores. Data moves between devices by JAX's collectives and lax.ppermute only.
A program may use at most 64 MiB of HBM per device.

v0:
```python
import jax
import jax.numpy as jnp
from jax import lax
from jax.sharding import PartitionSpec as P

LEVELS = 6


TAPS = (0.0625, 0.25, 0.375, 0.25, 0.0625)


def padded_2(value, sides, width):
    for axis, dim in sides:
        size, length = (lax.axis_size(axis), value.shape[dim])
        up = [(i, (i + 1) % size) for i in range(size - 1)]
        down = [(j, i) for i, j in up]
        last = lax.slice_in_dim(value, length - width, length, axis=dim)
        leading = lax.slice_in_dim(value, 0, width, axis=dim)
        before = lax.ppermute(last, axis, up)
        after = lax.ppermute(leading, axis, down)
        value = jnp.concatenate([before, value, after], axis=dim)
    return value


def reduce_level(padded):
    height = (padded.shape[1] - 4) // 2
    width = (padded.shape[2] - 4) // 2
    across = TAPS[0] * padded[:, 0 : 2 * height : 2, :]
    for offset in range(1, 5):
        across = across + TAPS[offset] * padded[:, offset : offset + 2 * height : 2, :]
    result = TAPS[0] * across[:, :, 0 : 2 * width : 2]
    for offset in range(1, 5):
        result = result + TAPS[offset] * across[:, :, offset : offset + 2 * width : 2]
    return result


def expand_level(padded):
    channels = padded.shape[0]
    height = padded.shape[1] - 2
    width = padded.shape[2] - 2
    centre = padded[:, 1:-1, :]
    below = padded[:, :-2, :]
    above = padded[:, 2:, :]
    even_rows = (6.0 * centre + below + above) * 0.125
    odd_rows = (centre + above) * 0.5
    tall = jnp.stack([even_rows, odd_rows], axis=2).reshape(channels, 2 * height, width + 2)
    centre = tall[:, :, 1:-1]
    below = tall[:, :, :-2]
    above = tall[:, :, 2:]
    even_cols = (6.0 * centre + below + above) * 0.125
    odd_cols = (centre + above) * 0.5
    return jnp.stack([even_cols, odd_cols], axis=3).reshape(channels, 2 * height, 2 * width)


def blend_bands(masks, laplace):
    planes = laplace.reshape(masks.shape[0], -1, laplace.shape[1], laplace.shape[2])
    return jnp.sum(masks[:, None] * planes, axis=0)


def shards(images, gains, labels):
    exposures, bands, height, width = images.shape
    inner = exposures * bands
    gained = (images * gains[:, :, None, None]).reshape(inner, height, width)
    masks = (labels[None] == jnp.arange(exposures, dtype=jnp.int32)[:, None, None]).astype(
        jnp.float32
    )
    level_zero = jnp.concatenate([gained, masks], 0)
    fine_levels = []
    fine_halos = []
    current = level_zero
    for step in range(2):
        padded = padded_2(current, (("ty", 1), ("tx", 2)), 2)
        fine_halos.append(padded)
        current = reduce_level(padded)
        fine_levels.append(current)
    level_one, level_two = fine_levels
    rim_one = fine_halos[1][:inner, 1:-1, 1:-1]
    band_zero = blend_bands(masks, gained - expand_level(rim_one))
    gauss = [level_two]
    rims = []
    for step in range(LEVELS - 2):
        padded = padded_2(gauss[-1], (("ty", 1), ("tx", 2)), 2)
        rims.append(padded[:inner, 1:-1, 1:-1])
        gauss.append(reduce_level(padded))
    rims.append(padded_2(gauss[-1][:inner], (("ty", 1), ("tx", 2)), 1))
    rim_two = rims[0]
    collapsed = blend_bands(gauss[-1][inner:], gauss[-1][:inner])
    for index in range(len(gauss) - 2, -1, -1):
        laplace = gauss[index][:inner] - expand_level(rims[index + 1])
        spread = padded_2(collapsed, (("ty", 1), ("tx", 2)), 1)
        collapsed = blend_bands(gauss[index][inner:], laplace) + expand_level(spread)
    band_one = blend_bands(level_one[inner:], level_one[:inner] - expand_level(rim_two))
    for band in (band_one, band_zero):
        spread = padded_2(collapsed, (("ty", 1), ("tx", 2)), 1)
        collapsed = band + expand_level(spread)
    return collapsed


def solution(mesh):
    placed = (P(None, None, ("grp", "ty"), "tx"), P(), P(("grp", "ty"), "tx"))
    return jax.shard_map(
        shards, mesh=mesh, in_specs=placed, out_specs=P(None, ("grp", "ty"), "tx"), check_vma=False
    )
```

profile of v0, /device:TPU:1, one launch (start us, length us, event | category | flops | bytes accessed | tf_op | source)
XLA Modules:
  0.0 277.2 jit_solution(7388561087323777467)
XLA Ops:
  2.0 8.8 %collective-permute-start.1 = (f32[16,2,128]{2,0,1:T(8,128)S(1)}, f32[16,2,128]{2,0,1:T(8,128)S(1)}, u32[]{:S(2)}, u32[]{:S(2)}) collective-permute-start(f32[16,2,128]{2,0,1:T(8,128)S(1)} %copy.472), channel_id=1, source_target_pairs={{4,0},{8,4},{12,8},{16,12},{20,16},{24,20},{28,24},{5,1},{9,5},{13... | collective-permute-start | bytes 49160 | tf_op jit(solution)/shard_map/ppermute | solution.py:20
  16.1 4.0 %collective-permute-start.2 = (f32[16,68,2]{1,0,2:T(8,128)S(1)}, f32[16,68,2]{1,0,2:T(8,128)S(1)}, u32[]{:S(2)}, u32[]{:S(2)}) collective-permute-start(f32[16,68,2]{1,0,2:T(8,128)S(1)} %copy.413), channel_id=1, source_target_pairs={{0,1},{1,2},{2,3},{4,5},{5,6},{6,7},{8,9},{9,10},{10,11},{12,13},{... | collective-permute-start | bytes 26120 | tf_op jit(solution)/shard_map/ppermute | solution.py:19
  22.8 9.7 %slice.604 = f32[16,32,132]{1,2,0:T(8,128)S(1)} slice(f32[16,68,132]{1,2,0:T(8,128)S(1)} %pad_maximum_fusion), slice={[0:16:1], [4:68:2], [0:132:1]} | slice | bytes 540672 | tf_op jit(solution)/shard_map/slice | solution.py:30
  32.5 9.7 %slice.603 = f32[16,32,132]{1,2,0:T(8,128)S(1)} slice(f32[16,68,132]{1,2,0:T(8,128)S(1)} %pad_maximum_fusion), slice={[0:16:1], [3:67:2], [0:132:1]} | slice | bytes 540672 | tf_op jit(solution)/shard_map/slice | solution.py:30
  42.3 10.2 %slice.602 = f32[16,32,132]{1,2,0:T(8,128)} slice(f32[16,68,132]{1,2,0:T(8,128)S(1)} %pad_maximum_fusion), slice={[0:16:1], [2:66:2], [0:132:1]} | slice | bytes 540672 | tf_op jit(solution)/shard_map/slice | solution.py:30
  52.5 10.2 %slice.601 = f32[16,32,132]{1,2,0:T(8,128)} slice(f32[16,68,132]{1,2,0:T(8,128)S(1)} %pad_maximum_fusion), slice={[0:16:1], [1:65:2], [0:132:1]} | slice | bytes 540672 | tf_op jit(solution)/shard_map/slice | solution.py:30
  62.8 10.0 %slice.600 = f32[16,32,132]{1,2,0:T(8,128)} slice(f32[16,68,132]{1,2,0:T(8,128)S(1)} %pad_maximum_fusion), slice={[0:16:1], [0:64:2], [0:132:1]} | slice | bytes 540672 | tf_op jit(solution)/shard_map/slice | solution.py:28
  78.9 5.0 %collective-permute-start.4 = (f32[16,2,64]{1,2,0:T(8,128)S(1)}, f32[16,2,64]{1,2,0:T(8,128)S(1)}, u32[]{:S(2)}, u32[]{:S(2)}) collective-permute-start(f32[16,2,64]{1,2,0:T(8,128)S(1)} %get-tuple-element.7), channel_id=1, source_target_pairs={{0,4},{4,8},{8,12},{12,16},{16,20},{20,24},{24,28},{1,5},{5,9},{9,... | collective-permute-start | bytes 24584 | tf_op jit(solution)/shard_map/ppermute | solution.py:19
  86.1 4.0 %collective-permute-done.4 = f32[16,2,64]{1,2,0:T(8,128)S(1)} collective-permute-done((f32[16,2,64]{1,2,0:T(8,128)S(1)}, f32[16,2,64]{1,2,0:T(8,128)S(1)}, u32[]{:S(2)}, u32[]{:S(2)}) %collective-permute-start.4) | collective-permute-done | bytes 8224 | tf_op jit(solution)/shard_map/ppermute | solution.py:19
  90.2 4.2 %collective-permute-done.5 = f32[16,2,64]{1,2,0:T(8,128)S(1)} collective-permute-done((f32[16,2,64]{1,2,0:T(8,128)S(1)}, f32[16,2,64]{1,2,0:T(8,128)S(1)}, u32[]{:S(2)}, u32[]{:S(2)}) %collective-permute-start.5) | collective-permute-done | bytes 8224 | tf_op jit(solution)/shard_map/ppermute | solution.py:20
  94.8 4.2 %collective-permute-start.6 = (f32[16,36,2]{2,0,1:T(8,128)S(1)}, f32[16,36,2]{2,0,1:T(8,128)S(1)}, u32[]{:S(2)}, u32[]{:S(2)}) collective-permute-start(f32[16,36,2]{2,0,1:T(8,128)S(1)} %get-tuple-element.24), channel_id=1, source_target_pairs={{0,1},{1,2},{2,3},{4,5},{5,6},{6,7},{8,9},{9,10},{10,11},{12,13},{... | collective-permute-start | bytes 13832 | tf_op jit(solution)/shard_map/ppermute | solution.py:19
  102.7 3.8 %collective-permute-done.7 = f32[16,36,2]{2,0,1:T(8,128)S(1)} collective-permute-done((f32[16,36,2]{2,0,1:T(8,128)S(1)}, f32[16,36,2]{2,0,1:T(8,128)S(1)}, u32[]{:S(2)}, u32[]{:S(2)}) %collective-permute-start.7) | collective-permute-done | bytes 4640 | tf_op jit(solution)/shard_map/ppermute | solution.py:20
  129.1 3.5 %collective-permute-start.12 = (f32[16,2,16]{0,2,1:T(8,128)S(1)}, f32[16,2,16]{0,2,1:T(8,128)S(1)}, u32[]{:S(2)}, u32[]{:S(2)}) collective-permute-start(f32[16,2,16]{0,2,1:T(8,128)S(1)} %get-tuple-element.40), channel_id=1, source_target_pairs={{0,4},{4,8},{8,12},{12,16},{16,20},{20,24},{24,28},{1,5},{5,9},{9,... | collective-permute-start | bytes 6152 | tf_op jit(solution)/shard_map/ppermute | solution.py:19
  145.6 3.4 %collective-permute-start.16 = (f32[16,2,8]{0,2,1:T(8,128)S(1)}, f32[16,2,8]{0,2,1:T(8,128)S(1)}, u32[]{:S(2)}, u32[]{:S(2)}) collective-permute-start(f32[16,2,8]{0,2,1:T(8,128)S(1)} %get-tuple-element.68), channel_id=1, source_target_pairs={{0,4},{4,8},{8,12},{12,16},{16,20},{20,24},{24,28},{1,5},{5,9},{9,... | collective-permute-start | bytes 3080 | tf_op jit(solution)/shard_map/ppermute | solution.py:19
  162.1 3.6 %collective-permute-start.20 = (f32[16,2,4]{0,2,1:T(4,128)S(1)}, f32[16,2,4]{0,2,1:T(4,128)S(1)}, u32[]{:S(2)}, u32[]{:S(2)}) collective-permute-start(f32[16,2,4]{0,2,1:T(4,128)S(1)} %multiply_add_fusion.9), channel_id=1, source_target_pairs={{0,4},{4,8},{8,12},{12,16},{16,20},{20,24},{24,28},{1,5},{5,9},{9,... | collective-permute-start | bytes 1544 | tf_op jit(solution)/shard_map/ppermute | solution.py:19
  175.4 5.4 %collective-permute-start.28 = (f32[3,1,2]{0,2,1:T(2,128)S(1)}, f32[3,1,2]{0,2,1:T(2,128)S(1)}, u32[]{:S(2)}, u32[]{:S(2)}) collective-permute-start(f32[3,1,2]{0,2,1:T(2,128)S(1)} %bitcast.167), channel_id=1, source_target_pairs={{0,4},{4,8},{8,12},{12,16},{16,20},{20,24},{24,28},{1,5},{5,9},{9,... | collective-permute-start | bytes 80 | tf_op jit(solution)/shard_map/ppermute | solution.py:19
  182.6 3.6 %collective-permute-start.24 = (f32[12,1,2]{0,2,1:T(2,128)S(1)}, f32[12,1,2]{0,2,1:T(2,128)S(1)}, u32[]{:S(2)}, u32[]{:S(2)}) collective-permute-start(f32[12,1,2]{0,2,1:T(2,128)S(1)} %bitcast.161), channel_id=1, source_target_pairs={{0,4},{4,8},{8,12},{12,16},{16,20},{20,24},{24,28},{1,5},{5,9},{9,... | collective-permute-start | bytes 296 | tf_op jit(solution)/shard_map/ppermute | solution.py:19
  199.7 4.5 %collective-permute-start.32 = (f32[3,1,4]{0,2,1:T(4,128)S(1)}, f32[3,1,4]{0,2,1:T(4,128)S(1)}, u32[]{:S(2)}, u32[]{:S(2)}) collective-permute-start(f32[3,1,4]{0,2,1:T(4,128)S(1)} %get-tuple-element.94), channel_id=1, source_target_pairs={{0,4},{4,8},{8,12},{12,16},{16,20},{20,24},{24,28},{1,5},{5,9},{9,... | collective-permute-start | bytes 152 | tf_op jit(solution)/shard_map/ppermute | solution.py:19
  215.7 3.4 %collective-permute-start.36 = (f32[3,1,8]{2,1,0:T(1,128)S(1)}, f32[3,1,8]{2,1,0:T(1,128)S(1)}, u32[]{:S(2)}, u32[]{:S(2)}) collective-permute-start(f32[3,1,8]{2,1,0:T(1,128)S(1)} %get-tuple-element.84), channel_id=1, source_target_pairs={{0,4},{4,8},{8,12},{12,16},{16,20},{20,24},{24,28},{1,5},{5,9},{9,... | collective-permute-start | bytes 296 | tf_op jit(solution)/shard_map/ppermute | solution.py:19
  230.5 3.4 %collective-permute-start.40 = (f32[3,1,16]{2,1,0:T(1,128)S(1)}, f32[3,1,16]{2,1,0:T(1,128)S(1)}, u32[]{:S(2)}, u32[]{:S(2)}) collective-permute-start(f32[3,1,16]{2,1,0:T(1,128)S(1)} %get-tuple-element.70), channel_id=1, source_target_pairs={{0,4},{4,8},{8,12},{12,16},{16,20},{20,24},{24,28},{1,5},{5,9},{9,... | collective-permute-start | bytes 584 | tf_op jit(solution)/shard_map/ppermute | solution.py:19
  245.6 3.4 %collective-permute-start.44 = (f32[3,1,32]{2,1,0:T(1,128)S(1)}, f32[3,1,32]{2,1,0:T(1,128)S(1)}, u32[]{:S(2)}, u32[]{:S(2)}) collective-permute-start(f32[3,1,32]{2,1,0:T(1,128)S(1)} %get-tuple-element.58), channel_id=1, source_target_pairs={{0,4},{4,8},{8,12},{12,16},{16,20},{20,24},{24,28},{1,5},{5,9},{9,... | collective-permute-start | bytes 1160 | tf_op jit(solution)/shard_map/ppermute | solution.py:19
  256.9 3.4 %collective-permute-done.47 = f32[3,18,1]{2,1,0:T(8,128)S(1)} collective-permute-done((f32[3,18,1]{2,1,0:T(8,128)S(1)}, f32[3,18,1]{2,1,0:T(8,128)S(1)}, u32[]{:S(2)}, u32[]{:S(2)}) %collective-permute-start.47) | collective-permute-done | bytes 248 | tf_op jit(solution)/shard_map/ppermute | solution.py:20
  260.8 3.4 %collective-permute-start.48 = (f32[3,1,64]{2,1,0:T(1,128)S(1)}, f32[3,1,64]{2,1,0:T(1,128)S(1)}, u32[]{:S(2)}, u32[]{:S(2)}) collective-permute-start(f32[3,1,64]{2,1,0:T(1,128)S(1)} %get-tuple-element.46), channel_id=1, source_target_pairs={{0,4},{4,8},{8,12},{12,16},{16,20},{20,24},{24,28},{1,5},{5,9},{9,... | collective-permute-start | bytes 2312 | tf_op jit(solution)/shard_map/ppermute | solution.py:19
  272.4 3.5 %collective-permute-done.51 = f32[3,34,1]{2,1,0:T(8,128)S(1)} collective-permute-done((f32[3,34,1]{2,1,0:T(8,128)S(1)}, f32[3,34,1]{2,1,0:T(8,128)S(1)}, u32[]{:S(2)}, u32[]{:S(2)}) %collective-permute-start.51) | collective-permute-done | bytes 440 | tf_op jit(solution)/shard_map/ppermute | solution.py:20
  (326 shorter events, 147.0 us)
Async XLA Ops:
  2.0 12.3 %collective-permute-start.1 = (f32[16,2,128]{2,0,1:T(8,128)S(1)}, f32[16,2,128]{2,0,1:T(8,128)S(1)}, u32[]{:S(2)}, u32[]{:S(2)}) collective-permute-start(f32[16,2,128]{2,0,1:T(8,128)S(1)} %copy.472), channel_id=1, source_target_pairs={{4,0},{8,4},{12,8},{16,12},{20,16},{24,20},{28,24},{5,1},{9,5},{13... | collective-permute-start | bytes 49160 | tf_op jit(solution)/shard_map/ppermute | solution.py:20
  14.8 5.3 %collective-permute-start.3 = (f32[16,68,2]{1,0,2:T(8,128)S(1)}, f32[16,68,2]{1,0,2:T(8,128)S(1)}, u32[]{:S(2)}, u32[]{:S(2)}) collective-permute-start(f32[16,68,2]{1,0,2:T(8,128)S(1)} %copy.414), channel_id=1, source_target_pairs={{1,0},{2,1},{3,2},{5,4},{6,5},{7,6},{9,8},{10,9},{11,10},{13,12},{... | collective-permute-start | bytes 26120 | tf_op jit(solution)/shard_map/ppermute | solution.py:20
  78.9 11.1 %collective-permute-start.4 = (f32[16,2,64]{1,2,0:T(8,128)S(1)}, f32[16,2,64]{1,2,0:T(8,128)S(1)}, u32[]{:S(2)}, u32[]{:S(2)}) collective-permute-start(f32[16,2,64]{1,2,0:T(8,128)S(1)} %get-tuple-element.7), channel_id=1, source_target_pairs={{0,4},{4,8},{8,12},{12,16},{16,20},{20,24},{24,28},{1,5},{5,9},{9,... | collective-permute-start | bytes 24584 | tf_op jit(solution)/shard_map/ppermute | solution.py:19
  83.9 10.5 %collective-permute-start.5 = (f32[16,2,64]{1,2,0:T(8,128)S(1)}, f32[16,2,64]{1,2,0:T(8,128)S(1)}, u32[]{:S(2)}, u32[]{:S(2)}) collective-permute-start(f32[16,2,64]{1,2,0:T(8,128)S(1)} %get-tuple-element.8), channel_id=1, source_target_pairs={{4,0},{8,4},{12,8},{16,12},{20,16},{24,20},{28,24},{5,1},{9,5},{13... | collective-permute-start | bytes 24584 | tf_op jit(solution)/shard_map/ppermute | solution.py:20
  94.8 7.9 %collective-permute-start.6 = (f32[16,36,2]{2,0,1:T(8,128)S(1)}, f32[16,36,2]{2,0,1:T(8,128)S(1)}, u32[]{:S(2)}, u32[]{:S(2)}) collective-permute-start(f32[16,36,2]{2,0,1:T(8,128)S(1)} %get-tuple-element.24), channel_id=1, source_target_pairs={{0,1},{1,2},{2,3},{4,5},{5,6},{6,7},{8,9},{9,10},{10,11},{12,13},{... | collective-permute-start | bytes 13832 | tf_op jit(solution)/shard_map/ppermute | solution.py:19
  99.1 7.5 %collective-permute-start.7 = (f32[16,36,2]{2,0,1:T(8,128)S(1)}, f32[16,36,2]{2,0,1:T(8,128)S(1)}, u32[]{:S(2)}, u32[]{:S(2)}) collective-permute-start(f32[16,36,2]{2,0,1:T(8,128)S(1)} %get-tuple-element.25), channel_id=1, source_target_pairs={{1,0},{2,1},{3,2},{5,4},{6,5},{7,6},{9,8},{10,9},{11,10},{13,12},{... | collective-permute-start | bytes 13832 | tf_op jit(solution)/shard_map/ppermute | solution.py:20
  113.4 5.2 %collective-permute-start.8 = (f32[16,2,32]{0,2,1:T(8,128)S(1)}, f32[16,2,32]{0,2,1:T(8,128)S(1)}, u32[]{:S(2)}, u32[]{:S(2)}) collective-permute-start(f32[16,2,32]{0,2,1:T(8,128)S(1)} %get-tuple-element.26), channel_id=1, source_target_pairs={{0,4},{4,8},{8,12},{12,16},{16,20},{20,24},{24,28},{1,5},{5,9},{9,... | collective-permute-start | bytes 12296 | tf_op jit(solution)/shard_map/ppermute | solution.py:19
  116.3 5.2 %collective-permute-start.9 = (f32[16,2,32]{0,2,1:T(8,128)S(1)}, f32[16,2,32]{0,2,1:T(8,128)S(1)}, u32[]{:S(2)}, u32[]{:S(2)}) collective-permute-start(f32[16,2,32]{0,2,1:T(8,128)S(1)} %get-tuple-element.27), channel_id=1, source_target_pairs={{4,0},{8,4},{12,8},{16,12},{20,16},{24,20},{28,24},{5,1},{9,5},{13... | collective-permute-start | bytes 12296 | tf_op jit(solution)/shard_map/ppermute | solution.py:20
  129.1 6.1 %collective-permute-start.12 = (f32[16,2,16]{0,2,1:T(8,128)S(1)}, f32[16,2,16]{0,2,1:T(8,128)S(1)}, u32[]{:S(2)}, u32[]{:S(2)}) collective-permute-start(f32[16,2,16]{0,2,1:T(8,128)S(1)} %get-tuple-element.40), channel_id=1, source_target_pairs={{0,4},{4,8},{8,12},{12,16},{16,20},{20,24},{24,28},{1,5},{5,9},{9,... | collective-permute-start | bytes 6152 | tf_op jit(solution)/shard_map/ppermute | solution.py:19
  132.6 5.1 %collective-permute-start.13 = (f32[16,2,16]{0,2,1:T(8,128)S(1)}, f32[16,2,16]{0,2,1:T(8,128)S(1)}, u32[]{:S(2)}, u32[]{:S(2)}) collective-permute-start(f32[16,2,16]{0,2,1:T(8,128)S(1)} %get-tuple-element.41), channel_id=1, source_target_pairs={{4,0},{8,4},{12,8},{16,12},{20,16},{24,20},{28,24},{5,1},{9,5},{13... | collective-permute-start | bytes 6152 | tf_op jit(solution)/shard_map/ppermute | solution.py:20
  137.7 5.0 %collective-permute-start.14 = (f32[16,12,2]{0,2,1:T(2,128)S(1)}, f32[16,12,2]{0,2,1:T(2,128)S(1)}, u32[]{:S(2)}, u32[]{:S(2)}) collective-permute-start(f32[16,12,2]{0,2,1:T(2,128)S(1)} %get-tuple-element.36), channel_id=1, source_target_pairs={{0,1},{1,2},{2,3},{4,5},{5,6},{6,7},{8,9},{9,10},{10,11},{12,13},{... | collective-permute-start | bytes 4616 | tf_op jit(solution)/shard_map/ppermute | solution.py:19
  145.6 5.7 %collective-permute-start.16 = (f32[16,2,8]{0,2,1:T(8,128)S(1)}, f32[16,2,8]{0,2,1:T(8,128)S(1)}, u32[]{:S(2)}, u32[]{:S(2)}) collective-permute-start(f32[16,2,8]{0,2,1:T(8,128)S(1)} %get-tuple-element.68), channel_id=1, source_target_pairs={{0,4},{4,8},{8,12},{12,16},{16,20},{20,24},{24,28},{1,5},{5,9},{9,... | collective-permute-start | bytes 3080 | tf_op jit(solution)/shard_map/ppermute | solution.py:19
  149.0 5.0 %collective-permute-start.17 = (f32[16,2,8]{0,2,1:T(8,128)S(1)}, f32[16,2,8]{0,2,1:T(8,128)S(1)}, u32[]{:S(2)}, u32[]{:S(2)}) collective-permute-start(f32[16,2,8]{0,2,1:T(8,128)S(1)} %get-tuple-element.69), channel_id=1, source_target_pairs={{4,0},{8,4},{12,8},{16,12},{20,16},{24,20},{28,24},{5,1},{9,5},{13... | collective-permute-start | bytes 3080 | tf_op jit(solution)/shard_map/ppermute | solution.py:20
  160.1 5.8 %collective-permute-start.21 = (f32[16,2,4]{0,2,1:T(4,128)S(1)}, f32[16,2,4]{0,2,1:T(4,128)S(1)}, u32[]{:S(2)}, u32[]{:S(2)}) collective-permute-start(f32[16,2,4]{0,2,1:T(4,128)S(1)} %multiply_add_fusion.9), channel_id=1, source_target_pairs={{4,0},{8,4},{12,8},{16,12},{20,16},{24,20},{28,24},{5,1},{9,5},{13... | collective-permute-start | bytes 1544 | tf_op jit(solution)/shard_map/ppermute | solution.py:20
  173.2 13.3 %collective-permute-start.29 = (f32[3,1,2]{0,2,1:T(2,128)S(1)}, f32[3,1,2]{0,2,1:T(2,128)S(1)}, u32[]{:S(2)}, u32[]{:S(2)}) collective-permute-start(f32[3,1,2]{0,2,1:T(2,128)S(1)} %bitcast.166), channel_id=1, source_target_pairs={{4,0},{8,4},{12,8},{16,12},{20,16},{24,20},{28,24},{5,1},{9,5},{13... | collective-permute-start | bytes 80 | tf_op jit(solution)/shard_map/ppermute | solution.py:20
  175.4 11.2 %collective-permute-start.28 = (f32[3,1,2]{0,2,1:T(2,128)S(1)}, f32[3,1,2]{0,2,1:T(2,128)S(1)}, u32[]{:S(2)}, u32[]{:S(2)}) collective-permute-start(f32[3,1,2]{0,2,1:T(2,128)S(1)} %bitcast.167), channel_id=1, source_target_pairs={{0,4},{4,8},{8,12},{12,16},{16,20},{20,24},{24,28},{1,5},{5,9},{9,... | collective-permute-start | bytes 80 | tf_op jit(solution)/shard_map/ppermute | solution.py:19
  180.7 12.4 %collective-permute-start.25 = (f32[12,1,2]{0,2,1:T(2,128)S(1)}, f32[12,1,2]{0,2,1:T(2,128)S(1)}, u32[]{:S(2)}, u32[]{:S(2)}) collective-permute-start(f32[12,1,2]{0,2,1:T(2,128)S(1)} %bitcast.160), channel_id=1, source_target_pairs={{4,0},{8,4},{12,8},{16,12},{20,16},{24,20},{28,24},{5,1},{9,5},{13... | collective-permute-start | bytes 296 | tf_op jit(solution)/shard_map/ppermute | solution.py:20
  182.6 10.4 %collective-permute-start.24 = (f32[12,1,2]{0,2,1:T(2,128)S(1)}, f32[12,1,2]{0,2,1:T(2,128)S(1)}, u32[]{:S(2)}, u32[]{:S(2)}) collective-permute-start(f32[12,1,2]{0,2,1:T(2,128)S(1)} %bitcast.161), channel_id=1, source_target_pairs={{0,4},{4,8},{8,12},{12,16},{16,20},{20,24},{24,28},{1,5},{5,9},{9,... | collective-permute-start | bytes 296 | tf_op jit(solution)/shard_map/ppermute | solution.py:19
  199.7 6.4 %collective-permute-start.32 = (f32[3,1,4]{0,2,1:T(4,128)S(1)}, f32[3,1,4]{0,2,1:T(4,128)S(1)}, u32[]{:S(2)}, u32[]{:S(2)}) collective-permute-start(f32[3,1,4]{0,2,1:T(4,128)S(1)} %get-tuple-element.94), channel_id=1, source_target_pairs={{0,4},{4,8},{8,12},{12,16},{16,20},{20,24},{24,28},{1,5},{5,9},{9,... | collective-permute-start | bytes 152 | tf_op jit(solution)/shard_map/ppermute | solution.py:19
  215.7 5.3 %collective-permute-start.36 = (f32[3,1,8]{2,1,0:T(1,128)S(1)}, f32[3,1,8]{2,1,0:T(1,128)S(1)}, u32[]{:S(2)}, u32[]{:S(2)}) collective-permute-start(f32[3,1,8]{2,1,0:T(1,128)S(1)} %get-tuple-element.84), channel_id=1, source_target_pairs={{0,4},{4,8},{8,12},{12,16},{16,20},{20,24},{24,28},{1,5},{5,9},{9,... | collective-permute-start | bytes 296 | tf_op jit(solution)/shard_map/ppermute | solution.py:19
  230.5 5.6 %collective-permute-start.40 = (f32[3,1,16]{2,1,0:T(1,128)S(1)}, f32[3,1,16]{2,1,0:T(1,128)S(1)}, u32[]{:S(2)}, u32[]{:S(2)}) collective-permute-start(f32[3,1,16]{2,1,0:T(1,128)S(1)} %get-tuple-element.70), channel_id=1, source_target_pairs={{0,4},{4,8},{8,12},{12,16},{16,20},{20,24},{24,28},{1,5},{5,9},{9,... | collective-permute-start | bytes 584 | tf_op jit(solution)/shard_map/ppermute | solution.py:19
  245.6 5.5 %collective-permute-start.44 = (f32[3,1,32]{2,1,0:T(1,128)S(1)}, f32[3,1,32]{2,1,0:T(1,128)S(1)}, u32[]{:S(2)}, u32[]{:S(2)}) collective-permute-start(f32[3,1,32]{2,1,0:T(1,128)S(1)} %get-tuple-element.58), channel_id=1, source_target_pairs={{0,4},{4,8},{8,12},{12,16},{16,20},{20,24},{24,28},{1,5},{5,9},{9,... | collective-permute-start | bytes 1160 | tf_op jit(solution)/shard_map/ppermute | solution.py:19
  260.8 6.2 %collective-permute-start.48 = (f32[3,1,64]{2,1,0:T(1,128)S(1)}, f32[3,1,64]{2,1,0:T(1,128)S(1)}, u32[]{:S(2)}, u32[]{:S(2)}) collective-permute-start(f32[3,1,64]{2,1,0:T(1,128)S(1)} %get-tuple-element.46), channel_id=1, source_target_pairs={{0,4},{4,8},{8,12},{12,16},{16,20},{20,24},{24,28},{1,5},{5,9},{9,... | collective-permute-start | bytes 2312 | tf_op jit(solution)/shard_map/ppermute | solution.py:19
  270.9 5.0 %collective-permute-start.51 = (f32[3,34,1]{2,1,0:T(8,128)S(1)}, f32[3,34,1]{2,1,0:T(8,128)S(1)}, u32[]{:S(2)}, u32[]{:S(2)}) collective-permute-start(f32[3,34,1]{2,1,0:T(8,128)S(1)} %get-tuple-element.45), channel_id=1, source_target_pairs={{1,0},{2,1},{3,2},{5,4},{6,5},{7,6},{9,8},{10,9},{11,10},{13,12},{... | collective-permute-start | bytes 1232 | tf_op jit(solution)/shard_map/ppermute | solution.py:20
  (35 other events, 159.2 us)
where the time goes:
time: 279 us; the launch traced here: 277 us
  starting transfers between devices  126 us (45%)
  waiting for transfers between devices  70.7 us (25%)
  local copies, waits for them, and re-layouts  65.1 us (23%)
  other arithmetic  14 us (5%)
    ppermute x26, starting transfers between devices, padded_2(): before = lax.ppermute(last, axis, up)  76.8 us
    ppermute x26, waiting for transfers between devices, padded_2(): after = lax.ppermute(leading, axis, down)  62.4 us
    ppermute x26, starting transfers between devices, padded_2(): after = lax.ppermute(leading, axis, down)  48.9 us
    slice x4, local copies, waits for them, and re-layouts, reduce_level(): across = across + TAPS[offset] * padded[:, offset:offset + 2 * height:2, :]  39.9 us
    slice x2, local copies, waits for them, and re-layouts, reduce_level(): across = TAPS[0] * padded[:, 0:2 * height:2, :]  10 us
    ppermute x26, waiting for transfers between devices, padded_2(): before = lax.ppermute(last, axis, up)  8.29 us
  transfers between devices with their start and end apart: 52, of which 26 were waited for; matrix products, arithmetic and copies ran while one was open for 2% of the time, Pallas kernels for 0%

commit v1 on v0

v1 whole, which is shorter than its diff:
```python
import jax
import jax.numpy as jnp
from jax import lax
from jax.experimental import pallas as pl
from jax.experimental.pallas import tpu as pltpu
from jax.sharding import PartitionSpec as P

EXPOSURES = 4
BANDS = 3
INNER = EXPOSURES * BANDS
PLANES = INNER + EXPOSURES
LANES = 128

SIDE = (64, 32, 16, 8, 4, 2, 1)
WIDE = (128, 64, 32, 16, 8, 4, 2)
ROWS = (64, 40, 24, 16, 8, 8, 8)
RIM = (0, 2, 3, 3, 3)
LEVEL_AT = (0, 0, 40, 64, 80)
PACKED = 88
PITCH_5 = 16
PITCH_6 = 8
AT_6 = 80
HALF = LANES // 2

f32 = jnp.float32
bf16 = jnp.bfloat16


def iota(shape, dim):
    return lax.broadcasted_iota(jnp.int32, shape, dim)


def reduce_weights(first):
    tap = iota((LANES, LANES), 0) - 2 * iota((LANES, LANES), 1) + first
    near = jnp.where((tap == 1) | (tap == 3), 0.25, 0.0)
    ends = jnp.where((tap == 0) | (tap == 4), 0.0625, 0.0)
    weights = jnp.where(tap == 2, 0.375, near + ends).astype(bf16)
    return jnp.concatenate([weights, weights], 0)


def expand_taps(source, target):
    half = jnp.bitwise_and(target, 1)
    away = 2 * source - target
    even = jnp.where(away == 0, 0.75, 0.0) + jnp.where((away == 2) | (away == -2), 0.125, 0.0)
    odd = jnp.where((away == 1) | (away == -1), 0.5, 0.0)
    return jnp.where(half == 1, odd, even)


def expand_weights(first):
    shape = (LANES, LANES)
    weights = expand_taps(iota(shape, 0) - 1, iota(shape, 1) - first).astype(bf16)
    return jnp.concatenate([weights, weights], 0)


def split_dot(values, weights):
    high = values.astype(bf16)
    low = (values - high.astype(f32)).astype(bf16)
    return jnp.dot(jnp.concatenate([high, low], 1), weights, preferred_element_type=f32)


def in_slab(level, row, col, rows, cols):
    shape = (ROWS[level], LANES)
    along, across = iota(shape, 0), iota(shape, 1)
    first = jnp.where(row == 0, 1, 0)
    last = jnp.where(row == rows - 1, SIDE[level] + 1, ROWS[level])
    left = jnp.where(col == 0, 1, 0)
    right = jnp.where(col == cols - 1, WIDE[level] + 1, LANES)
    return (along >= first) & (along < last) & (across >= left) & (across < right)


def expand_rows(source, target, count):
    before = source[:, 0:count, :]
    centre = source[:, 1 : count + 1, :]
    after = source[:, 2 : count + 2, :]
    target[:, pl.ds(0, count, stride=2), :] = (before + centre) * 0.5
    target[:, pl.ds(1, count, stride=2), :] = centre * 0.75 + (before + after) * 0.125


def expand_rows_tile(source, target, count):
    before = source[:, 0:count, :]
    centre = source[:, 1 : count + 1, :]
    after = source[:, 2 : count + 2, :]
    target[:, pl.ds(0, count, stride=2), :] = centre * 0.75 + (before + after) * 0.125
    target[:, pl.ds(1, count, stride=2), :] = (centre + after) * 0.5


def pairs_of(level):
    return {0: 32, 1: 20, 2: 12, 3: 6, 4: 4}[level]


def partial_kernel(
    grid, place, gains, images, labels, x1, x2, x3, x4, packed, send_a, send_b, patch,
    s0, s1, s2, s3, s4, s5, y5, y6, across, strips, turned, low, high,
):
    row, col = place[0], place[1]
    s0[:, 0:8, :] = jnp.zeros((PLANES, 8, LANES), f32)
    s0[:, 72:88, :] = jnp.zeros((PLANES, 16, LANES), f32)
    for e in range(EXPOSURES):
        for b in range(BANDS):
            s0[e * BANDS + b, 8:72, :] = images[e * BANDS + b] * gains[e, b]
        s0[INNER + e, 8:72, :] = jnp.where(labels[...] == e, 1.0, 0.0)

    def reduce(source, level, first, weights):
        count = ROWS[level]
        for p in range(PLANES):
            tap = [source[p, pl.ds(first + k, count, stride=2), :] for k in range(5)]
            total = tap[2] * 0.375 + (tap[1] + tap[3]) * 0.25 + (tap[0] + tap[4]) * 0.0625
            across[p * count : (p + 1) * count, :] = total
        result = split_dot(across[0 : PLANES * count, :], weights)
        inside = in_slab(level, row, col, *grid)
        return jnp.where(inside[None], result.reshape(PLANES, count, LANES), 0.0)

    def keep(store, result):
        count, depth = result.shape[1], store.shape[1]
        store[:, 0:8, :] = jnp.zeros((PLANES, 8, LANES), f32)
        store[:, 8 : 8 + count, :] = result
        if depth > 8 + count:
            store[:, 8 + count : depth, :] = jnp.zeros((PLANES, depth - 8 - count, LANES), f32)

    weights = reduce_weights(3)
    result = reduce(s0, 1, 4, reduce_weights(4))
    x1[...] = result
    keep(s1, result)
    for level, source, store, out in ((2, s1, s2, x2), (3, s2, s3, x3), (4, s3, s4, x4)):
        result = reduce(source, level, 5, weights)
        out[...] = result
        keep(store, result)
    result = reduce(s4, 5, 5, weights)
    y5[...] = result.reshape(PLANES * 8, LANES)
    keep(s5, result)
    y6[...] = reduce(s5, 6, 5, weights).reshape(PLANES * 8, LANES)

    coarse = jnp.zeros((PLANES, LANES), f32)
    for k in range(SIDE[5] + 3):
        line = y5[pl.ds(k, PLANES, stride=8), :]
        coarse = coarse + (pltpu.roll(line, PITCH_5 * k, 1) if k else line)
    for k in range(SIDE[6] + 3):
        coarse = coarse + pltpu.roll(y6[pl.ds(k, PLANES, stride=8), :], AT_6 + PITCH_6 * k, 1)
    patch[...] = coarse

    levels = (None, x1, x2, x3, x4)
    for level in range(1, 5):
        count, wide = ROWS[level], WIDE[level]
        lane = iota((count, LANES), 1)
        total = jnp.zeros((count, LANES), f32)
        for p in range(PLANES):
            plane = levels[level][p]
            at = 6 * p
            first = pltpu.roll(plane, at, 1) if at else plane
            last = pltpu.roll(plane, (at + 3 - wide) % LANES, 1)
            total = jnp.where((lane >= at) & (lane < at + 3), first, total)
            total = jnp.where((lane >= at + 3) & (lane < at + 6), last, total)
        strips[LEVEL_AT[level] : LEVEL_AT[level] + count, :] = total

    packed[...] = jnp.zeros((PACKED, LANES), f32)
    for here, there, count in packing():
        packed[here : here + count, :] = strips[there : there + count, :]

    for p in range(PLANES):
        turned[p] = pltpu.roll(x4[p], HALF, 1)
    for rim, at in ((low, (0, 0, 0, 0, 0)), (high, SIDE)):
        rim[0:PLANES, 0:2, :] = x1[:, at[1] : at[1] + 2, :]
        rim[0:PLANES, 2:5, :] = x2[:, at[2] : at[2] + 3, :]
        rim[0:PLANES, 5:8, :] = x3[:, at[3] : at[3] + 3, :] + turned[:, at[4] : at[4] + 3, :]
    for k in range(2):
        low[PLANES + k] = packed[8 * k : 8 * k + 8, :]
        high[PLANES + k] = packed[16 + 8 * k : 24 + 8 * k, :]
    odd = jnp.bitwise_and(row, 1) == 1
    send_a[...] = jnp.where(odd, low[...], high[...])
    send_b[...] = jnp.where(odd, high[...], low[...])


def packing():
    moves = []
    for start, last in ((0, False), (16, True)):
        here = start
        for level in range(1, 5):
            there = LEVEL_AT[level] + (SIDE[level] if last else 0)
            moves.append((here, there, RIM[level]))
            here += RIM[level]
    here = 32
    for level in range(1, 5):
        count = SIDE[level] - RIM[level]
        moves.append((here, LEVEL_AT[level] + RIM[level], count))
        here += count
    return moves


def fine_kernel(
    place, gains, images, labels, x1, x2, x3, x4, got_a, got_b, side_a, side_b,
    b0, b1, b2, b3, t4,
    t1, t2, t3, left, right, low, high, turned, across, spread,
):
    row_odd = jnp.bitwise_and(place[0], 1) == 1
    col_odd = jnp.bitwise_and(place[1], 1) == 1
    low[...] = jnp.where(row_odd, got_a[0:PLANES], got_b[0:PLANES])
    high[...] = jnp.where(row_odd, got_b[0:PLANES], got_a[0:PLANES])
    turned[0] = jnp.where(col_odd, side_a[...], side_b[...])
    turned[1] = jnp.where(col_odd, side_b[...], side_a[...])
    left[...] = jnp.zeros((PACKED, LANES), f32)
    right[...] = jnp.zeros((PACKED, LANES), f32)
    for here, there, count in packing():
        left[there : there + count, :] = turned[0, here : here + count, :]
        right[there : there + count, :] = turned[1, here : here + count, :]

    totals = (None, t1, t2, t3, t4)
    parts = (None, x1, x2, x3, x4)
    for level in range(1, 5):
        totals[level][...] = parts[level][...]
    for rim, at in ((low, (0, 0, 0, 0, 0)), (high, SIDE)):
        t1[:, at[1] : at[1] + 2, :] += rim[:, 0:2, :]
        t2[:, at[2] : at[2] + 3, :] += rim[:, 2:5, :]
        t3[:, at[3] : at[3] + 3, :] += rim[:, 5:8, :]
        for p in range(PLANES):
            rim[p] = pltpu.roll(rim[p], HALF, 1)
        t4[:, at[4] : at[4] + 3, :] += rim[:, 5:8, :]
    for level in range(1, 5):
        count, wide, at = ROWS[level], WIDE[level], LEVEL_AT[level]
        lane = iota((count, LANES), 1)
        from_left = left[at : at + count, :]
        from_right = right[at : at + count, :]
        for p in range(PLANES):
            first = pltpu.roll(from_left, (-6 * p - 3) % LANES, 1)
            last = pltpu.roll(from_right, (wide - 6 * p) % LANES, 1)
            last = jnp.where((lane >= wide) & (lane < wide + 3), last, 0.0)
            totals[level][p] = totals[level][p] + jnp.where(lane < 3, first, last)

    weights = expand_weights(1)
    for level in (3, 2, 1):
        above, count, out = totals[level + 1], ROWS[level + 1], (None, b1, b2, b3)[level]
        coarse = above[0:INNER].reshape(INNER * count, LANES)
        across[:, 0:count, :] = split_dot(coarse, weights).reshape(INNER, count, LANES)
        if level == 3:
            spread[:, 0 : ROWS[3], :] = jnp.zeros((INNER, ROWS[3], LANES), f32)
        expand_rows(across, spread, pairs_of(level))
        for b in range(BANDS):
            total = jnp.zeros((ROWS[level], LANES), f32)
            for e in range(EXPOSURES):
                p = e * BANDS + b
                laplace = totals[level][p] - spread[p, 0 : ROWS[level], :]
                total = total + totals[level][INNER + e] * laplace
            out[b] = total
    across[...] = split_dot(t1[0:INNER].reshape(INNER * ROWS[1], LANES), expand_weights(0)).reshape(
        INNER, ROWS[1], LANES
    )
    expand_rows_tile(across, spread, pairs_of(0))
    for b in range(BANDS):
        total = jnp.zeros((ROWS[0], LANES), f32)
        for e in range(EXPOSURES):
            p = e * BANDS + b
            laplace = images[p] * gains[e, b] - spread[p]
            total = total + jnp.where(labels[...] == e, laplace, 0.0)
        b0[b] = total


def collapse_kernel(
    grid, place, patches, b0, b1, b2, b3, t4, out,
    v5, v6, window, c4, c3, c2, c1, across, spread,
):
    rows, cols = grid
    row, col = place[0], place[1]
    lane = iota((PLANES, LANES), 1)
    zero = jnp.zeros((PLANES, LANES), f32)
    five, six = [zero, zero], zero
    for r in range(rows):
        for c in range(cols):
            at = (r * cols + c) * PLANES
            source = patches[at : at + PLANES, :]
            start = PITCH_5 * (SIDE[5] * r - 1) + WIDE[5] * c - 1
            stop = start + AT_6
            turned = pltpu.roll(source, start % LANES, 1)
            for k in range(2):
                begin, end = max(start - LANES * k, 0), min(stop - LANES * k, LANES)
                if begin < end:
                    five[k] = five[k] + jnp.where((lane >= begin) & (lane < end), turned, 0.0)
            start = PITCH_6 * (r - 1) + WIDE[6] * c - 1
            begin, end = max(start, 0), min(start + 4 * PITCH_6, PITCH_6 * rows)
            turned = pltpu.roll(source, (start - AT_6) % LANES, 1)
            six = six + jnp.where((lane >= begin) & (lane < end), turned, 0.0)

    def blend(planes, less):
        total = None
        for e in range(EXPOSURES):
            part = planes[e * BANDS : (e + 1) * BANDS, :]
            if less is not None:
                part = part - less[e * BANDS : (e + 1) * BANDS, :]
            part = part * planes[INNER + e : INNER + e + 1, :]
            total = part if total is None else total + part
        return total

    v6[...] = six
    top = blend(v6, None)
    v6[INNER : INNER + BANDS, :] = top
    v6[INNER + BANDS : PLANES, :] = jnp.zeros((1, LANES), f32)
    source, target = iota((LANES, 2 * LANES), 0), iota((LANES, 2 * LANES), 1)
    along = expand_taps(lax.shift_right_logical(source, 3), lax.shift_right_logical(target, 4))
    aside = expand_taps(jnp.bitwise_and(source, 7), jnp.bitwise_and(target, 15))
    weights = (along * aside).astype(bf16)
    weights = jnp.concatenate([weights, weights], 0)
    v5[:, 0:LANES] = five[0]
    v5[:, LANES : 2 * LANES] = five[1]
    window_5 = split_dot(v6[...], weights)
    spread_5 = spread
    spread_5[0, 0:PLANES, :] = window_5[:, 0:LANES]
    spread_5[1, 0:PLANES, :] = window_5[:, LANES : 2 * LANES]
    for k in range(2):
        planes = v5[:, LANES * k : LANES * k + LANES]
        less = spread_5[k, 0:PLANES, :]
        v5[INNER : INNER + BANDS, LANES * k : LANES * k + LANES] = (
            blend(planes, less) + less[INNER : INNER + BANDS, :]
        )
    v5[INNER + BANDS : PLANES, :] = jnp.zeros((1, 2 * LANES), f32)

    window[...] = jnp.zeros((PLANES * 8, LANES), f32)
    first, second = v5[:, 0:LANES], v5[:, LANES : 2 * LANES]
    where = lane + (WIDE[5] * col - 1)
    valid = (where >= 0) & (where < WIDE[5] * cols) & (lane < WIDE[5] + 3)
    for k in range(SIDE[5] + 3):
        line = SIDE[5] * row - 1 + k
        start = PITCH_5 * jnp.bitwise_and(line, 7) + WIDE[5] * col - 1
        turned = pltpu.roll(jnp.where(line < 8, first, second), jnp.bitwise_and(-start, LANES - 1), 1)
        held = valid & (line >= 0) & (line < SIDE[5] * rows)
        window[pl.ds(k, PLANES, stride=8), :] = jnp.where(held, turned, 0.0)

    weights = expand_weights(1)
    across[:, 0:8, :] = split_dot(window[...], weights).reshape(PLANES, 8, LANES)
    expand_rows(across, spread, pairs_of(4))
    inside = in_slab(4, row, col, rows, cols)
    for b in range(BANDS):
        total = spread[INNER + b, 0:8, :]
        for e in range(EXPOSURES):
            p = e * BANDS + b
            total = total + t4[INNER + e] * (t4[p] - spread[p, 0:8, :])
        c4[b] = jnp.where(inside, total, 0.0)
    c4[BANDS] = jnp.zeros((8, LANES), f32)

    for level, source, target, band in ((3, c4, c3, b3), (2, c3, c2, b2), (1, c2, c1, b1)):
        count, depth = ROWS[level + 1], ROWS[level]
        wide = split_dot(source[...].reshape(EXPOSURES * count, LANES), weights)
        across[0:EXPOSURES, 0:count, :] = wide.reshape(EXPOSURES, count, LANES)
        some = spread.at[0:EXPOSURES]
        if level == 3:
            some[:, 0:depth, :] = jnp.zeros((EXPOSURES, depth, LANES), f32)
        expand_rows(across.at[0:EXPOSURES], some, pairs_of(level))
        inside = in_slab(level, row, col, rows, cols)
        for b in range(BANDS):
            target[b] = jnp.where(inside, band[b] + spread[b, 0:depth, :], 0.0)
        target[BANDS] = jnp.zeros((depth, LANES), f32)
    wide = split_dot(c1[...].reshape(EXPOSURES * ROWS[1], LANES), expand_weights(0))
    across[0:EXPOSURES] = wide.reshape(EXPOSURES, ROWS[1], LANES)
    expand_rows_tile(across.at[0:BANDS], spread.at[0:BANDS], pairs_of(0))
    out[...] = b0[...] + spread[0:BANDS]


VMEM = pl.BlockSpec(memory_space=pltpu.VMEM)
SMEM = pl.BlockSpec(memory_space=pltpu.SMEM)
PARAMS = pltpu.CompilerParams(vmem_limit_bytes=32 * 1024 * 1024)


def floats(*shape):
    return jax.ShapeDtypeStruct(shape, f32)


def scratch(*shape):
    return pltpu.VMEM(shape, f32)


def swaps(size, first):
    return [p for i in range(first, size - 1, 2) for p in ((i, i + 1), (i + 1, i))]


def shards(images, gains, labels):
    rows, cols = lax.axis_size("ty"), lax.axis_size("tx")
    grid = (rows, cols)
    row, col = lax.axis_index("ty"), lax.axis_index("tx")
    place = jnp.stack([row, col]).astype(jnp.int32)
    images = images.reshape(INNER, ROWS[0], LANES)
    levels = [floats(PLANES, ROWS[level], LANES) for level in range(1, 5)]
    x1, x2, x3, x4, packed, send_a, send_b, patch = pl.pallas_call(
        lambda *refs: partial_kernel(grid, *refs),
        out_shape=[
            *levels,
            floats(PACKED, LANES),
            floats(PLANES + 2, 8, LANES),
            floats(PLANES + 2, 8, LANES),
            floats(PLANES, LANES),
        ],
        in_specs=[SMEM, SMEM, VMEM, VMEM],
        out_specs=[VMEM] * 8,
        scratch_shapes=[
            scratch(PLANES, 88, LANES),
            scratch(PLANES, 56, LANES),
            scratch(PLANES, 40, LANES),
            scratch(PLANES, 24, LANES),
            scratch(PLANES, 24, LANES),
            scratch(PLANES, 24, LANES),
            scratch(PLANES * 8, LANES),
            scratch(PLANES * 8, LANES),
            scratch(PLANES * ROWS[1], LANES),
            scratch(PACKED, LANES),
            scratch(PLANES, 8, LANES),
            scratch(PLANES + 2, 8, LANES),
            scratch(PLANES + 2, 8, LANES),
        ],
        compiler_params=PARAMS,
        name="partial_levels",
    )(place, gains, images, labels)
    patches = lax.all_gather(patch, ("ty", "tx"), axis=0, tiled=True)
    got_a = lax.ppermute(send_a, "ty", swaps(rows, 0))
    got_b = lax.ppermute(send_b, "ty", swaps(rows, 1))
    rim_a = got_a[PLANES:].reshape(16, LANES)
    rim_b = got_b[PLANES:].reshape(16, LANES)
    odd = row % 2 == 1
    rims = jnp.concatenate([jnp.where(odd, rim_a, rim_b), jnp.where(odd, rim_b, rim_a)], 0)
    whole = packed + jnp.pad(rims, ((0, PACKED - 32), (0, 0)))
    side_a = lax.ppermute(whole, "tx", swaps(cols, 0))
    side_b = lax.ppermute(whole, "tx", swaps(cols, 1))
    b0, b1, b2, b3, t4 = pl.pallas_call(
        fine_kernel,
        out_shape=[floats(BANDS, ROWS[level], LANES) for level in range(4)] + [levels[3]],
        in_specs=[SMEM, SMEM] + [VMEM] * 10,
        out_specs=[VMEM] * 5,
        scratch_shapes=[
            scratch(PLANES, ROWS[1], LANES),
            scratch(PLANES, ROWS[2], LANES),
            scratch(PLANES, ROWS[3], LANES),
            scratch(PACKED, LANES),
            scratch(PACKED, LANES),
            scratch(PLANES, 8, LANES),
            scratch(PLANES, 8, LANES),
            scratch(2, PACKED, LANES),
            scratch(INNER, ROWS[1], LANES),
            scratch(INNER, ROWS[0], LANES),
        ],
        compiler_params=PARAMS,
        name="fine_laplacians",
    )(place, gains, images, labels, x1, x2, x3, x4, got_a, got_b, side_a, side_b)
    return pl.pallas_call(
        lambda *refs: collapse_kernel(grid, *refs),
        out_shape=floats(BANDS, ROWS[0], LANES),
        in_specs=[SMEM] + [VMEM] * 6,
        out_specs=VMEM,
        scratch_shapes=[
            scratch(PLANES, 2 * LANES),
            scratch(PLANES, LANES),
            scratch(PLANES * 8, LANES),
            scratch(EXPOSURES, ROWS[4], LANES),
            scratch(EXPOSURES, ROWS[3], LANES),
            scratch(EXPOSURES, ROWS[2], LANES),
            scratch(EXPOSURES, ROWS[1], LANES),
            scratch(PLANES, ROWS[1], LANES),
            scratch(PLANES, ROWS[0], LANES),
        ],
        compiler_params=PARAMS,
        name="collapse",
    )(place, patches, b0, b1, b2, b3, t4)


def solution(mesh):
    placed = (P(None, None, ("grp", "ty"), "tx"), P(), P(("grp", "ty"), "tx"))
    return jax.shard_map(
        shards, mesh=mesh, in_specs=placed, out_specs=P(None, ("grp", "ty"), "tx"), check_vma=False
    )
```

time: 279 us -> 65.1 us (0.23)
  starting transfers between devices: 126 us -> 13.3 us
  waiting for transfers between devices: 70.7 us -> 3.73 us
  local copies, waits for them, and re-layouts: 65.1 us -> 2.37 us
  blocking collectives: 0 us -> 39.6 us
  other arithmetic: 14 us -> 0.09 us
  Pallas kernels: 0 us -> 5.56 us
    ppermute x52 -> x4, starting transfers between devices: 126 us -> 13.3 us  [the longest x1 8.79 us: shards(): got_a = lax.ppermute(send_a, 'ty', swaps(rows, 0))]
    ppermute x52 -> x4, waiting for transfers between devices: 70.7 us -> 3.73 us  [the longest x1 3.72 us: shards(): got_b = lax.ppermute(send_b, 'ty', swaps(rows, 1))]
    slice x65 -> x0, local copies, waits for them, and re-layouts: 56.2 us -> none  [the longest x4 39.9 us: reduce_level(): across = across + TAPS[offset] * padded[:, offset:offset + 2 * height:2, :]]
    all_gather x0 -> x1, blocking collectives: none -> 39.6 us  [shards(): patches = lax.all_gather(patch, ('ty', 'tx'), axis=0, tiled=True)]
    add x18 -> x1, other arithmetic: 5.76 us -> 0.01 us  [shards(): whole = packed + jnp.pad(rims, ((0, PACKED - 32), (0, 0)))]
    pallas_call x0 -> x3, Pallas kernels: none -> 5.56 us  [the longest x1 2.36 us: shards(): pl.pallas_call(lambda *refs: collapse_kernel(grid, *refs), out_shape=floa...]
    concatenate x24 -> x0, other arithmetic: 2.85 us -> none  [the longest x22 2.8 us: padded_2(): value = jnp.concatenate([before, value, after], axis=dim)]
  transfers between devices with their start and end apart: 52 -> 4, of which waited for: 26 -> 1; matrix products, arithmetic and copies ran while one was open for 2% -> 0% of each run, Pallas kernels for 0% -> 0%
where the time goes in v1:
time: 65.1 us; the launch traced here: 64.7 us
  blocking collectives  39.6 us (61%)
  starting transfers between devices  13.3 us (20%)
  Pallas kernels  5.56 us (9%)
  waiting for transfers between devices  3.73 us (6%)
  local copies, waits for them, and re-layouts  2.37 us (4%)
    all_gather x1, blocking collectives, shards(): patches = lax.all_gather(patch, ('ty', 'tx'), axis=0, tiled=True)  39.6 us
    ppermute x1, starting transfers between devices, shards(): got_a = lax.ppermute(send_a, 'ty', swaps(rows, 0))  8.79 us
    ppermute x1, waiting for transfers between devices, shards(): got_b = lax.ppermute(send_b, 'ty', swaps(rows, 1))  3.72 us
    unnamed x10, local copies, waits for them, and re-layouts  2.37 us
    pallas_call x1, Pallas kernels, shards(): pl.pallas_call(lambda *refs: collapse_kernel(grid, *refs), out_shape=floa...  2.36 us
    ppermute x1, starting transfers between devices, shards(): got_b = lax.ppermute(send_b, 'ty', swaps(rows, 1))  1.92 us
    ppermute x1, starting transfers between devices, shards(): side_a = lax.ppermute(whole, 'tx', swaps(cols, 0))  1.92 us
    pallas_call x1, Pallas kernels, shards(): pl.pallas_call(lambda *refs: partial_kernel(grid, *refs), out_shape=[*lev...  1.88 us
  transfers between devices with their start and end apart: 4, of which 1 were waited for; matrix products, arithmetic and copies ran while one was open for 0% of the time, Pallas kernels for 0%

profile of v1, /device:TPU:1, one launch (start us, length us, event | category | flops | bytes accessed | tf_op | source)
XLA Modules:
  0.0 64.7 jit_solution(5913161982639001270)
XLA Ops:
  0.0 0.0 copy-start.4
  0.0 0.1 pad_add_fusion.refs_0_.place
  0.1 0.6 copy-done.4
  0.7 0.0 copy-start
  0.7 1.0 %copy-done = f32[4,3,64,128]{3,2,1,0:T(8,128)S(1)} copy-done((f32[4,3,64,128]{3,2,1,0:T(8,128)S(1)}, f32[4,3,64,128]{3,2,1,0:T(8,128)}, u32[]{:S(2)}) %copy-start) | copy-done | bytes 393240
  1.7 0.0 copy-start.2
  1.7 0.8 %copy-done.2 = s32[64,128]{1,0:T(8,128)S(1)} copy-done((s32[64,128]{1,0:T(8,128)S(1)}, s32[64,128]{1,0:T(8,128)}, u32[]{:S(2)}) %copy-start.2) | copy-done | bytes 32792
  2.4 0.0 copy-start.1
  2.4 1.9 %partial_levels.1 = (f32[16,40,128]{2,1,0:T(8,128)S(1)}, f32[16,24,128]{2,1,0:T(8,128)S(1)}, f32[16,16,128]{2,1,0:T(8,128)S(1)}, f32[16,8,128]{2,1,0:T(8,128)S(1...) custom-call(s32[2]{0:T(128)S(1)} %pad_add_fusion.refs_0_.place, ...), custom_call_target="tpu_custom_call" | custom-call | tf_op jit(solution)/shard_map/partial_levels/pallas_call | solution.py:379
  4.3 8.8 %collective-permute-start = (f32[18,8,128]{2,1,0:T(8,128)S(1)}, f32[18,8,128]{2,1,0:T(8,128)S(1)}, u32[]{:S(2)}, u32[]{:S(2)}) collective-permute-start(f32[18,8,128]{2,1,0:T(8,128)S(1)} %get-tuple-element.23), channel_id=1, source_target_pairs={{0,4},{4,0},{8,12},{12,8},{16,20},{20,16},{24,28},{28,24},{1,5},{5... | collective-permute-start | bytes 221192 | tf_op jit(solution)/shard_map/ppermute | solution.py:409
  13.1 1.9 %collective-permute-start.1 = (f32[18,8,128]{2,1,0:T(8,128)S(1)}, f32[18,8,128]{2,1,0:T(8,128)S(1)}, u32[]{:S(2)}, u32[]{:S(2)}) collective-permute-start(f32[18,8,128]{2,1,0:T(8,128)S(1)} %get-tuple-element.24), channel_id=1, source_target_pairs={{4,8},{8,4},{12,16},{16,12},{20,24},{24,20},{5,9},{9,5},{13,17},{1... | collective-permute-start | bytes 221192 | tf_op jit(solution)/shard_map/ppermute | solution.py:410
  15.1 0.0 collective-permute-done.got_a
  15.1 3.7 %collective-permute-done.1.got_b = f32[18,8,128]{2,1,0:T(8,128)S(1)} collective-permute-done((f32[18,8,128]{2,1,0:T(8,128)S(1)}, f32[18,8,128]{2,1,0:T(8,128)S(1)}, u32[]{:S(2)}, u32[]{:S(2)}) %collective-permute-start.1) | collective-permute-done | bytes 73760 | tf_op jit(solution)/shard_map/ppermute | solution.py:410
  18.8 0.7 %collective-permute-start.3 = (f32[88,128]{1,0:T(8,128)S(1)}, f32[88,128]{1,0:T(8,128)S(1)}, u32[]{:S(2)}, u32[]{:S(2)}) collective-permute-start(f32[88,128]{1,0:T(8,128)S(1)} %fusion), channel_id=1, source_target_pairs={{1,2},{2,1},{5,6},{6,5},{9,10},{10,9},{13,14},{14,13},{17,18},{18,... | collective-permute-start | bytes 135176 | tf_op jit(solution)/shard_map/ppermute | solution.py:417
  19.5 1.9 %collective-permute-start.2 = (f32[88,128]{1,0:T(8,128)S(1)}, f32[88,128]{1,0:T(8,128)S(1)}, u32[]{:S(2)}, u32[]{:S(2)}) collective-permute-start(f32[88,128]{1,0:T(8,128)S(1)} %fusion), channel_id=1, source_target_pairs={{0,1},{1,0},{2,3},{3,2},{4,5},{5,4},{6,7},{7,6},{8,9},{9,8},{10,11... | collective-permute-start | bytes 135176 | tf_op jit(solution)/shard_map/ppermute | solution.py:416
  21.4 0.0 copy-start.3
  21.4 39.6 %all_gather.3.refs_1_ = f32[512,128]{1,0:T(8,128)S(1)} all-gather(f32[16,128]{1,0:T(8,128)S(1)} %get-tuple-element.18), channel_id=1, replica_groups=mesh['grp'=16,'ty'=8,'tx'=4] {'ty','tx'}, dimensions={0}, use_global_device_ids=true | all-gather | bytes 270336 | tf_op jit(solution)/shard_map/all_gather | solution.py:408
  61.0 0.0 collective-permute-done.3.side_b
  61.0 0.0 collective-permute-done.2.side_a
  61.0 0.0 copy-done.1
  61.0 0.0 copy-done.3
  61.0 1.3 %fine_laplacians.1 = (f32[3,64,128]{2,1,0:T(8,128)S(1)}, f32[3,40,128]{2,1,0:T(8,128)S(1)}, f32[3,24,128]{2,1,0:T(8,128)S(1)}, f32[3,16,128]{2,1,0:T(8,128)S(1)}, f32[16,8,128]{2,1,0:T(8,128)S(1)}) custom-call(s32[2]{0:T(128)S(1)} %pad_add_fusion.refs_0_.place, f32[4,3]{1,0:T(4,128)S(1)} %copy-done.4, f32[12,64,128]{2,1,0:T(8,128)S(1)} %bitcast.8, ...), custom_call_target="tpu_custom_call" | custom-call | tf_op jit(solution)/shard_map/fine_laplacians/pallas_call | solution.py:418
  62.4 2.4 %collapse.1 = f32[3,64,128]{2,1,0:T(8,128)} custom-call(s32[2]{0:T(128)S(1)} %pad_add_fusion.refs_0_.place, f32[512,128]{1,0:T(8,128)S(1)} %all_gather.3.refs_1_, f32[3,64,128]{2,1,0:T(8,128)S(1)} %get-tuple-element.26.refs_2_, f32[3,40,128]{2,1,0:T(8,128)S(1)} %get-tuple-element.27.refs_3_, f32[3,24,128]{2,1,0:T(8,128)S(1)} %get-tuple-element.28.refs_4_, ...), custom_call_target="tpu_custom_call" | custom-call | tf_op jit(solution)/shard_map/collapse/pallas_call | solution.py:438
  (2 shorter events, 0.0 us)
Async XLA Ops:
  0.0 0.7 %copy-start.4 = (f32[4,3]{1,0:T(4,128)S(1)}, f32[4,3]{1,0:T(4,128)}, u32[]{:S(2)}) copy-start(f32[4,3]{1,0:T(4,128)} %gains.1) | copy-start | bytes 148
  0.7 1.0 %copy-start = (f32[4,3,64,128]{3,2,1,0:T(8,128)S(1)}, f32[4,3,64,128]{3,2,1,0:T(8,128)}, u32[]{:S(2)}) copy-start(f32[4,3,64,128]{3,2,1,0:T(8,128)} %param.3) | copy-start | bytes 1179652
  1.7 0.8 %copy-start.2 = (s32[64,128]{1,0:T(8,128)S(1)}, s32[64,128]{1,0:T(8,128)}, u32[]{:S(2)}) copy-start(s32[64,128]{1,0:T(8,128)} %labels.1) | copy-start | bytes 98308
  2.4 58.6 %copy-start.1 = (f32[4,3,64,128]{3,2,1,0:T(8,128)S(1)}, f32[4,3,64,128]{3,2,1,0:T(8,128)}, u32[]{:S(2)}) copy-start(f32[4,3,64,128]{3,2,1,0:T(8,128)} %param.3) | copy-start | bytes 1179652
  4.3 10.7 %collective-permute-start = (f32[18,8,128]{2,1,0:T(8,128)S(1)}, f32[18,8,128]{2,1,0:T(8,128)S(1)}, u32[]{:S(2)}, u32[]{:S(2)}) collective-permute-start(f32[18,8,128]{2,1,0:T(8,128)S(1)} %get-tuple-element.23), channel_id=1, source_target_pairs={{0,4},{4,0},{8,12},{12,8},{16,20},{20,16},{24,28},{28,24},{1,5},{5... | collective-permute-start | bytes 221192 | tf_op jit(solution)/shard_map/ppermute | solution.py:409
  13.1 5.7 %collective-permute-start.1 = (f32[18,8,128]{2,1,0:T(8,128)S(1)}, f32[18,8,128]{2,1,0:T(8,128)S(1)}, u32[]{:S(2)}, u32[]{:S(2)}) collective-permute-start(f32[18,8,128]{2,1,0:T(8,128)S(1)} %get-tuple-element.24), channel_id=1, source_target_pairs={{4,8},{8,4},{12,16},{16,12},{20,24},{24,20},{5,9},{9,5},{13,17},{1... | collective-permute-start | bytes 221192 | tf_op jit(solution)/shard_map/ppermute | solution.py:410
  18.8 42.2 %collective-permute-start.3 = (f32[88,128]{1,0:T(8,128)S(1)}, f32[88,128]{1,0:T(8,128)S(1)}, u32[]{:S(2)}, u32[]{:S(2)}) collective-permute-start(f32[88,128]{1,0:T(8,128)S(1)} %fusion), channel_id=1, source_target_pairs={{1,2},{2,1},{5,6},{6,5},{9,10},{10,9},{13,14},{14,13},{17,18},{18,... | collective-permute-start | bytes 135176 | tf_op jit(solution)/shard_map/ppermute | solution.py:417
  19.5 41.5 %collective-permute-start.2 = (f32[88,128]{1,0:T(8,128)S(1)}, f32[88,128]{1,0:T(8,128)S(1)}, u32[]{:S(2)}, u32[]{:S(2)}) collective-permute-start(f32[88,128]{1,0:T(8,128)S(1)} %fusion), channel_id=1, source_target_pairs={{0,1},{1,0},{2,3},{3,2},{4,5},{5,4},{6,7},{7,6},{8,9},{9,8},{10,11... | collective-permute-start | bytes 135176 | tf_op jit(solution)/shard_map/ppermute | solution.py:416
  21.4 39.6 %copy-start.3 = (s32[64,128]{1,0:T(8,128)S(1)}, s32[64,128]{1,0:T(8,128)}, u32[]{:S(2)}) copy-start(s32[64,128]{1,0:T(8,128)} %labels.1) | copy-start | bytes 98308

commit v2 on v1

v2 whole, which is shorter than its diff:
```python
import jax
import jax.numpy as jnp
from jax import lax
from jax.experimental import pallas as pl
from jax.experimental.pallas import tpu as pltpu
from jax.sharding import PartitionSpec as P

EXPOSURES = 4
BANDS = 3
INNER = EXPOSURES * BANDS
PLANES = INNER + EXPOSURES
LANES = 128
HALF = LANES // 2

SIDE = (64, 32, 16, 8, 4, 2, 1)
WIDE = (128, 64, 32, 16, 8, 4, 2)
ROWS = (64, 40, 24, 16, 8, 8, 8)
PAIRS = (32, 20, 12, 6, 4)
SLOTS = 3
MOVES = (
    (1, 0, 0, 0), (1, 1, 1, 0),
    (2, 0, 0, 66), (2, 1, 1, 66), (2, 2, 2, 0),
    (3, 0, 2, 35), (3, 1, 2, 54), (3, 2, 2, 73),
    (4, 0, 2, 92), (4, 1, 2, 103), (4, 2, 2, 114),
)
STRIP_AT = (0, 0, 0, 24, 40)
STRIP = 48
PITCH_5 = 16
PITCH_6 = 8
AT_6 = 80
RIMS = 2 * SLOTS + 6
COARSE = 6

f32 = jnp.float32
bf16 = jnp.bfloat16


def iota(shape, dim):
    return lax.broadcasted_iota(jnp.int32, shape, dim)


def reduce_weights(first):
    tap = iota((LANES, LANES), 0) - 2 * iota((LANES, LANES), 1) + first
    near = jnp.where((tap == 1) | (tap == 3), 0.25, 0.0)
    ends = jnp.where((tap == 0) | (tap == 4), 0.0625, 0.0)
    weights = jnp.where(tap == 2, 0.375, near + ends).astype(bf16)
    return jnp.concatenate([weights, weights], 0)


def expand_taps(source, target):
    away = 2 * source - target
    even = jnp.where(away == 0, 0.75, 0.0) + jnp.where((away == 2) | (away == -2), 0.125, 0.0)
    odd = jnp.where((away == 1) | (away == -1), 0.5, 0.0)
    return jnp.where(jnp.bitwise_and(target, 1) == 1, odd, even)


def expand_weights(first):
    shape = (LANES, LANES)
    weights = expand_taps(iota(shape, 0) - 1, iota(shape, 1) - first).astype(bf16)
    return jnp.concatenate([weights, weights], 0)


def split_dot(values, weights):
    high = values.astype(bf16)
    low = (values - high.astype(f32)).astype(bf16)
    return jnp.dot(jnp.concatenate([high, low], 1), weights, preferred_element_type=f32)


def in_slab(level, row, col, rows, cols):
    shape = (ROWS[level], LANES)
    along, across = iota(shape, 0), iota(shape, 1)
    first = jnp.where(row == 0, 1, 0)
    last = jnp.where(row == rows - 1, SIDE[level] + 1, ROWS[level])
    left = jnp.where(col == 0, 1, 0)
    right = jnp.where(col == cols - 1, WIDE[level] + 1, LANES)
    return (along >= first) & (along < last) & (across >= left) & (across < right)


def expand_rows(source, target, count):
    before = source[:, 0:count, :]
    centre = source[:, 1 : count + 1, :]
    after = source[:, 2 : count + 2, :]
    target[:, pl.ds(0, count, stride=2), :] = (before + centre) * 0.5
    target[:, pl.ds(1, count, stride=2), :] = centre * 0.75 + (before + after) * 0.125


def expand_rows_tile(source, target, count):
    before = source[:, 0:count, :]
    centre = source[:, 1 : count + 1, :]
    after = source[:, 2 : count + 2, :]
    target[:, pl.ds(0, count, stride=2), :] = centre * 0.75 + (before + after) * 0.125
    target[:, pl.ds(1, count, stride=2), :] = (centre + after) * 0.5


def plane_of(level, p):
    return pl.ds(p * ROWS[level], ROWS[level])


def line_of(level, line):
    return pl.ds(line, PLANES, stride=ROWS[level])


def partial_kernel(
    rows, cols, images, gains, labels,
    x1, x2, x3, x4, send_a, send_b, strip_a, strip_b,
    s0, s1, s2, s3, s4, s5, y5, y6, across, label, gain, first_part, other_part, low, high, done,
):
    row, col = lax.axis_index("ty"), lax.axis_index("tx")
    s0[:, 0:8, :] = jnp.zeros((PLANES, 8, LANES), f32)
    s0[:, 72:88, :] = jnp.zeros((PLANES, 16, LANES), f32)
    copies = [pltpu.make_async_copy(labels, label, done.at[INNER])]
    copies.append(pltpu.make_async_copy(gains, gain, done.at[INNER + 1]))
    for p in range(INNER):
        copies.append(pltpu.make_async_copy(images.at[p], s0.at[p, pl.ds(8, 64)], done.at[p]))
    for copy in copies:
        copy.start()
    for store in (s1, s2, s3, s4, s5):
        depth = store.shape[1]
        store[:, 0:8, :] = jnp.zeros((PLANES, 8, LANES), f32)
        store[:, depth - 8 : depth, :] = jnp.zeros((PLANES, 8, LANES), f32)
    edge_weights, weights = reduce_weights(4), reduce_weights(3)

    def reduce_rows(source, level, first, planes, scales):
        count = ROWS[level]
        for p in planes:
            tap = [source[p, pl.ds(first + k, count, stride=2), :] for k in range(5)]
            total = tap[2] * 0.375 + (tap[1] + tap[3]) * 0.25 + (tap[0] + tap[4]) * 0.0625
            across[plane_of(level, p), :] = total if scales is None else total * scales[p]

    def reduce_columns(level, planes, weights):
        count, held = ROWS[level], planes[-1] + 1 - planes[0]
        inside = in_slab(level, row, col, rows, cols)
        values = across[pl.ds(planes[0] * count, held * count), :]
        result = split_dot(values, weights).reshape(held, count, LANES)
        return jnp.where(inside[None], result, 0.0)

    def finish(level, planes, result, store, out):
        count, held = ROWS[level], len(planes)
        if out is not None:
            out[pl.ds(planes[0] * count, held * count), :] = result.reshape(held * count, LANES)
        if store is not None:
            store[planes[0] : planes[0] + held, 8 : 8 + count, :] = result

    copies[0].wait()
    for e in range(EXPOSURES):
        s0[INNER + e, 8:72, :] = jnp.where(label[...] == e, 1.0, 0.0)
    planes = range(INNER, PLANES)
    reduce_rows(s0, 1, 4, planes, None)
    finish(1, planes, reduce_columns(1, planes, edge_weights), s1, x1)
    copies[1].wait()
    for e in range(EXPOSURES):
        planes = range(e * BANDS, (e + 1) * BANDS)
        scales = {e * BANDS + b: gain[e, b] for b in range(BANDS)}
        for p in planes:
            copies[2 + p].wait()
        reduce_rows(s0, 1, 4, planes, scales)
        finish(1, planes, reduce_columns(1, planes, edge_weights), s1, x1)
    planes = range(PLANES)
    stores = ((2, s1, s2, x2), (3, s2, s3, x3), (4, s3, s4, x4), (5, s4, s5, y5), (6, s5, None, y6))
    for level, source, store, out in stores:
        reduce_rows(source, level, 5, planes, None)
        finish(level, planes, reduce_columns(level, planes, weights), store, out)

    patch = jnp.zeros((PLANES, LANES), f32)
    for k in range(SIDE[5] + 3):
        line = y5[line_of(5, k), :]
        patch = patch + (pltpu.roll(line, PITCH_5 * k, 1) if k else line)
    for k in range(SIDE[6] + 3):
        patch = patch + pltpu.roll(y6[line_of(6, k), :], AT_6 + PITCH_6 * k, 1)
    lane = iota((PLANES, LANES), 1)
    start = PITCH_5 * (SIDE[5] * row - 1) + WIDE[5] * col - 1
    turned = pltpu.roll(patch, jnp.bitwise_and(start, LANES - 1), 1)
    coarse = []
    for k in range(2):
        away = lane + (LANES * k - start)
        coarse.append(jnp.where((away >= 0) & (away < AT_6), turned, 0.0))
    start = PITCH_6 * (row - 1) + WIDE[6] * col - 1
    turned = pltpu.roll(patch, jnp.bitwise_and(start - AT_6, LANES - 1), 1)
    away = lane - start
    held = (away >= 0) & (away < 4 * PITCH_6) & (lane < PITCH_6 * rows)
    coarse.append(jnp.where(held, turned, 0.0))
    for k in range(3):
        send_a[RIMS + 2 * k : RIMS + 2 * k + 2] = coarse[k].reshape(2, 8, LANES)

    levels = (None, x1, x2, x3, x4)
    for level in range(1, 5):
        count, wide = ROWS[level], WIDE[level]
        lane = iota((count, LANES), 1)
        before = jnp.zeros((count, LANES), f32)
        after = jnp.zeros((count, LANES), f32)
        for p in range(PLANES):
            plane = levels[level][plane_of(level, p), :]
            at = 3 * p if level == 1 else HALF + 3 * p
            here = (lane >= at) & (lane < at + 3)
            before = jnp.where(here, pltpu.roll(plane, at, 1) if at else plane, before)
            after = jnp.where(here, pltpu.roll(plane, (at - wide) % LANES, 1), after)
        before = jnp.where(col == 0, 0.0, before)
        after = jnp.where(col == cols - 1, 0.0, after)
        odd = jnp.bitwise_and(col, 1) == 1
        for k, strip in enumerate((jnp.where(odd, before, after), jnp.where(odd, after, before))):
            if level == 1:
                first_part[k] = strip
            else:
                other_part[k, pl.ds(STRIP_AT[level], count), :] = strip
    for k, strip in enumerate((strip_a, strip_b)):
        strip[0:5] = (first_part[k] + other_part[k, 0:40, :]).reshape(5, 8, LANES)
        strip[5] = other_part[k, 40:48, :]

    low[...] = jnp.zeros((RIMS, 8, LANES), f32)
    high[...] = jnp.zeros((RIMS, 8, LANES), f32)
    for rim, at in ((low, (0,) * 5), (high, SIDE)):
        slots = [None] * SLOTS
        for level, line, slot, lane in MOVES:
            values = levels[level][line_of(level, at[level] + line), :]
            values = pltpu.roll(values, lane, 1) if lane else values
            slots[slot] = values if slots[slot] is None else slots[slot] + values
        for k in range(SLOTS):
            rim[2 * k : 2 * k + 2] = slots[k].reshape(2, 8, LANES)
    for k in range(2):
        at = 2 * SLOTS + 3 * k
        low[at, 0:3, :] = other_part[k, 0:3, :]
        low[at + 1, 0:3, :] = other_part[k, 24:27, :]
        low[at + 1, 0:2, :] += first_part[k, 0:2, :]
        low[at + 2, 4:7, :] = other_part[k, 40:43, :]
        high[at, 0:3, :] = other_part[k, 16:19, :]
        high[at, 0:2, :] += first_part[k, 32:34, :]
        high[at + 1, 0:3, :] = other_part[k, 32:35, :]
        high[at + 2, 0:3, :] = other_part[k, 44:47, :]
    odd = jnp.bitwise_and(row, 1) == 1
    downward = jnp.where(row == 0, 0.0, low[...])
    upward = jnp.where(row == rows - 1, 0.0, high[...])
    send_a[0:RIMS] = jnp.where(odd, downward, upward)
    send_b[...] = jnp.where(odd, upward, downward)


def tables_kernel(after, inner, tile, top):
    inner[...] = expand_weights(1)
    tile[...] = expand_weights(0)
    source, target = iota((LANES, 2 * LANES), 0), iota((LANES, 2 * LANES), 1)
    along = expand_taps(lax.shift_right_logical(source, 3), lax.shift_right_logical(target, 4))
    aside = expand_taps(jnp.bitwise_and(source, 7), jnp.bitwise_and(target, 15))
    weights = (along * aside).astype(bf16)
    top[...] = jnp.concatenate([weights, weights], 0)


def fine_kernel(
    gains, images, labels, x1, x2, x3, x4, got_a, got_b, side_a, side_b, inner, tile,
    b0, b1, b2, b3, t4,
    t1, t2, t3, left, right, across, spread,
):
    row_odd = jnp.bitwise_and(lax.axis_index("ty"), 1) == 1
    col_odd = jnp.bitwise_and(lax.axis_index("tx"), 1) == 1
    left[...] = jnp.where(col_odd, side_a[0:6], side_b[0:6]).reshape(STRIP, LANES)
    right[...] = jnp.where(col_odd, side_b[0:6], side_a[0:6]).reshape(STRIP, LANES)

    totals = (None, t1, t2, t3, t4)
    parts = (None, x1, x2, x3, x4)
    for level in range(1, 5):
        count, wide, at = ROWS[level], WIDE[level], STRIP_AT[level]
        lane = iota((count, LANES), 1)
        from_left = left[at : at + count, :]
        from_right = right[at : at + count, :]
        start = 0 if level == 1 else HALF
        for p in range(PLANES):
            first = pltpu.roll(from_left, (-start - 3 * p) % LANES, 1) if start + p else from_left
            last = pltpu.roll(from_right, (wide - start - 3 * p) % LANES, 1)
            last = jnp.where((lane >= wide) & (lane < wide + 3), last, 0.0)
            place = plane_of(level, p)
            totals[level][place, :] = parts[level][place, :] + jnp.where(lane < 3, first, last)
    rims_a, rims_b = got_a[0 : 2 * SLOTS], got_b[0 : 2 * SLOTS]
    below = jnp.where(row_odd, rims_a, rims_b).reshape(SLOTS, PLANES, LANES)
    above = jnp.where(row_odd, rims_b, rims_a).reshape(SLOTS, PLANES, LANES)
    for rim, at in ((below, (0,) * 5), (above, SIDE)):
        for level, line, slot, lane in MOVES:
            values = rim[slot]
            values = pltpu.roll(values, LANES - lane, 1) if lane else values
            totals[level][line_of(level, at[level] + line), :] += values

    for level in (3, 2, 1):
        source, count, out = totals[level + 1], ROWS[level + 1], (None, b1, b2, b3)[level]
        wide = split_dot(source[0 : INNER * count, :], inner[...])
        across[:, 0:count, :] = wide.reshape(INNER, count, LANES)
        if level == 3:
            spread[:, 0 : ROWS[3], :] = jnp.zeros((INNER, ROWS[3], LANES), f32)
        expand_rows(across, spread, PAIRS[level])
        here = totals[level]
        for b in range(BANDS):
            total = jnp.zeros((ROWS[level], LANES), f32)
            for e in range(EXPOSURES):
                p = e * BANDS + b
                laplace = here[plane_of(level, p), :] - spread[p, 0 : ROWS[level], :]
                total = total + here[plane_of(level, INNER + e), :] * laplace
            out[b] = total
    across[...] = split_dot(t1[0 : INNER * ROWS[1], :], tile[...]).reshape(INNER, ROWS[1], LANES)
    expand_rows_tile(across, spread, PAIRS[0])
    for b in range(BANDS):
        total = jnp.zeros((ROWS[0], LANES), f32)
        for e in range(EXPOSURES):
            p = e * BANDS + b
            laplace = images[p] * gains[e, b] - spread[p]
            total = total + jnp.where(labels[...] == e, laplace, 0.0)
        b0[b] = total


def collapse_kernel(
    rows, cols, coarse, other, b0, b1, b2, b3, t4, inner, tile, top_weights, out,
    v5, v6, less_5, window, c4, c3, c2, c1, across, spread,
):
    row, col = lax.axis_index("ty"), lax.axis_index("tx")
    total = (coarse[...] + other[...]).reshape(3, PLANES, LANES)

    def blend(planes, less):
        total = None
        for e in range(EXPOSURES):
            part = planes[e * BANDS : (e + 1) * BANDS, :]
            if less is not None:
                part = part - less[e * BANDS : (e + 1) * BANDS, :]
            part = part * planes[INNER + e : INNER + e + 1, :]
            total = part if total is None else total + part
        return total

    v6[...] = total[2]
    v6[INNER : INNER + BANDS, :] = blend(total[2], None)
    less_5[...] = split_dot(v6[...], top_weights[...])
    for k in range(2):
        at = LANES * k
        less = less_5[:, at : at + LANES]
        v5[:, at : at + LANES] = total[k]
        v5[INNER : INNER + BANDS, at : at + LANES] = blend(total[k], less) + less[INNER : INNER + BANDS, :]

    window[...] = jnp.zeros((PLANES * 8, LANES), f32)
    lane = iota((PLANES, LANES), 1)
    first, second = v5[:, 0:LANES], v5[:, LANES : 2 * LANES]
    where = lane + (WIDE[5] * col - 1)
    valid = (where >= 0) & (where < WIDE[5] * cols) & (lane < WIDE[5] + 3)
    for k in range(SIDE[5] + 3):
        line = SIDE[5] * row - 1 + k
        start = PITCH_5 * jnp.bitwise_and(line, 7) + WIDE[5] * col - 1
        turned = pltpu.roll(jnp.where(line < 8, first, second), jnp.bitwise_and(-start, LANES - 1), 1)
        held = valid & (line >= 0) & (line < SIDE[5] * rows)
        window[line_of(5, k), :] = jnp.where(held, turned, 0.0)

    across[:, 0:8, :] = split_dot(window[...], inner[...]).reshape(PLANES, 8, LANES)
    expand_rows(across, spread, PAIRS[4])
    inside = in_slab(4, row, col, rows, cols)
    for b in range(BANDS):
        total = spread[INNER + b, 0:8, :]
        for e in range(EXPOSURES):
            p = e * BANDS + b
            laplace = t4[plane_of(4, p), :] - spread[p, 0:8, :]
            total = total + t4[plane_of(4, INNER + e), :] * laplace
        c4[b] = jnp.where(inside, total, 0.0)
    c4[BANDS] = jnp.zeros((8, LANES), f32)

    for level, source, target, band in ((3, c4, c3, b3), (2, c3, c2, b2), (1, c2, c1, b1)):
        count, depth = ROWS[level + 1], ROWS[level]
        wide = split_dot(source[...].reshape(EXPOSURES * count, LANES), inner[...])
        across[0:EXPOSURES, 0:count, :] = wide.reshape(EXPOSURES, count, LANES)
        if level == 3:
            spread[0:BANDS, 0:depth, :] = jnp.zeros((BANDS, depth, LANES), f32)
        expand_rows(across.at[0:BANDS], spread.at[0:BANDS], PAIRS[level])
        inside = in_slab(level, row, col, rows, cols)
        for b in range(BANDS):
            target[b] = jnp.where(inside, band[b] + spread[b, 0:depth, :], 0.0)
        target[BANDS] = jnp.zeros((depth, LANES), f32)
    wide = split_dot(c1[...].reshape(EXPOSURES * ROWS[1], LANES), tile[...])
    across[0:EXPOSURES] = wide.reshape(EXPOSURES, ROWS[1], LANES)
    expand_rows_tile(across.at[0:BANDS], spread.at[0:BANDS], PAIRS[0])
    out[...] = b0[...] + spread[0:BANDS]


VMEM = pl.BlockSpec(memory_space=pltpu.VMEM)
SMEM = pl.BlockSpec(memory_space=pltpu.SMEM)
HBM = pl.BlockSpec(memory_space=pltpu.HBM)
PARAMS = pltpu.CompilerParams(vmem_limit_bytes=32 * 1024 * 1024)


def floats(*shape):
    return jax.ShapeDtypeStruct(shape, f32)


def halves(*shape):
    return jax.ShapeDtypeStruct(shape, bf16)


def scratch(*shape):
    return pltpu.VMEM(shape, f32)


def swaps(size, first):
    return [(i, ((i - first) ^ 1) + first) for i in range(first, size - first)]


def around(size):
    return swaps(size, 1) + [(0, size - 1), (size - 1, 0)]


def shards(images, gains, labels):
    rows, cols = lax.axis_size("ty"), lax.axis_size("tx")
    images = images.reshape(INNER, ROWS[0], LANES)
    levels = [floats(PLANES * ROWS[level], LANES) for level in range(1, 5)]
    x1, x2, x3, x4, send_a, send_b, strip_a, strip_b = pl.pallas_call(
        lambda *refs: partial_kernel(rows, cols, *refs),
        out_shape=[
            *levels,
            floats(RIMS + COARSE, 8, LANES),
            floats(RIMS, 8, LANES),
            floats(6, 8, LANES),
            floats(6, 8, LANES),
        ],
        in_specs=[HBM] * 3,
        out_specs=[VMEM] * 8,
        scratch_shapes=[
            scratch(PLANES, 88, LANES),
            scratch(PLANES, 56, LANES),
            scratch(PLANES, 40, LANES),
            scratch(PLANES, 24, LANES),
            scratch(PLANES, 24, LANES),
            scratch(PLANES, 24, LANES),
            scratch(PLANES * 8, LANES),
            scratch(PLANES * 8, LANES),
            scratch(PLANES * ROWS[1], LANES),
            pltpu.VMEM((ROWS[0], LANES), jnp.int32),
            pltpu.SMEM((EXPOSURES, BANDS), f32),
            scratch(2, ROWS[1], LANES),
            scratch(2, STRIP, LANES),
            scratch(RIMS, 8, LANES),
            scratch(RIMS, 8, LANES),
            pltpu.SemaphoreType.DMA((INNER + 2,)),
        ],
        compiler_params=PARAMS,
        name="partial_levels",
    )(images, gains, labels)
    inner, tile, top = pl.pallas_call(
        tables_kernel,
        out_shape=[halves(2 * LANES, LANES), halves(2 * LANES, LANES), halves(2 * LANES, 2 * LANES)],
        in_specs=[VMEM],
        out_specs=[VMEM] * 3,
        compiler_params=PARAMS,
        name="expand_tables",
    )(strip_a)
    got_a = lax.ppermute(send_a, "ty", swaps(rows, 0))
    coarse = send_a[RIMS:] + got_a[RIMS:]
    got_b = lax.ppermute(jnp.concatenate([send_b, coarse], 0), "ty", around(rows))
    coarse = coarse + got_b[RIMS:]
    odd = lax.axis_index("ty") % 2 == 1
    rims_a, rims_b = got_a[2 * SLOTS : RIMS], got_b[2 * SLOTS : RIMS]
    below, above = jnp.where(odd, rims_a, rims_b), jnp.where(odd, rims_b, rims_a)
    strips = []
    for k, strip in enumerate((strip_a, strip_b)):
        low, high = below[3 * k : 3 * k + 3], above[3 * k : 3 * k + 3]
        none = jnp.zeros((1, 8, LANES), f32)
        rims = [low[0:1], none, high[0:1], low[1:2], high[1:2], low[2:3] + high[2:3]]
        strips.append(strip + jnp.concatenate(rims, 0))
    side_a = lax.ppermute(jnp.concatenate([strips[0], coarse], 0), "tx", swaps(cols, 0))
    coarse = coarse + side_a[6:]
    side_b = lax.ppermute(jnp.concatenate([strips[1], coarse], 0), "tx", around(cols))
    coarse = coarse + side_b[6:]
    other = lax.ppermute(coarse, "ty", [(i, (i + rows // 2) % rows) for i in range(rows)])
    b0, b1, b2, b3, t4 = pl.pallas_call(
        fine_kernel,
        out_shape=[floats(BANDS, ROWS[level], LANES) for level in range(4)] + [levels[3]],
        in_specs=[SMEM] + [VMEM] * 12,
        out_specs=[VMEM] * 5,
        scratch_shapes=[
            scratch(PLANES * ROWS[1], LANES),
            scratch(PLANES * ROWS[2], LANES),
            scratch(PLANES * ROWS[3], LANES),
            scratch(STRIP, LANES),
            scratch(STRIP, LANES),
            scratch(INNER, ROWS[1], LANES),
            scratch(INNER, ROWS[0], LANES),
        ],
        compiler_params=PARAMS,
        name="fine_laplacians",
    )(gains, images, labels, x1, x2, x3, x4, got_a, got_b, side_a, side_b, inner, tile)
    return pl.pallas_call(
        lambda *refs: collapse_kernel(rows, cols, *refs),
        out_shape=floats(BANDS, ROWS[0], LANES),
        in_specs=[VMEM] * 10,
        out_specs=VMEM,
        scratch_shapes=[
            scratch(PLANES, 2 * LANES),
            scratch(PLANES, LANES),
            scratch(PLANES, 2 * LANES),
            scratch(PLANES * 8, LANES),
            scratch(EXPOSURES, ROWS[4], LANES),
            scratch(EXPOSURES, ROWS[3], LANES),
            scratch(EXPOSURES, ROWS[2], LANES),
            scratch(EXPOSURES, ROWS[1], LANES),
            scratch(PLANES, ROWS[1], LANES),
            scratch(PLANES, ROWS[0], LANES),
        ],
        compiler_params=PARAMS,
        name="collapse",
    )(coarse, other, b0, b1, b2, b3, t4, inner, tile, top)


def solution(mesh):
    placed = (P(None, None, ("grp", "ty"), "tx"), P(), P(("grp", "ty"), "tx"))
    return jax.shard_map(
        shards, mesh=mesh, in_specs=placed, out_specs=P(None, ("grp", "ty"), "tx"), check_vma=False
    )
```

time: 65.1 us -> 40.7 us (0.63)
  the two profiles are of different devices: /device:TPU:1 before, /device:TPU:4 now
where the time goes in v2:
time: 40.7 us; the launch traced here: 40.2 us
  starting transfers between devices  21.6 us (53%)
  waiting for transfers between devices  9.41 us (23%)
  Pallas kernels  5.8 us (14%)
  local copies, waits for them, and re-layouts  3.12 us (8%)
    ppermute x1, starting transfers between devices, shards(): lax.ppermute(coarse, 'ty', [(i, (i + rows // 2) % rows) for i in range(ro...  9.12 us
    ppermute x1, starting transfers between devices, shards(): lax.ppermute(jnp.concatenate([strips[1], coarse], 0), 'tx', around(cols))  4.92 us
    ppermute x1, starting transfers between devices, shards(): lax.ppermute(jnp.concatenate([strips[0], coarse], 0), 'tx', swaps(cols, 0))  3.48 us
    ppermute x1, waiting for transfers between devices, shards(): lax.ppermute(jnp.concatenate([send_b, coarse], 0), 'ty', around(rows))  3.44 us
    unnamed x17, local copies, waits for them, and re-layouts  3.12 us
    pallas_call x1, Pallas kernels, shards(): pl.pallas_call(lambda *refs: partial_kernel(rows, cols, *refs), out_shape...  2.58 us
    ppermute x1, waiting for transfers between devices, shards(): lax.ppermute(jnp.concatenate([strips[0], coarse], 0), 'tx', swaps(cols, 0))  2.48 us
    ppermute x1, waiting for transfers between devices, shards(): lax.ppermute(jnp.concatenate([strips[1], coarse], 0), 'tx', around(cols))  2.26 us
  transfers between devices with their start and end apart: 5, of which 4 were waited for; matrix products, arithmetic and copies ran while one was open for 0% of the time, Pallas kernels for 4%

profile of v2, /device:TPU:4, one launch (start us, length us, event | category | flops | bytes accessed | tf_op | source)
XLA Modules:
  0.0 40.2 jit_solution(9294053191797444007)
XLA Ops:
  0.0 0.0 copy-start
  0.0 1.0 %copy-done = f32[4,3,64,128]{3,2,1,0:T(8,128)S(1)} copy-done((f32[4,3,64,128]{3,2,1,0:T(8,128)S(1)}, f32[4,3,64,128]{3,2,1,0:T(8,128)}, u32[]{:S(2)}) %copy-start) | copy-done | bytes 393240
  1.0 0.0 copy-start.2
  1.0 0.8 %copy-done.2 = s32[64,128]{1,0:T(8,128)S(1)} copy-done((s32[64,128]{1,0:T(8,128)S(1)}, s32[64,128]{1,0:T(8,128)}, u32[]{:S(2)}) %copy-start.2) | copy-done | bytes 32792
  1.8 0.7 %copy-done.4 = f32[4,3]{1,0:T(4,128)S(1)} copy-done((f32[4,3]{1,0:T(4,128)S(1)}, f32[4,3]{1,0:T(4,128)}, u32[]{:S(2)}) %copy-start.4) | copy-done | bytes 72
  2.4 2.6 %partial_levels.1 = (f32[640,128]{1,0:T(8,128)S(1)}, f32[384,128]{1,0:T(8,128)S(1)}, f32[256,128]{1,0:T(8,128)S(1)}, f32[128,128]{1,0:T(8,128)S(1)}, f32[18,8,12...) custom-call(f32[12,64,128]{2,1,0:T(8,128)S(1)} %bitcast.1, ...), custom_call_target="tpu_custom_call" | custom-call | tf_op jit(solution)/shard_map/partial_levels/pallas_call | solution.py:402
  5.0 1.9 %collective-permute-start = (f32[18,8,128]{2,1,0:T(8,128)S(1)}, f32[18,8,128]{2,1,0:T(8,128)S(1)}, u32[]{:S(2)}, u32[]{:S(2)}) collective-permute-start(f32[18,8,128]{2,1,0:T(8,128)S(1)} %get-tuple-element.21), channel_id=1, source_target_pairs={{0,4},{4,0},{8,12},{12,8},{16,20},{20,16},{24,28},{28,24},{1,5},{5... | collective-permute-start | bytes 221192 | tf_op jit(solution)/shard_map/ppermute | solution.py:442
  7.0 1.2 %collective-permute-done.got_a = f32[18,8,128]{2,1,0:T(8,128)S(1)} collective-permute-done((f32[18,8,128]{2,1,0:T(8,128)S(1)}, f32[18,8,128]{2,1,0:T(8,128)S(1)}, u32[]{:S(2)}, u32[]{:S(2)}) %collective-permute-start) | collective-permute-done | bytes 73760 | tf_op jit(solution)/shard_map/ppermute | solution.py:442
  8.2 2.2 %collective-permute-start.1 = (f32[18,8,128]{2,1,0:T(8,128)S(1)}, f32[18,8,128]{2,1,0:T(8,128)S(1)}, u32[]{:S(2)}, u32[]{:S(2)}) collective-permute-start(f32[18,8,128]{2,1,0:T(8,128)S(1)} %pad_maximum_fusion), channel_id=1, source_target_pairs={{4,8},{8,4},{12,16},{16,12},{20,24},{24,20},{0,28},{28,0},{5,9},{9... | collective-permute-start | bytes 221192 | tf_op jit(solution)/shard_map/ppermute | solution.py:444
  10.4 0.0 copy-start.1
  10.4 3.4 %collective-permute-done.1.got_b = f32[18,8,128]{2,1,0:T(8,128)S(1)} collective-permute-done((f32[18,8,128]{2,1,0:T(8,128)S(1)}, f32[18,8,128]{2,1,0:T(8,128)S(1)}, u32[]{:S(2)}, u32[]{:S(2)}) %collective-permute-start.1) | collective-permute-done | bytes 73760 | tf_op jit(solution)/shard_map/ppermute | solution.py:444
  14.0 3.5 %collective-permute-start.2 = (f32[12,8,128]{2,1,0:T(8,128)S(1)}, f32[12,8,128]{2,1,0:T(8,128)S(1)}, u32[]{:S(2)}, u32[]{:S(2)}) collective-permute-start(f32[12,8,128]{2,1,0:T(8,128)S(1)} %pad_maximum_fusion.1), channel_id=1, source_target_pairs={{0,1},{1,0},{2,3},{3,2},{4,5},{5,4},{6,7},{7,6},{8,9},{9,8},{10,11... | collective-permute-start | bytes 147464 | tf_op jit(solution)/shard_map/ppermute | solution.py:455
  17.5 2.5 %collective-permute-done.2.side_a = f32[12,8,128]{2,1,0:T(8,128)S(1)} collective-permute-done((f32[12,8,128]{2,1,0:T(8,128)S(1)}, f32[12,8,128]{2,1,0:T(8,128)S(1)}, u32[]{:S(2)}, u32[]{:S(2)}) %collective-permute-start.2) | collective-permute-done | bytes 49184 | tf_op jit(solution)/shard_map/ppermute | solution.py:455
  20.0 4.9 %collective-permute-start.3 = (f32[12,8,128]{2,1,0:T(8,128)S(1)}, f32[12,8,128]{2,1,0:T(8,128)S(1)}, u32[]{:S(2)}, u32[]{:S(2)}) collective-permute-start(f32[12,8,128]{2,1,0:T(8,128)S(1)} %pad_maximum_fusion.2), channel_id=1, source_target_pairs={{1,2},{2,1},{0,3},{3,0},{5,6},{6,5},{4,7},{7,4},{9,10},{10,9},{8,1... | collective-permute-start | bytes 147464 | tf_op jit(solution)/shard_map/ppermute | solution.py:457
  24.9 2.3 %collective-permute-done.3.side_b = f32[12,8,128]{2,1,0:T(8,128)S(1)} collective-permute-done((f32[12,8,128]{2,1,0:T(8,128)S(1)}, f32[12,8,128]{2,1,0:T(8,128)S(1)}, u32[]{:S(2)}, u32[]{:S(2)}) %collective-permute-start.3) | collective-permute-done | bytes 49184 | tf_op jit(solution)/shard_map/ppermute | solution.py:457
  27.2 9.1 %collective-permute-start.4 = (f32[6,8,128]{2,1,0:T(8,128)S(1)}, f32[6,8,128]{2,1,0:T(8,128)S(1)}, u32[]{:S(2)}, u32[]{:S(2)}) collective-permute-start(f32[6,8,128]{2,1,0:T(8,128)S(1)} %slice_add_fusion.refs_0_), channel_id=1, source_target_pairs={{0,16},{4,20},{8,24},{12,28},{16,0},{20,4},{24,8},{28,12},{1,17},{... | collective-permute-start | bytes 73736 | tf_op jit(solution)/shard_map/ppermute | solution.py:459
  36.3 0.2 expand_tables.1
  36.5 0.0 copy-start.5
  36.5 0.0 copy-done.1
  36.5 0.0 copy-done.3
  36.5 0.7 %copy-done.5 = f32[4,3]{1,0:T(4,128)S(1)} copy-done((f32[4,3]{1,0:T(4,128)S(1)}, f32[4,3]{1,0:T(4,128)}, u32[]{:S(2)}) %copy-start.5) | copy-done | bytes 72
  37.2 1.4 %fine_laplacians.1 = (f32[3,64,128]{2,1,0:T(8,128)S(1)}, f32[3,40,128]{2,1,0:T(8,128)S(1)}, f32[3,24,128]{2,1,0:T(8,128)S(1)}, f32[3,16,128]{2,1,0:T(8,128)S(1)}, f32[128,128]{1,0:T(8,128)S(1)}) custom-call(f32[4,3]{1,0:T(4,128)S(1)} %copy-done.5, f32[12,64,128]{2,1,0:T(8,128)S(1)} %bitcast.2, s32[64,128]{1,0:T(8,128)S(1)} %copy-done.3, ...), custom_call_target="tpu_custom_call" | custom-call | tf_op jit(solution)/shard_map/fine_laplacians/pallas_call | solution.py:460
  38.6 0.0 collective-permute-done.4.refs_1_
  38.6 1.7 %collapse.1 = f32[3,64,128]{2,1,0:T(8,128)} custom-call(f32[6,8,128]{2,1,0:T(8,128)S(1)} %slice_add_fusion.refs_0_, f32[6,8,128]{2,1,0:T(8,128)S(1)} %collective-permute-done.4.refs_1_, f32[3,64,128]{2,1,0:T(8,128)S(1)} %get-tuple-element.31.refs_2_, f32[3,40,128]{2,1,0:T(8,128)S(1)} %get-tuple-element.32.refs_3_, ...), custom_call_target="tpu_custom_call" | custom-call | tf_op jit(solution)/shard_map/collapse/pallas_call | solution.py:477
  (17 shorter events, 0.1 us)
Async XLA Ops:
  0.0 1.0 %copy-start = (f32[4,3,64,128]{3,2,1,0:T(8,128)S(1)}, f32[4,3,64,128]{3,2,1,0:T(8,128)}, u32[]{:S(2)}) copy-start(f32[4,3,64,128]{3,2,1,0:T(8,128)} %param.3) | copy-start | bytes 1179652
  1.0 0.8 %copy-start.2 = (s32[64,128]{1,0:T(8,128)S(1)}, s32[64,128]{1,0:T(8,128)}, u32[]{:S(2)}) copy-start(s32[64,128]{1,0:T(8,128)} %labels.1) | copy-start | bytes 98308
  1.8 0.7 %copy-start.4 = (f32[4,3]{1,0:T(4,128)S(1)}, f32[4,3]{1,0:T(4,128)}, u32[]{:S(2)}) copy-start(f32[4,3]{1,0:T(4,128)} %gains.1) | copy-start | bytes 148
  5.0 3.2 %collective-permute-start = (f32[18,8,128]{2,1,0:T(8,128)S(1)}, f32[18,8,128]{2,1,0:T(8,128)S(1)}, u32[]{:S(2)}, u32[]{:S(2)}) collective-permute-start(f32[18,8,128]{2,1,0:T(8,128)S(1)} %get-tuple-element.21), channel_id=1, source_target_pairs={{0,4},{4,0},{8,12},{12,8},{16,20},{20,16},{24,28},{28,24},{1,5},{5... | collective-permute-start | bytes 221192 | tf_op jit(solution)/shard_map/ppermute | solution.py:442
  8.2 5.7 %collective-permute-start.1 = (f32[18,8,128]{2,1,0:T(8,128)S(1)}, f32[18,8,128]{2,1,0:T(8,128)S(1)}, u32[]{:S(2)}, u32[]{:S(2)}) collective-permute-start(f32[18,8,128]{2,1,0:T(8,128)S(1)} %pad_maximum_fusion), channel_id=1, source_target_pairs={{4,8},{8,4},{12,16},{16,12},{20,24},{24,20},{0,28},{28,0},{5,9},{9... | collective-permute-start | bytes 221192 | tf_op jit(solution)/shard_map/ppermute | solution.py:444
  10.4 26.1 %copy-start.1 = (f32[4,3,64,128]{3,2,1,0:T(8,128)S(1)}, f32[4,3,64,128]{3,2,1,0:T(8,128)}, u32[]{:S(2)}) copy-start(f32[4,3,64,128]{3,2,1,0:T(8,128)} %param.3) | copy-start | bytes 1179652
  14.0 6.0 %collective-permute-start.2 = (f32[12,8,128]{2,1,0:T(8,128)S(1)}, f32[12,8,128]{2,1,0:T(8,128)S(1)}, u32[]{:S(2)}, u32[]{:S(2)}) collective-permute-start(f32[12,8,128]{2,1,0:T(8,128)S(1)} %pad_maximum_fusion.1), channel_id=1, source_target_pairs={{0,1},{1,0},{2,3},{3,2},{4,5},{5,4},{6,7},{7,6},{8,9},{9,8},{10,11... | collective-permute-start | bytes 147464 | tf_op jit(solution)/shard_map/ppermute | solution.py:455
  20.0 7.2 %collective-permute-start.3 = (f32[12,8,128]{2,1,0:T(8,128)S(1)}, f32[12,8,128]{2,1,0:T(8,128)S(1)}, u32[]{:S(2)}, u32[]{:S(2)}) collective-permute-start(f32[12,8,128]{2,1,0:T(8,128)S(1)} %pad_maximum_fusion.2), channel_id=1, source_target_pairs={{1,2},{2,1},{0,3},{3,0},{5,6},{6,5},{4,7},{7,4},{9,10},{10,9},{8,1... | collective-permute-start | bytes 147464 | tf_op jit(solution)/shard_map/ppermute | solution.py:457
  27.2 9.3 %copy-start.3 = (s32[64,128]{1,0:T(8,128)S(1)}, s32[64,128]{1,0:T(8,128)}, u32[]{:S(2)}) copy-start(s32[64,128]{1,0:T(8,128)} %labels.1) | copy-start | bytes 98308
  27.2 11.4 %collective-permute-start.4 = (f32[6,8,128]{2,1,0:T(8,128)S(1)}, f32[6,8,128]{2,1,0:T(8,128)S(1)}, u32[]{:S(2)}, u32[]{:S(2)}) collective-permute-start(f32[6,8,128]{2,1,0:T(8,128)S(1)} %slice_add_fusion.refs_0_), channel_id=1, source_target_pairs={{0,16},{4,20},{8,24},{12,28},{16,0},{20,4},{24,8},{28,12},{1,17},{... | collective-permute-start | bytes 73736 | tf_op jit(solution)/shard_map/ppermute | solution.py:459
  36.5 0.7 %copy-start.5 = (f32[4,3]{1,0:T(4,128)S(1)}, f32[4,3]{1,0:T(4,128)}, u32[]{:S(2)}) copy-start(f32[4,3]{1,0:T(4,128)} %gains.1) | copy-start | bytes 148

commit v3 on v2

--- a/solution.py
+++ b/solution.py
@@ -25,11 +25,10 @@
 )
 STRIP_AT = (0, 0, 0, 24, 40)
 STRIP = 48
-PITCH_5 = 16
-PITCH_6 = 8
-AT_6 = 80
+PITCH_5 = 8
+PITCH_6 = 6
+AT_6 = 40
 RIMS = 2 * SLOTS + 6
-COARSE = 6
 
 f32 = jnp.float32
 bf16 = jnp.bfloat16
@@ -69,10 +68,8 @@
 def in_slab(level, row, col, rows, cols):
     shape = (ROWS[level], LANES)
     along, across = iota(shape, 0), iota(shape, 1)
-    first = jnp.where(row == 0, 1, 0)
-    last = jnp.where(row == rows - 1, SIDE[level] + 1, ROWS[level])
-    left = jnp.where(col == 0, 1, 0)
-    right = jnp.where(col == cols - 1, WIDE[level] + 1, LANES)
+    first, last = 1 - SIDE[level] * row, 1 + SIDE[level] * (rows - row)
+    left, right = 1 - WIDE[level] * col, 1 + WIDE[level] * (cols - col)
     return (along >= first) & (along < last) & (across >= left) & (across < right)
 
 
@@ -100,10 +97,21 @@
     return pl.ds(line, PLANES, stride=ROWS[level])
 
 
+def patch_places(shape, dim):
+    lane = jnp.bitwise_and(iota(shape, dim), HALF - 1)
+    row_5, col_5 = lax.shift_right_logical(lane, 3), jnp.bitwise_and(lane, PITCH_5 - 1)
+    past = lane - AT_6
+    row_6 = lax.shift_right_arithmetic(past * 43, 8)
+    col_6 = past - PITCH_6 * row_6
+    is_5 = (lane < AT_6) & (col_5 < WIDE[5] + 3)
+    is_6 = (lane >= AT_6) & (col_6 < WIDE[6] + 3)
+    return (is_5, row_5, col_5), (is_6, row_6, col_6)
+
+
 def partial_kernel(
     rows, cols, images, gains, labels,
-    x1, x2, x3, x4, send_a, send_b, strip_a, strip_b,
-    s0, s1, s2, s3, s4, s5, y5, y6, across, label, gain, first_part, other_part, low, high, done,
+    s0, scale, x1, x2, x3, x4, send_a, send_b, strip_a, strip_b, patches,
+    s1, s2, s3, s4, s5, y5, y6, across, label, gain, first_part, other_part, low, high, done,
 ):
     row, col = lax.axis_index("ty"), lax.axis_index("tx")
     s0[:, 0:8, :] = jnp.zeros((PLANES, 8, LANES), f32)
@@ -148,6 +156,8 @@
     reduce_rows(s0, 1, 4, planes, None)
     finish(1, planes, reduce_columns(1, planes, edge_weights), s1, x1)
     copies[1].wait()
+    for p in range(INNER):
+        scale[p] = jnp.full((8, LANES), gain[p // BANDS, p % BANDS], f32)
     for e in range(EXPOSURES):
         planes = range(e * BANDS, (e + 1) * BANDS)
         scales = {e * BANDS + b: gain[e, b] for b in range(BANDS)}
@@ -167,20 +177,20 @@
         patch = patch + (pltpu.roll(line, PITCH_5 * k, 1) if k else line)
     for k in range(SIDE[6] + 3):
         patch = patch + pltpu.roll(y6[line_of(6, k), :], AT_6 + PITCH_6 * k, 1)
-    lane = iota((PLANES, LANES), 1)
-    start = PITCH_5 * (SIDE[5] * row - 1) + WIDE[5] * col - 1
-    turned = pltpu.roll(patch, jnp.bitwise_and(start, LANES - 1), 1)
-    coarse = []
-    for k in range(2):
-        away = lane + (LANES * k - start)
-        coarse.append(jnp.where((away >= 0) & (away < AT_6), turned, 0.0))
-    start = PITCH_6 * (row - 1) + WIDE[6] * col - 1
-    turned = pltpu.roll(patch, jnp.bitwise_and(start - AT_6, LANES - 1), 1)
-    away = lane - start
-    held = (away >= 0) & (away < 4 * PITCH_6) & (lane < PITCH_6 * rows)
-    coarse.append(jnp.where(held, turned, 0.0))
-    for k in range(3):
-        send_a[RIMS + 2 * k : RIMS + 2 * k + 2] = coarse[k].reshape(2, 8, LANES)
+    patch = patch[0:8, :] + pltpu.roll(patch[8:16, :], HALF, 1)
+    (is_5, row_5, col_5), (is_6, row_6, col_6) = patch_places((8, LANES), 1)
+    for r in range(rows):
+        down = r - row
+        rows_5 = is_5 & (row_5 + 2 * down >= 0) & (row_5 + 2 * down < SIDE[5] + 3)
+        rows_6 = is_6 & (row_6 + down >= 0) & (row_6 + down < SIDE[6] + 3)
+        for c in range(cols):
+            over = c - col
+            held = rows_5 & (col_5 + 4 * over >= 0) & (col_5 + 4 * over < WIDE[5] + 3)
+            away = jnp.bitwise_and(-(2 * PITCH_5 * down + 4 * over), LANES - 1)
+            block = jnp.where(held, pltpu.roll(patch, away, 1), 0.0)
+            held = rows_6 & (col_6 + 2 * over >= 0) & (col_6 + 2 * over < WIDE[6] + 3)
+            away = jnp.bitwise_and(-(PITCH_6 * down + 2 * over), LANES - 1)
+            patches[r * cols + c] = jnp.where(held, pltpu.roll(patch, away, 1), block)
 
     levels = (None, x1, x2, x3, x4)
     for level in range(1, 5):
@@ -229,22 +239,23 @@
     odd = jnp.bitwise_and(row, 1) == 1
     downward = jnp.where(row == 0, 0.0, low[...])
     upward = jnp.where(row == rows - 1, 0.0, high[...])
-    send_a[0:RIMS] = jnp.where(odd, downward, upward)
+    send_a[...] = jnp.where(odd, downward, upward)
     send_b[...] = jnp.where(odd, upward, downward)
 
 
 def tables_kernel(after, inner, tile, top):
     inner[...] = expand_weights(1)
     tile[...] = expand_weights(0)
-    source, target = iota((LANES, 2 * LANES), 0), iota((LANES, 2 * LANES), 1)
-    along = expand_taps(lax.shift_right_logical(source, 3), lax.shift_right_logical(target, 4))
-    aside = expand_taps(jnp.bitwise_and(source, 7), jnp.bitwise_and(target, 15))
-    weights = (along * aside).astype(bf16)
+    _, (is_6, row_6, col_6) = patch_places((LANES, LANES), 0)
+    (is_5, row_5, col_5), _ = patch_places((LANES, LANES), 1)
+    low = (iota((LANES, LANES), 0) < HALF) & (iota((LANES, LANES), 1) < HALF)
+    taps = expand_taps(row_6 - 1, row_5 - 1) * expand_taps(col_6 - 1, col_5 - 1)
+    weights = jnp.where(is_5 & is_6 & low, taps, 0.0).astype(bf16)
     top[...] = jnp.concatenate([weights, weights], 0)
 
 
 def fine_kernel(
-    gains, images, labels, x1, x2, x3, x4, got_a, got_b, side_a, side_b, inner, tile,
+    s0, scale, x1, x2, x3, x4, got_a, got_b, side_a, side_b, inner, tile,
     b0, b1, b2, b3, t4,
     t1, t2, t3, left, right, across, spread,
 ):
@@ -297,48 +308,46 @@
         total = jnp.zeros((ROWS[0], LANES), f32)
         for e in range(EXPOSURES):
             p = e * BANDS + b
-            laplace = images[p] * gains[e, b] - spread[p]
-            total = total + jnp.where(labels[...] == e, laplace, 0.0)
+            laplace = s0[p, 8:72, :] * scale[p, 0:1, :] - spread[p]
+            total = total + s0[INNER + e, 8:72, :] * laplace
         b0[b] = total
 
 
 def collapse_kernel(
-    rows, cols, coarse, other, b0, b1, b2, b3, t4, inner, tile, top_weights, out,
-    v5, v6, less_5, window, c4, c3, c2, c1, across, spread,
+    rows, cols, patches, b0, b1, b2, b3, t4, inner, tile, top_weights, out,
+    v5, window, c4, c3, c2, c1, across, spread,
 ):
     row, col = lax.axis_index("ty"), lax.axis_index("tx")
-    total = (coarse[...] + other[...]).reshape(3, PLANES, LANES)
-
-    def blend(planes, less):
+    total = patches[0]
+    for k in range(1, rows * cols):
+        total = total + patches[k]
+    lane = iota((PLANES, LANES), 1)
+    total = jnp.concatenate([total, pltpu.roll(total, HALF, 1)], 0)
+    v5[...] = jnp.where(lane < HALF, total, 0.0)
+
+    def blend(less):
         total = None
         for e in range(EXPOSURES):
-            part = planes[e * BANDS : (e + 1) * BANDS, :]
+            part = v5[e * BANDS : (e + 1) * BANDS, :]
             if less is not None:
                 part = part - less[e * BANDS : (e + 1) * BANDS, :]
-            part = part * planes[INNER + e : INNER + e + 1, :]
+            part = part * v5[INNER + e : INNER + e + 1, :]
             total = part if total is None else total + part
         return total
 
-    v6[...] = total[2]
-    v6[INNER : INNER + BANDS, :] = blend(total[2], None)
-    less_5[...] = split_dot(v6[...], top_weights[...])
-    for k in range(2):
-        at = LANES * k
-        less = less_5[:, at : at + LANES]
-        v5[:, at : at + LANES] = total[k]
-        v5[INNER : INNER + BANDS, at : at + LANES] = blend(total[k], less) + less[INNER : INNER + BANDS, :]
+    window[0:PLANES, :] = v5[...]
+    window[INNER : INNER + BANDS, :] = blend(None)
+    less = split_dot(window[0:PLANES, :], top_weights[...])
+    (is_5, row_5, col_5), _ = patch_places((BANDS, LANES), 1)
+    along, aside = row_5 + (SIDE[5] * row - 1), col_5 + (WIDE[5] * col - 1)
+    held = is_5 & (along >= 0) & (along < SIDE[5] * rows) & (aside >= 0) & (aside < WIDE[5] * cols)
+    v5[INNER : INNER + BANDS, :] = jnp.where(held, blend(less) + less[INNER : INNER + BANDS, :], 0.0)
 
     window[...] = jnp.zeros((PLANES * 8, LANES), f32)
-    lane = iota((PLANES, LANES), 1)
-    first, second = v5[:, 0:LANES], v5[:, LANES : 2 * LANES]
-    where = lane + (WIDE[5] * col - 1)
-    valid = (where >= 0) & (where < WIDE[5] * cols) & (lane < WIDE[5] + 3)
     for k in range(SIDE[5] + 3):
-        line = SIDE[5] * row - 1 + k
-        start = PITCH_5 * jnp.bitwise_and(line, 7) + WIDE[5] * col - 1
-        turned = pltpu.roll(jnp.where(line < 8, first, second), jnp.bitwise_and(-start, LANES - 1), 1)
-        held = valid & (line >= 0) & (line < SIDE[5] * rows)
-        window[line_of(5, k), :] = jnp.where(held, turned, 0.0)
+        line = v5[...]
+        line = pltpu.roll(line, LANES - PITCH_5 * k, 1) if k else line
+        window[line_of(5, k), :] = jnp.where(lane < WIDE[5] + 3, line, 0.0)
 
     across[:, 0:8, :] = split_dot(window[...], inner[...]).reshape(PLANES, 8, LANES)
     expand_rows(across, spread, PAIRS[4])
@@ -391,27 +400,26 @@
     return [(i, ((i - first) ^ 1) + first) for i in range(first, size - first)]
 
 
-def around(size):
-    return swaps(size, 1) + [(0, size - 1), (size - 1, 0)]
-
-
 def shards(images, gains, labels):
     rows, cols = lax.axis_size("ty"), lax.axis_size("tx")
     images = images.reshape(INNER, ROWS[0], LANES)
+    pinned = [pltpu.with_memory_space_constraint(x, pltpu.HBM) for x in (images, gains, labels)]
     levels = [floats(PLANES * ROWS[level], LANES) for level in range(1, 5)]
-    x1, x2, x3, x4, send_a, send_b, strip_a, strip_b = pl.pallas_call(
+    s0, scale, x1, x2, x3, x4, send_a, send_b, strip_a, strip_b, patches = pl.pallas_call(
         lambda *refs: partial_kernel(rows, cols, *refs),
         out_shape=[
+            floats(PLANES, 88, LANES),
+            floats(INNER, 8, LANES),
             *levels,
-            floats(RIMS + COARSE, 8, LANES),
+            floats(RIMS, 8, LANES),
             floats(RIMS, 8, LANES),
             floats(6, 8, LANES),
             floats(6, 8, LANES),
+            floats(rows * cols, 8, LANES),
         ],
         in_specs=[HBM] * 3,
-        out_specs=[VMEM] * 8,
+        out_specs=[VMEM] * 11,
         scratch_shapes=[
-            scratch(PLANES, 88, LANES),
             scratch(PLANES, 56, LANES),
             scratch(PLANES, 40, LANES),
             scratch(PLANES, 24, LANES),
@@ -430,21 +438,20 @@
         ],
         compiler_params=PARAMS,
         name="partial_levels",
-    )(images, gains, labels)
+    )(*pinned)
+    got_a = lax.ppermute(send_a, "ty", swaps(rows, 0))
+    got_b = lax.ppermute(send_b, "ty", swaps(rows, 1))
     inner, tile, top = pl.pallas_call(
         tables_kernel,
-        out_shape=[halves(2 * LANES, LANES), halves(2 * LANES, LANES), halves(2 * LANES, 2 * LANES)],
+        out_shape=[halves(2 * LANES, LANES)] * 3,
         in_specs=[VMEM],
         out_specs=[VMEM] * 3,
         compiler_params=PARAMS,
         name="expand_tables",
     )(strip_a)
-    got_a = lax.ppermute(send_a, "ty", swaps(rows, 0))
-    coarse = send_a[RIMS:] + got_a[RIMS:]
-    got_b = lax.ppermute(jnp.concatenate([send_b, coarse], 0), "ty", around(rows))
-    coarse = coarse + got_b[RIMS:]
+    patches = lax.all_to_all(patches, ("ty", "tx"), 0, 0, tiled=True)
     odd = lax.axis_index("ty") % 2 == 1
-    rims_a, rims_b = got_a[2 * SLOTS : RIMS], got_b[2 * SLOTS : RIMS]
+    rims_a, rims_b = got_a[2 * SLOTS :], got_b[2 * SLOTS :]
     below, above = jnp.where(odd, rims_a, rims_b), jnp.where(odd, rims_b, rims_a)
     strips = []
     for k, strip in enumerate((strip_a, strip_b)):
@@ -452,15 +459,13 @@
         none = jnp.zeros((1, 8, LANES), f32)
         rims = [low[0:1], none, high[0:1], low[1:2], high[1:2], low[2:3] + high[2:3]]
         strips.append(strip + jnp.concatenate(rims, 0))
-    side_a = lax.ppermute(jnp.concatenate([strips[0], coarse], 0), "tx", swaps(cols, 0))
-    coarse = coarse + side_a[6:]
-    side_b = lax.ppermute(jnp.concatenate([strips[1], coarse], 0), "tx", around(cols))
-    coarse = coarse + side_b[6:]
-    other = lax.ppermute(coarse, "ty", [(i, (i + rows // 2) % rows) for i in range(rows)])
+    strips, inner, tile, top = lax.optimization_barrier((strips, inner, tile, top))
+    side_a = lax.ppermute(strips[0], "tx", swaps(cols, 0))
+    side_b = lax.ppermute(strips[1], "tx", swaps(cols, 1))
     b0, b1, b2, b3, t4 = pl.pallas_call(
         fine_kernel,
         out_shape=[floats(BANDS, ROWS[level], LANES) for level in range(4)] + [levels[3]],
-        in_specs=[SMEM] + [VMEM] * 12,
+        in_specs=[VMEM] * 12,
         out_specs=[VMEM] * 5,
         scratch_shapes=[
             scratch(PLANES * ROWS[1], LANES),
@@ -473,16 +478,14 @@
         ],
         compiler_params=PARAMS,
         name="fine_laplacians",
-    )(gains, images, labels, x1, x2, x3, x4, got_a, got_b, side_a, side_b, inner, tile)
+    )(s0, scale, x1, x2, x3, x4, got_a, got_b, side_a, side_b, inner, tile)
     return pl.pallas_call(
         lambda *refs: collapse_kernel(rows, cols, *refs),
         out_shape=floats(BANDS, ROWS[0], LANES),
-        in_specs=[VMEM] * 10,
+        in_specs=[VMEM] * 9,
         out_specs=VMEM,
         scratch_shapes=[
-            scratch(PLANES, 2 * LANES),
             scratch(PLANES, LANES),
-            scratch(PLANES, 2 * LANES),
             scratch(PLANES * 8, LANES),
             scratch(EXPOSURES, ROWS[4], LANES),
             scratch(EXPOSURES, ROWS[3], LANES),
@@ -493,7 +496,7 @@
         ],
         compiler_params=PARAMS,
         name="collapse",
-    )(coarse, other, b0, b1, b2, b3, t4, inner, tile, top)
+    )(patches, b0, b1, b2, b3, t4, inner, tile, top)
 
 
 def solution(mesh):

time: 40.7 us -> 28.5 us (0.70)
  the two profiles are of different devices: /device:TPU:4 before, /device:TPU:16 now
where the time goes in v3:
time: 28.5 us; the launch traced here: 28.2 us
  starting transfers between devices  18.1 us (64%)
  Pallas kernels  6.06 us (21%)
  waiting for transfers between devices  3.8 us (13%)
    all_to_all x1, starting transfers between devices, shards(): patches = lax.all_to_all(patches, ('ty', 'tx'), 0, 0, tiled=True)  10.5 us
    pallas_call x1, Pallas kernels, shards(): pl.pallas_call(lambda *refs: partial_kernel(rows, cols, *refs), out_shape...  3.45 us
    ppermute x1, starting transfers between devices, shards(): side_a = lax.ppermute(strips[0], 'tx', swaps(cols, 0))  3.08 us
    ppermute x1, waiting for transfers between devices, shards(): side_b = lax.ppermute(strips[1], 'tx', swaps(cols, 1))  3 us
    ppermute x1, starting transfers between devices, shards(): got_a = lax.ppermute(send_a, 'ty', swaps(rows, 0))  1.92 us
    ppermute x1, starting transfers between devices, shards(): side_b = lax.ppermute(strips[1], 'tx', swaps(cols, 1))  1.92 us
    pallas_call x1, Pallas kernels, shards(): pl.pallas_call(lambda *refs: collapse_kernel(rows, cols, *refs), out_shap...  1.73 us
    pallas_call x1, Pallas kernels, shards(): pl.pallas_call(fine_kernel, out_shape=[floats(BANDS, ROWS[level], LANES)...  0.8 us
  transfers between devices with their start and end apart: 5, of which 2 were waited for; matrix products, arithmetic and copies ran while one was open for 0% of the time, Pallas kernels for 3%

profile of v3, /device:TPU:16, one launch (start us, length us, event | category | flops | bytes accessed | tf_op | source)
XLA Modules:
  0.0 28.2 jit_solution(15307424634161631408)
XLA Ops:
  0.0 3.4 %partial_levels.1 = (f32[16,88,128]{2,1,0:T(8,128)S(1)}, f32[12,8,128]{2,1,0:T(8,128)S(1)}, f32[640,128]{1,0:T(8,128)S(1)}, f32[384,128]{1,0:T(8,128)S(1)}, f32[...) custom-call(f32[12,64,128]{2,1,0:T(8,128)} %bitcast.1, ...), custom_call_target="tpu_custom_call" | custom-call | tf_op jit(solution)/shard_map/partial_levels/pallas_call | solution.py:408
  3.5 1.9 %collective-permute-start = (f32[12,8,128]{2,1,0:T(8,128)S(1)}, f32[12,8,128]{2,1,0:T(8,128)S(1)}, u32[]{:S(2)}, u32[]{:S(2)}) collective-permute-start(f32[12,8,128]{2,1,0:T(8,128)S(1)} %get-tuple-element.36), channel_id=1, source_target_pairs={{0,4},{4,0},{8,12},{12,8},{16,20},{20,16},{24,28},{28,24},{1,5},{5... | collective-permute-start | bytes 147464 | tf_op jit(solution)/shard_map/ppermute | solution.py:442
  5.4 0.7 %collective-permute-start.1 = (f32[12,8,128]{2,1,0:T(8,128)S(1)}, f32[12,8,128]{2,1,0:T(8,128)S(1)}, u32[]{:S(2)}, u32[]{:S(2)}) collective-permute-start(f32[12,8,128]{2,1,0:T(8,128)S(1)} %get-tuple-element.37), channel_id=1, source_target_pairs={{4,8},{8,4},{12,16},{16,12},{20,24},{24,20},{5,9},{9,5},{13,17},{1... | collective-permute-start | bytes 147464 | tf_op jit(solution)/shard_map/ppermute | solution.py:443
  6.1 10.5 %all-to-all-start = ((f32[32,8,128]{2,1,0:T(8,128)}), f32[32,8,128]{2,1,0:T(8,128)S(1)}, u32[]{:S(2)}, u32[]{:S(2)}) async-start(f32[32,8,128]{2,1,0:T(8,128)} %get-tuple-element.29), calls=%async_computation | async-start | bytes 262144 | tf_op jit(solution)/shard_map/all_to_all | solution.py:452
  16.6 0.1 expand_tables.1
  16.7 0.0 collective-permute-done.got_a
  16.7 0.0 collective-permute-done.1.got_b
  16.8 3.1 %collective-permute-start.2 = (f32[6,8,128]{2,1,0:T(8,128)S(1)}, f32[6,8,128]{2,1,0:T(8,128)S(1)}, u32[]{:S(2)}, u32[]{:S(2)}) collective-permute-start(f32[6,8,128]{2,1,0:T(8,128)S(1)} %add.18), channel_id=1, source_target_pairs={{0,1},{1,0},{2,3},{3,2},{4,5},{5,4},{6,7},{7,6},{8,9},{9,8},{10,11... | collective-permute-start | bytes 73736 | tf_op jit(solution)/shard_map/ppermute | solution.py:463
  19.9 1.9 %collective-permute-start.3 = (f32[6,8,128]{2,1,0:T(8,128)S(1)}, f32[6,8,128]{2,1,0:T(8,128)S(1)}, u32[]{:S(2)}, u32[]{:S(2)}) collective-permute-start(f32[6,8,128]{2,1,0:T(8,128)S(1)} %add.20), channel_id=1, source_target_pairs={{1,2},{2,1},{5,6},{6,5},{9,10},{10,9},{13,14},{14,13},{17,18},{18,... | collective-permute-start | bytes 73736 | tf_op jit(solution)/shard_map/ppermute | solution.py:464
  21.8 0.8 %collective-permute-done.2.side_a = f32[6,8,128]{2,1,0:T(8,128)S(1)} collective-permute-done((f32[6,8,128]{2,1,0:T(8,128)S(1)}, f32[6,8,128]{2,1,0:T(8,128)S(1)}, u32[]{:S(2)}, u32[]{:S(2)}) %collective-permute-start.2) | collective-permute-done | bytes 24608 | tf_op jit(solution)/shard_map/ppermute | solution.py:463
  22.6 3.0 %collective-permute-done.3.side_b = f32[6,8,128]{2,1,0:T(8,128)S(1)} collective-permute-done((f32[6,8,128]{2,1,0:T(8,128)S(1)}, f32[6,8,128]{2,1,0:T(8,128)S(1)}, u32[]{:S(2)}, u32[]{:S(2)}) %collective-permute-start.3) | collective-permute-done | bytes 24608 | tf_op jit(solution)/shard_map/ppermute | solution.py:464
  25.6 0.8 %fine_laplacians.1 = (f32[3,64,128]{2,1,0:T(8,128)S(1)}, f32[3,40,128]{2,1,0:T(8,128)S(1)}, f32[3,24,128]{2,1,0:T(8,128)S(1)}, f32[3,16,128]{2,1,0:T(8,128)S(1)}, f32[128,128]{1,0:T(8,128)S(1)}) custom-call(f32[16,88,128]{2,1,0:T(8,128)S(1)} %get-tuple-element.30.s0, f32[12,8,128]{2,1,0:T(8,128)S(1)} %get-tuple-element.31.scale, ...), custom_call_target="tpu_custom_call" | custom-call | tf_op jit(solution)/shard_map/fine_laplacians/pallas_call | solution.py:465
  26.4 0.0 all-to-all-done.refs_0_
  26.4 1.7 %collapse.1 = f32[3,64,128]{2,1,0:T(8,128)} custom-call(f32[32,8,128]{2,1,0:T(8,128)S(1)} %all-to-all-done.refs_0_, f32[3,64,128]{2,1,0:T(8,128)S(1)} %get-tuple-element.47.refs_1_, f32[3,40,128]{2,1,0:T(8,128)S(1)} %get-tuple-element.48.refs_2_, f32[3,24,128]{2,1,0:T(8,128)S(1)} %get-tuple-element.49.refs_3_, f32[3,16,128]{2,1,0:T(8,128)S(1)} %get-tuple-element.50.refs_4_, ...), custom_call_target="tpu_custom_call" | custom-call | tf_op jit(solution)/shard_map/collapse/pallas_call | solution.py:482
  (9 shorter events, 0.0 us)
Async XLA Ops:
  3.5 13.2 %collective-permute-start = (f32[12,8,128]{2,1,0:T(8,128)S(1)}, f32[12,8,128]{2,1,0:T(8,128)S(1)}, u32[]{:S(2)}, u32[]{:S(2)}) collective-permute-start(f32[12,8,128]{2,1,0:T(8,128)S(1)} %get-tuple-element.36), channel_id=1, source_target_pairs={{0,4},{4,0},{8,12},{12,8},{16,20},{20,16},{24,28},{28,24},{1,5},{5... | collective-permute-start | bytes 147464 | tf_op jit(solution)/shard_map/ppermute | solution.py:442
  5.4 11.3 %collective-permute-start.1 = (f32[12,8,128]{2,1,0:T(8,128)S(1)}, f32[12,8,128]{2,1,0:T(8,128)S(1)}, u32[]{:S(2)}, u32[]{:S(2)}) collective-permute-start(f32[12,8,128]{2,1,0:T(8,128)S(1)} %get-tuple-element.37), channel_id=1, source_target_pairs={{4,8},{8,4},{12,16},{16,12},{20,24},{24,20},{5,9},{9,5},{13,17},{1... | collective-permute-start | bytes 147464 | tf_op jit(solution)/shard_map/ppermute | solution.py:443
  6.1 20.4 %all-to-all-start = ((f32[32,8,128]{2,1,0:T(8,128)}), f32[32,8,128]{2,1,0:T(8,128)S(1)}, u32[]{:S(2)}, u32[]{:S(2)}) async-start(f32[32,8,128]{2,1,0:T(8,128)} %get-tuple-element.29), calls=%async_computation | async-start | bytes 262144 | tf_op jit(solution)/shard_map/all_to_all | solution.py:452
  16.8 5.8 %collective-permute-start.2 = (f32[6,8,128]{2,1,0:T(8,128)S(1)}, f32[6,8,128]{2,1,0:T(8,128)S(1)}, u32[]{:S(2)}, u32[]{:S(2)}) collective-permute-start(f32[6,8,128]{2,1,0:T(8,128)S(1)} %add.18), channel_id=1, source_target_pairs={{0,1},{1,0},{2,3},{3,2},{4,5},{5,4},{6,7},{7,6},{8,9},{9,8},{10,11... | collective-permute-start | bytes 73736 | tf_op jit(solution)/shard_map/ppermute | solution.py:463
  19.9 5.7 %collective-permute-start.3 = (f32[6,8,128]{2,1,0:T(8,128)S(1)}, f32[6,8,128]{2,1,0:T(8,128)S(1)}, u32[]{:S(2)}, u32[]{:S(2)}) collective-permute-start(f32[6,8,128]{2,1,0:T(8,128)S(1)} %add.20), channel_id=1, source_target_pairs={{1,2},{2,1},{5,6},{6,5},{9,10},{10,9},{13,14},{14,13},{17,18},{18,... | collective-permute-start | bytes 73736 | tf_op jit(solution)/shard_map/ppermute | solution.py:464

commit v4 on v3

--- a/solution.py
+++ b/solution.py
@@ -3,7 +3,7 @@
 from jax import lax
 from jax.experimental import pallas as pl
 from jax.experimental.pallas import tpu as pltpu
-from jax.sharding import PartitionSpec as P
+from jax.sharding import Mesh, PartitionSpec as P
 
 EXPOSURES = 4
 BANDS = 3
@@ -29,6 +29,7 @@
 PITCH_6 = 6
 AT_6 = 40
 RIMS = 2 * SLOTS + 6
+CORES = 2
 
 f32 = jnp.float32
 bf16 = jnp.bfloat16
@@ -108,12 +109,16 @@
     return (is_5, row_5, col_5), (is_6, row_6, col_6)
 
 
+def place_of(cores):
+    return lax.axis_index("chip") * cores + lax.axis_index("core"), lax.axis_index("tx")
+
+
 def partial_kernel(
     rows, cols, images, gains, labels,
-    s0, scale, x1, x2, x3, x4, send_a, send_b, strip_a, strip_b, patches,
-    s1, s2, s3, s4, s5, y5, y6, across, label, gain, first_part, other_part, low, high, done,
+    s0, scale, x1, x2, x3, x4, send_a, send_b, strip_a, strip_b,
+    s1, s2, s3, s4, s5, y5, y6, label, gain, first_part, other_part, low, high, done,
 ):
-    row, col = lax.axis_index("ty"), lax.axis_index("tx")
+    row, col = place_of(CORES)
     s0[:, 0:8, :] = jnp.zeros((PLANES, 8, LANES), f32)
     s0[:, 72:88, :] = jnp.zeros((PLANES, 16, LANES), f32)
     copies = [pltpu.make_async_copy(labels, label, done.at[INNER])]
@@ -128,19 +133,14 @@
         store[:, depth - 8 : depth, :] = jnp.zeros((PLANES, 8, LANES), f32)
     edge_weights, weights = reduce_weights(4), reduce_weights(3)
 
-    def reduce_rows(source, level, first, planes, scales):
-        count = ROWS[level]
+    def reduce(source, level, first, planes, scales, weights):
+        count, held, sums = ROWS[level], len(planes), []
         for p in planes:
             tap = [source[p, pl.ds(first + k, count, stride=2), :] for k in range(5)]
             total = tap[2] * 0.375 + (tap[1] + tap[3]) * 0.25 + (tap[0] + tap[4]) * 0.0625
-            across[plane_of(level, p), :] = total if scales is None else total * scales[p]
-
-    def reduce_columns(level, planes, weights):
-        count, held = ROWS[level], planes[-1] + 1 - planes[0]
-        inside = in_slab(level, row, col, rows, cols)
-        values = across[pl.ds(planes[0] * count, held * count), :]
-        result = split_dot(values, weights).reshape(held, count, LANES)
-        return jnp.where(inside[None], result, 0.0)
+            sums.append(total if scales is None else total * scales[p])
+        result = split_dot(jnp.concatenate(sums, 0), weights).reshape(held, count, LANES)
+        return jnp.where(in_slab(level, row, col, rows, cols)[None], result, 0.0)
 
     def finish(level, planes, result, store, out):
         count, held = ROWS[level], len(planes)
@@ -153,8 +153,7 @@
     for e in range(EXPOSURES):
         s0[INNER + e, 8:72, :] = jnp.where(label[...] == e, 1.0, 0.0)
     planes = range(INNER, PLANES)
-    reduce_rows(s0, 1, 4, planes, None)
-    finish(1, planes, reduce_columns(1, planes, edge_weights), s1, x1)
+    finish(1, planes, reduce(s0, 1, 4, planes, None, edge_weights), s1, x1)
     copies[1].wait()
     for p in range(INNER):
         scale[p] = jnp.full((8, LANES), gain[p // BANDS, p % BANDS], f32)
@@ -163,13 +162,13 @@
         scales = {e * BANDS + b: gain[e, b] for b in range(BANDS)}
         for p in planes:
             copies[2 + p].wait()
-        reduce_rows(s0, 1, 4, planes, scales)
-        finish(1, planes, reduce_columns(1, planes, edge_weights), s1, x1)
-    planes = range(PLANES)
+        finish(1, planes, reduce(s0, 1, 4, planes, scales, edge_weights), s1, x1)
     stores = ((2, s1, s2, x2), (3, s2, s3, x3), (4, s3, s4, x4), (5, s4, s5, y5), (6, s5, None, y6))
     for level, source, store, out in stores:
-        reduce_rows(source, level, 5, planes, None)
-        finish(level, planes, reduce_columns(level, planes, weights), store, out)
+        held = {2: 4, 3: 8}.get(level, PLANES)
+        for at in range(0, PLANES, held):
+            planes = range(at, at + held)
+            finish(level, planes, reduce(source, level, 5, planes, None, weights), store, out)
 
     patch = jnp.zeros((PLANES, LANES), f32)
     for k in range(SIDE[5] + 3):
@@ -178,21 +177,10 @@
     for k in range(SIDE[6] + 3):
         patch = patch + pltpu.roll(y6[line_of(6, k), :], AT_6 + PITCH_6 * k, 1)
     patch = patch[0:8, :] + pltpu.roll(patch[8:16, :], HALF, 1)
-    (is_5, row_5, col_5), (is_6, row_6, col_6) = patch_places((8, LANES), 1)
-    for r in range(rows):
-        down = r - row
-        rows_5 = is_5 & (row_5 + 2 * down >= 0) & (row_5 + 2 * down < SIDE[5] + 3)
-        rows_6 = is_6 & (row_6 + down >= 0) & (row_6 + down < SIDE[6] + 3)
-        for c in range(cols):
-            over = c - col
-            held = rows_5 & (col_5 + 4 * over >= 0) & (col_5 + 4 * over < WIDE[5] + 3)
-            away = jnp.bitwise_and(-(2 * PITCH_5 * down + 4 * over), LANES - 1)
-            block = jnp.where(held, pltpu.roll(patch, away, 1), 0.0)
-            held = rows_6 & (col_6 + 2 * over >= 0) & (col_6 + 2 * over < WIDE[6] + 3)
-            away = jnp.bitwise_and(-(PITCH_6 * down + 2 * over), LANES - 1)
-            patches[r * cols + c] = jnp.where(held, pltpu.roll(patch, away, 1), block)
+    send_a[RIMS] = patch
 
     levels = (None, x1, x2, x3, x4)
+    odd = jnp.bitwise_and(col, 1) == 1
     for level in range(1, 5):
         count, wide = ROWS[level], WIDE[level]
         lane = iota((count, LANES), 1)
@@ -200,13 +188,16 @@
         after = jnp.zeros((count, LANES), f32)
         for p in range(PLANES):
             plane = levels[level][plane_of(level, p), :]
-            at = 3 * p if level == 1 else HALF + 3 * p
-            here = (lane >= at) & (lane < at + 3)
-            before = jnp.where(here, pltpu.roll(plane, at, 1) if at else plane, before)
-            after = jnp.where(here, pltpu.roll(plane, (at - wide) % LANES, 1), after)
+            plane = pltpu.roll(plane, 3 * p, 1) if p else plane
+            before = jnp.where((lane >= 3 * p) & (lane < 3 * p + 3), plane, before)
+            after = jnp.where((lane >= wide + 3 * p) & (lane < wide + 3 * p + 3), plane, after)
+        if level == 1:
+            after = pltpu.roll(after, HALF, 1)
+        else:
+            before = pltpu.roll(before, HALF, 1)
+            after = pltpu.roll(after, HALF - wide, 1)
         before = jnp.where(col == 0, 0.0, before)
         after = jnp.where(col == cols - 1, 0.0, after)
-        odd = jnp.bitwise_and(col, 1) == 1
         for k, strip in enumerate((jnp.where(odd, before, after), jnp.where(odd, after, before))):
             if level == 1:
                 first_part[k] = strip
@@ -239,8 +230,33 @@
     odd = jnp.bitwise_and(row, 1) == 1
     downward = jnp.where(row == 0, 0.0, low[...])
     upward = jnp.where(row == rows - 1, 0.0, high[...])
-    send_a[...] = jnp.where(odd, downward, upward)
+    send_a[0:RIMS] = jnp.where(odd, downward, upward)
     send_b[...] = jnp.where(odd, upward, downward)
+
+
+def coarse_kernel(rows, cols, own, other, patches):
+    row, col = place_of(CORES)
+    sources = ((own[RIMS], row), (other[RIMS], jnp.bitwise_xor(row, 1)))
+    core = jnp.bitwise_and(row, 1)
+    (is_5, row_5, col_5), (is_6, row_6, col_6) = patch_places((8, LANES), 1)
+    for chip in range(rows // CORES):
+        downs, held_5, held_6 = [], [], []
+        for _, at in sources:
+            down = CORES * chip + core - at
+            downs.append(down)
+            held_5.append(is_5 & (row_5 + 2 * down >= 0) & (row_5 + 2 * down < SIDE[5] + 3))
+            held_6.append(is_6 & (row_6 + down >= 0) & (row_6 + down < SIDE[6] + 3))
+        for c in range(cols):
+            over = c - col
+            cols_5 = (col_5 + 4 * over >= 0) & (col_5 + 4 * over < WIDE[5] + 3)
+            cols_6 = (col_6 + 2 * over >= 0) & (col_6 + 2 * over < WIDE[6] + 3)
+            block = jnp.zeros((8, LANES), f32)
+            for (patch, _), down, rows_5, rows_6 in zip(sources, downs, held_5, held_6):
+                away = jnp.bitwise_and(-(2 * PITCH_5 * down + 4 * over), LANES - 1)
+                block = block + jnp.where(rows_5 & cols_5, pltpu.roll(patch, away, 1), 0.0)
+                away = jnp.bitwise_and(-(PITCH_6 * down + 2 * over), LANES - 1)
+                block = block + jnp.where(rows_6 & cols_6, pltpu.roll(patch, away, 1), 0.0)
+            patches[chip * cols + c] = block
 
 
 def tables_kernel(after, inner, tile, top):
@@ -259,7 +275,7 @@
     b0, b1, b2, b3, t4,
     t1, t2, t3, left, right, across, spread,
 ):
-    row_odd = jnp.bitwise_and(lax.axis_index("ty"), 1) == 1
+    row_odd = lax.axis_index("core") == 1
     col_odd = jnp.bitwise_and(lax.axis_index("tx"), 1) == 1
     left[...] = jnp.where(col_odd, side_a[0:6], side_b[0:6]).reshape(STRIP, LANES)
     right[...] = jnp.where(col_odd, side_b[0:6], side_a[0:6]).reshape(STRIP, LANES)
@@ -271,13 +287,19 @@
         lane = iota((count, LANES), 1)
         from_left = left[at : at + count, :]
         from_right = right[at : at + count, :]
-        start = 0 if level == 1 else HALF
+        if level == 1:
+            both = jnp.where(lane < HALF, from_left, pltpu.roll(from_right, HALF, 1))
+            ends = jnp.bitwise_and(lane, HALF - 1) < 3
         for p in range(PLANES):
-            first = pltpu.roll(from_left, (-start - 3 * p) % LANES, 1) if start + p else from_left
-            last = pltpu.roll(from_right, (wide - start - 3 * p) % LANES, 1)
-            last = jnp.where((lane >= wide) & (lane < wide + 3), last, 0.0)
             place = plane_of(level, p)
-            totals[level][place, :] = parts[level][place, :] + jnp.where(lane < 3, first, last)
+            if level == 1:
+                rim = jnp.where(ends, pltpu.roll(both, LANES - 3 * p, 1) if p else both, 0.0)
+            else:
+                first = pltpu.roll(from_left, HALF - 3 * p, 1)
+                last = pltpu.roll(from_right, HALF + wide - 3 * p, 1)
+                last = jnp.where((lane >= wide) & (lane < wide + 3), last, 0.0)
+                rim = jnp.where(lane < 3, first, last)
+            totals[level][place, :] = parts[level][place, :] + rim
     rims_a, rims_b = got_a[0 : 2 * SLOTS], got_b[0 : 2 * SLOTS]
     below = jnp.where(row_odd, rims_a, rims_b).reshape(SLOTS, PLANES, LANES)
     above = jnp.where(row_odd, rims_b, rims_a).reshape(SLOTS, PLANES, LANES)
@@ -317,9 +339,9 @@
     rows, cols, patches, b0, b1, b2, b3, t4, inner, tile, top_weights, out,
     v5, window, c4, c3, c2, c1, across, spread,
 ):
-    row, col = lax.axis_index("ty"), lax.axis_index("tx")
+    row, col = place_of(CORES)
     total = patches[0]
-    for k in range(1, rows * cols):
+    for k in range(1, rows // CORES * cols):
         total = total + patches[k]
     lane = iota((PLANES, LANES), 1)
     total = jnp.concatenate([total, pltpu.roll(total, HALF, 1)], 0)
@@ -401,24 +423,24 @@
 
 
 def shards(images, gains, labels):
-    rows, cols = lax.axis_size("ty"), lax.axis_size("tx")
+    chips, cols = lax.axis_size("chip"), lax.axis_size("tx")
+    rows = CORES * chips
     images = images.reshape(INNER, ROWS[0], LANES)
     pinned = [pltpu.with_memory_space_constraint(x, pltpu.HBM) for x in (images, gains, labels)]
     levels = [floats(PLANES * ROWS[level], LANES) for level in range(1, 5)]
-    s0, scale, x1, x2, x3, x4, send_a, send_b, strip_a, strip_b, patches = pl.pallas_call(
+    s0, scale, x1, x2, x3, x4, send_a, send_b, strip_a, strip_b = pl.pallas_call(
         lambda *refs: partial_kernel(rows, cols, *refs),
         out_shape=[
             floats(PLANES, 88, LANES),
             floats(INNER, 8, LANES),
             *levels,
-            floats(RIMS, 8, LANES),
+            floats(RIMS + 1, 8, LANES),
             floats(RIMS, 8, LANES),
             floats(6, 8, LANES),
             floats(6, 8, LANES),
-            floats(rows * cols, 8, LANES),
         ],
         in_specs=[HBM] * 3,
-        out_specs=[VMEM] * 11,
+        out_specs=[VMEM] * 10,
         scratch_shapes=[
             scratch(PLANES, 56, LANES),
             scratch(PLANES, 40, LANES),
@@ -427,7 +449,6 @@
             scratch(PLANES, 24, LANES),
             scratch(PLANES * 8, LANES),
             scratch(PLANES * 8, LANES),
-            scratch(PLANES * ROWS[1], LANES),
             pltpu.VMEM((ROWS[0], LANES), jnp.int32),
             pltpu.SMEM((EXPOSURES, BANDS), f32),
             scratch(2, ROWS[1], LANES),
@@ -439,8 +460,8 @@
         compiler_params=PARAMS,
         name="partial_levels",
     )(*pinned)
-    got_a = lax.ppermute(send_a, "ty", swaps(rows, 0))
-    got_b = lax.ppermute(send_b, "ty", swaps(rows, 1))
+    got_a = lax.ppermute(send_a, "core", swaps(CORES, 0))
+    got_b = lax.ppermute(send_b, ("chip", "core"), swaps(rows, 1))
     inner, tile, top = pl.pallas_call(
         tables_kernel,
         out_shape=[halves(2 * LANES, LANES)] * 3,
@@ -449,9 +470,16 @@
         compiler_params=PARAMS,
         name="expand_tables",
     )(strip_a)
-    patches = lax.all_to_all(patches, ("ty", "tx"), 0, 0, tiled=True)
-    odd = lax.axis_index("ty") % 2 == 1
-    rims_a, rims_b = got_a[2 * SLOTS :], got_b[2 * SLOTS :]
+    patches = pl.pallas_call(
+        lambda *refs: coarse_kernel(rows, cols, *refs),
+        out_shape=floats(chips * cols, 8, LANES),
+        in_specs=[VMEM] * 2,
+        out_specs=VMEM,
+        compiler_params=PARAMS,
+        name="coarse_patches",
+    )(send_a, got_a)
+    odd = lax.axis_index("core") == 1
+    rims_a, rims_b = got_a[2 * SLOTS : RIMS], got_b[2 * SLOTS :]
     below, above = jnp.where(odd, rims_a, rims_b), jnp.where(odd, rims_b, rims_a)
     strips = []
     for k, strip in enumerate((strip_a, strip_b)):
@@ -459,7 +487,8 @@
         none = jnp.zeros((1, 8, LANES), f32)
         rims = [low[0:1], none, high[0:1], low[1:2], high[1:2], low[2:3] + high[2:3]]
         strips.append(strip + jnp.concatenate(rims, 0))
-    strips, inner, tile, top = lax.optimization_barrier((strips, inner, tile, top))
+    strips, inner, tile, top, _ = lax.optimization_barrier((strips, inner, tile, top, patches))
+    patches = lax.all_to_all(patches, ("chip", "tx"), 0, 0, tiled=True)
     side_a = lax.ppermute(strips[0], "tx", swaps(cols, 0))
     side_b = lax.ppermute(strips[1], "tx", swaps(cols, 1))
     b0, b1, b2, b3, t4 = pl.pallas_call(
@@ -500,7 +529,14 @@
 
 
 def solution(mesh):
-    placed = (P(None, None, ("grp", "ty"), "tx"), P(), P(("grp", "ty"), "tx"))
+    groups, rows, cols = mesh.devices.shape
+    devices = mesh.devices.reshape(groups, rows // CORES, CORES, cols)
+    split = Mesh(devices, ("grp", "chip", "core", "tx"))
+    down = ("grp", "chip", "core")
     return jax.shard_map(
-        shards, mesh=mesh, in_specs=placed, out_specs=P(None, ("grp", "ty"), "tx"), check_vma=False
+        shards,
+        mesh=split,
+        in_specs=(P(None, None, down, "tx"), P(), P(down, "tx")),
+        out_specs=P(None, down, "tx"),
+        check_vma=False,
     )

time: 28.5 us -> 28.2 us (0.989)
  starting transfers between devices: 18.1 us -> 17.5 us
  waiting for transfers between devices: 3.8 us -> 4.23 us
    pallas_call x1, Pallas kernels: 3.45 us -> 2.64 us  [shards(): pl.pallas_call(lambda *refs: partial_kernel(rows, cols, *refs), out_shape...]
    pallas_call x0 -> x1, Pallas kernels: none -> 0.78 us  [shards(): pl.pallas_call(lambda *refs: coarse_kernel(rows, cols, *refs), out_shape=...]
    all_to_all x1, starting transfers between devices: 10.5 us -> 9.98 us  [shards(): patches = lax.all_to_all(patches, ('chip', 'tx'), 0, 0, tiled=True)]
    ppermute x2, waiting for transfers between devices: 0.01 us -> 0.44 us  [the longest x1 0.44 us: shards(): got_a = lax.ppermute(send_a, 'core', swaps(CORES, 0))]
  transfers between devices with their start and end apart: 5 -> 5, of which waited for: 2 -> 3; matrix products, arithmetic and copies ran while one was open for 0% -> 0% of each run, Pallas kernels for 3% -> 6%
where the time goes in v4:
time: 28.2 us; the launch traced here: 27.9 us
  starting transfers between devices  17.5 us (62%)
  Pallas kernels  5.92 us (21%)
  waiting for transfers between devices  4.23 us (15%)
    all_to_all x1, starting transfers between devices, shards(): patches = lax.all_to_all(patches, ('chip', 'tx'), 0, 0, tiled=True)  9.98 us
    ppermute x1, starting transfers between devices, shards(): side_a = lax.ppermute(strips[0], 'tx', swaps(cols, 0))  3.05 us
    ppermute x1, waiting for transfers between devices, shards(): side_b = lax.ppermute(strips[1], 'tx', swaps(cols, 1))  3.04 us
    pallas_call x1, Pallas kernels, shards(): pl.pallas_call(lambda *refs: partial_kernel(rows, cols, *refs), out_shape...  2.64 us
    ppermute x1, starting transfers between devices, shards(): got_a = lax.ppermute(send_a, 'core', swaps(CORES, 0))  1.92 us
    ppermute x1, starting transfers between devices, shards(): side_b = lax.ppermute(strips[1], 'tx', swaps(cols, 1))  1.92 us
    pallas_call x1, Pallas kernels, shards(): pl.pallas_call(lambda *refs: collapse_kernel(rows, cols, *refs), out_shap...  1.72 us
    pallas_call x1, Pallas kernels, shards(): pl.pallas_call(lambda *refs: coarse_kernel(rows, cols, *refs), out_shape=...  0.78 us
  transfers between devices with their start and end apart: 5, of which 3 were waited for; matrix products, arithmetic and copies ran while one was open for 0% of the time, Pallas kernels for 6%

profile of v4, /device:TPU:16, one launch (start us, length us, event | category | flops | bytes accessed | tf_op | source)
XLA Modules:
  0.0 27.9 jit_solution(7527529134652014597)
XLA Ops:
  0.0 2.6 %partial_levels.1 = (f32[16,88,128]{2,1,0:T(8,128)S(1)}, f32[12,8,128]{2,1,0:T(8,128)S(1)}, f32[640,128]{1,0:T(8,128)S(1)}, f32[384,128]{1,0:T(8,128)S(1)}, f32[...) custom-call(f32[12,64,128]{2,1,0:T(8,128)} %bitcast.1, ...), custom_call_target="tpu_custom_call" | custom-call | tf_op jit(solution)/shard_map/partial_levels/pallas_call | solution.py:431
  2.6 1.9 %collective-permute-start = (f32[13,8,128]{2,1,0:T(8,128)S(1)}, f32[13,8,128]{2,1,0:T(8,128)S(1)}, u32[]{:S(2)}, u32[]{:S(2)}) collective-permute-start(f32[13,8,128]{2,1,0:T(8,128)S(1)} %get-tuple-element.28.refs_0_), channel_id=1, source_target_pairs={{0,4},{4,0},{1,5},{5,1},{2,6},{6,2},{3,7},{7,3},{8,12},{12,8},{9,1... | collective-permute-start | bytes 159752 | tf_op jit(solution)/shard_map/ppermute | solution.py:463
  4.6 0.7 %collective-permute-start.1 = (f32[12,8,128]{2,1,0:T(8,128)S(1)}, f32[12,8,128]{2,1,0:T(8,128)S(1)}, u32[]{:S(2)}, u32[]{:S(2)}) collective-permute-start(f32[12,8,128]{2,1,0:T(8,128)S(1)} %get-tuple-element.35), channel_id=1, source_target_pairs={{4,8},{8,4},{12,16},{16,12},{20,24},{24,20},{5,9},{9,5},{13,17},{1... | collective-permute-start | bytes 147464 | tf_op jit(solution)/shard_map/ppermute | solution.py:464
  5.2 0.1 expand_tables.1
  5.3 0.4 %collective-permute-done.refs_1_.got_a = f32[13,8,128]{2,1,0:T(8,128)S(1)} collective-permute-done((f32[13,8,128]{2,1,0:T(8,128)S(1)}, f32[13,8,128]{2,1,0:T(8,128)S(1)}, u32[]{:S(2)}, u32[]{:S(2)}) %collective-permute-start) | collective-permute-done | bytes 53280 | tf_op jit(solution)/shard_map/ppermute | solution.py:463
  5.8 0.8 %coarse_patches.1 = f32[16,8,128]{2,1,0:T(8,128)} custom-call(f32[13,8,128]{2,1,0:T(8,128)S(1)} %get-tuple-element.28.refs_0_, f32[13,8,128]{2,1,0:T(8,128)S(1)} %collective-permute-done.refs_1_.got_a), custom_call_target="tpu_custom_call" | custom-call | tf_op jit(solution)/shard_map/coarse_patches/pallas_call | solution.py:473
  6.6 10.0 %all-to-all-start = ((f32[16,8,128]{2,1,0:T(8,128)}), f32[16,8,128]{2,1,0:T(8,128)S(1)}, u32[]{:S(2)}, u32[]{:S(2)}) async-start(f32[16,8,128]{2,1,0:T(8,128)} %coarse_patches.1), calls=%async_computation | async-start | bytes 131072 | tf_op jit(solution)/shard_map/all_to_all | solution.py:491
  16.5 0.0 collective-permute-done.1.got_b
  16.7 3.0 %collective-permute-start.2 = (f32[6,8,128]{2,1,0:T(8,128)S(1)}, f32[6,8,128]{2,1,0:T(8,128)S(1)}, u32[]{:S(2)}, u32[]{:S(2)}) collective-permute-start(f32[6,8,128]{2,1,0:T(8,128)S(1)} %add.13), channel_id=1, source_target_pairs={{0,1},{1,0},{2,3},{3,2},{4,5},{5,4},{6,7},{7,6},{8,9},{9,8},{10,11... | collective-permute-start | bytes 73736 | tf_op jit(solution)/shard_map/ppermute | solution.py:492
  19.7 1.9 %collective-permute-start.3 = (f32[6,8,128]{2,1,0:T(8,128)S(1)}, f32[6,8,128]{2,1,0:T(8,128)S(1)}, u32[]{:S(2)}, u32[]{:S(2)}) collective-permute-start(f32[6,8,128]{2,1,0:T(8,128)S(1)} %add.15), channel_id=1, source_target_pairs={{1,2},{2,1},{5,6},{6,5},{9,10},{10,9},{13,14},{14,13},{17,18},{18,... | collective-permute-start | bytes 73736 | tf_op jit(solution)/shard_map/ppermute | solution.py:493
  21.6 0.8 %collective-permute-done.2.side_a = f32[6,8,128]{2,1,0:T(8,128)S(1)} collective-permute-done((f32[6,8,128]{2,1,0:T(8,128)S(1)}, f32[6,8,128]{2,1,0:T(8,128)S(1)}, u32[]{:S(2)}, u32[]{:S(2)}) %collective-permute-start.2) | collective-permute-done | bytes 24608 | tf_op jit(solution)/shard_map/ppermute | solution.py:492
  22.4 3.0 %collective-permute-done.3.side_b = f32[6,8,128]{2,1,0:T(8,128)S(1)} collective-permute-done((f32[6,8,128]{2,1,0:T(8,128)S(1)}, f32[6,8,128]{2,1,0:T(8,128)S(1)}, u32[]{:S(2)}, u32[]{:S(2)}) %collective-permute-start.3) | collective-permute-done | bytes 24608 | tf_op jit(solution)/shard_map/ppermute | solution.py:493
  25.4 0.7 %fine_laplacians.1 = (f32[3,64,128]{2,1,0:T(8,128)S(1)}, f32[3,40,128]{2,1,0:T(8,128)S(1)}, f32[3,24,128]{2,1,0:T(8,128)S(1)}, f32[3,16,128]{2,1,0:T(8,128)S(1)}, f32[128,128]{1,0:T(8,128)S(1)}) custom-call(f32[16,88,128]{2,1,0:T(8,128)S(1)} %get-tuple-element.29.s0, f32[12,8,128]{2,1,0:T(8,128)S(1)} %get-tuple-element.30.scale, ...), custom_call_target="tpu_custom_call" | custom-call | tf_op jit(solution)/shard_map/fine_laplacians/pallas_call | solution.py:494
  26.2 0.0 all-to-all-done.refs_0_
  26.2 1.7 %collapse.1 = f32[3,64,128]{2,1,0:T(8,128)} custom-call(f32[16,8,128]{2,1,0:T(8,128)S(1)} %all-to-all-done.refs_0_, f32[3,64,128]{2,1,0:T(8,128)S(1)} %get-tuple-element.45.refs_1_, f32[3,40,128]{2,1,0:T(8,128)S(1)} %get-tuple-element.46.refs_2_, f32[3,24,128]{2,1,0:T(8,128)S(1)} %get-tuple-element.47.refs_3_, f32[3,16,128]{2,1,0:T(8,128)S(1)} %get-tuple-element.48.refs_4_, ...), custom_call_target="tpu_custom_call" | custom-call | tf_op jit(solution)/shard_map/collapse/pallas_call | solution.py:511
  (9 shorter events, 0.0 us)
Async XLA Ops:
  2.6 3.1 %collective-permute-start = (f32[13,8,128]{2,1,0:T(8,128)S(1)}, f32[13,8,128]{2,1,0:T(8,128)S(1)}, u32[]{:S(2)}, u32[]{:S(2)}) collective-permute-start(f32[13,8,128]{2,1,0:T(8,128)S(1)} %get-tuple-element.28.refs_0_), channel_id=1, source_target_pairs={{0,4},{4,0},{1,5},{5,1},{2,6},{6,2},{3,7},{7,3},{8,12},{12,8},{9,1... | collective-permute-start | bytes 159752 | tf_op jit(solution)/shard_map/ppermute | solution.py:463
  4.6 12.0 %collective-permute-start.1 = (f32[12,8,128]{2,1,0:T(8,128)S(1)}, f32[12,8,128]{2,1,0:T(8,128)S(1)}, u32[]{:S(2)}, u32[]{:S(2)}) collective-permute-start(f32[12,8,128]{2,1,0:T(8,128)S(1)} %get-tuple-element.35), channel_id=1, source_target_pairs={{4,8},{8,4},{12,16},{16,12},{20,24},{24,20},{5,9},{9,5},{13,17},{1... | collective-permute-start | bytes 147464 | tf_op jit(solution)/shard_map/ppermute | solution.py:464
  6.6 19.6 %all-to-all-start = ((f32[16,8,128]{2,1,0:T(8,128)}), f32[16,8,128]{2,1,0:T(8,128)S(1)}, u32[]{:S(2)}, u32[]{:S(2)}) async-start(f32[16,8,128]{2,1,0:T(8,128)} %coarse_patches.1), calls=%async_computation | async-start | bytes 131072 | tf_op jit(solution)/shard_map/all_to_all | solution.py:491
  16.7 5.7 %collective-permute-start.2 = (f32[6,8,128]{2,1,0:T(8,128)S(1)}, f32[6,8,128]{2,1,0:T(8,128)S(1)}, u32[]{:S(2)}, u32[]{:S(2)}) collective-permute-start(f32[6,8,128]{2,1,0:T(8,128)S(1)} %add.13), channel_id=1, source_target_pairs={{0,1},{1,0},{2,3},{3,2},{4,5},{5,4},{6,7},{7,6},{8,9},{9,8},{10,11... | collective-permute-start | bytes 73736 | tf_op jit(solution)/shard_map/ppermute | solution.py:492
  19.7 5.7 %collective-permute-start.3 = (f32[6,8,128]{2,1,0:T(8,128)S(1)}, f32[6,8,128]{2,1,0:T(8,128)S(1)}, u32[]{:S(2)}, u32[]{:S(2)}) collective-permute-start(f32[6,8,128]{2,1,0:T(8,128)S(1)} %add.15), channel_id=1, source_target_pairs={{1,2},{2,1},{5,6},{6,5},{9,10},{10,9},{13,14},{14,13},{17,18},{18,... | collective-permute-start | bytes 73736 | tf_op jit(solution)/shard_map/ppermute | solution.py:493

commit v5 on v4

--- a/solution.py
+++ b/solution.py
@@ -30,6 +30,8 @@
 AT_6 = 40
 RIMS = 2 * SLOTS + 6
 CORES = 2
+REACH_ROWS = 3
+REACH_COLS = 2
 
 f32 = jnp.float32
 bf16 = jnp.bfloat16
@@ -115,18 +117,21 @@
 
 def partial_kernel(
     rows, cols, images, gains, labels,
-    s0, scale, x1, x2, x3, x4, send_a, send_b, strip_a, strip_b,
+    s0, scale, x1, x2, x3, x4, send_a, send_b, strip_a, strip_b, patch_out,
     s1, s2, s3, s4, s5, y5, y6, label, gain, first_part, other_part, low, high, done,
 ):
     row, col = place_of(CORES)
+    copies = [
+        pltpu.make_async_copy(labels, label, done.at[EXPOSURES]),
+        pltpu.make_async_copy(gains, gain, done.at[EXPOSURES + 1]),
+    ]
+    for e in range(EXPOSURES):
+        planes = pl.ds(e * BANDS, BANDS)
+        copies.append(pltpu.make_async_copy(images.at[planes], s0.at[planes, pl.ds(8, 64)], done.at[e]))
+    for copy in copies:
+        copy.start()
     s0[:, 0:8, :] = jnp.zeros((PLANES, 8, LANES), f32)
     s0[:, 72:88, :] = jnp.zeros((PLANES, 16, LANES), f32)
-    copies = [pltpu.make_async_copy(labels, label, done.at[INNER])]
-    copies.append(pltpu.make_async_copy(gains, gain, done.at[INNER + 1]))
-    for p in range(INNER):
-        copies.append(pltpu.make_async_copy(images.at[p], s0.at[p, pl.ds(8, 64)], done.at[p]))
-    for copy in copies:
-        copy.start()
     for store in (s1, s2, s3, s4, s5):
         depth = store.shape[1]
         store[:, 0:8, :] = jnp.zeros((PLANES, 8, LANES), f32)
@@ -160,8 +165,7 @@
     for e in range(EXPOSURES):
         planes = range(e * BANDS, (e + 1) * BANDS)
         scales = {e * BANDS + b: gain[e, b] for b in range(BANDS)}
-        for p in planes:
-            copies[2 + p].wait()
+        copies[2 + e].wait()
         finish(1, planes, reduce(s0, 1, 4, planes, scales, edge_weights), s1, x1)
     stores = ((2, s1, s2, x2), (3, s2, s3, x3), (4, s3, s4, x4), (5, s4, s5, y5), (6, s5, None, y6))
     for level, source, store, out in stores:
@@ -177,7 +181,7 @@
     for k in range(SIDE[6] + 3):
         patch = patch + pltpu.roll(y6[line_of(6, k), :], AT_6 + PITCH_6 * k, 1)
     patch = patch[0:8, :] + pltpu.roll(patch[8:16, :], HALF, 1)
-    send_a[RIMS] = patch
+    patch_out[...] = patch
 
     levels = (None, x1, x2, x3, x4)
     odd = jnp.bitwise_and(col, 1) == 1
@@ -230,33 +234,32 @@
     odd = jnp.bitwise_and(row, 1) == 1
     downward = jnp.where(row == 0, 0.0, low[...])
     upward = jnp.where(row == rows - 1, 0.0, high[...])
-    send_a[0:RIMS] = jnp.where(odd, downward, upward)
+    send_a[...] = jnp.where(odd, downward, upward)
     send_b[...] = jnp.where(odd, upward, downward)
 
 
-def coarse_kernel(rows, cols, own, other, patches):
+def coarse_kernel(rows, cols, patch, rims, patches, send, slots):
     row, col = place_of(CORES)
-    sources = ((own[RIMS], row), (other[RIMS], jnp.bitwise_xor(row, 1)))
-    core = jnp.bitwise_and(row, 1)
+    send[...] = rims[...]
+    slots[...] = jnp.zeros(slots.shape, f32)
+    width = cols + 2 * REACH_COLS
     (is_5, row_5, col_5), (is_6, row_6, col_6) = patch_places((8, LANES), 1)
-    for chip in range(rows // CORES):
-        downs, held_5, held_6 = [], [], []
-        for _, at in sources:
-            down = CORES * chip + core - at
-            downs.append(down)
-            held_5.append(is_5 & (row_5 + 2 * down >= 0) & (row_5 + 2 * down < SIDE[5] + 3))
-            held_6.append(is_6 & (row_6 + down >= 0) & (row_6 + down < SIDE[6] + 3))
+    values = patch[...]
+    for down in range(-REACH_ROWS, REACH_ROWS + 1):
+        for over in range(-REACH_COLS, REACH_COLS + 1):
+            along, aside = row_6 + down, col_6 + 2 * over
+            held = is_6 & (along >= 0) & (along < SIDE[6] + 3) & (aside >= 0) & (aside < WIDE[6] + 3)
+            away = -(PITCH_6 * down + 2 * over) % LANES
+            block = jnp.where(held, pltpu.roll(values, away, 1) if away else values, 0.0)
+            if abs(down) < REACH_ROWS and abs(over) < REACH_COLS:
+                along, aside = row_5 + 2 * down, col_5 + 4 * over
+                held = is_5 & (along >= 0) & (along < SIDE[5] + 3) & (aside >= 0) & (aside < WIDE[5] + 3)
+                away = -(2 * PITCH_5 * down + 4 * over) % LANES
+                block = jnp.where(held, pltpu.roll(values, away, 1) if away else values, block)
+            slots[(row + (down + REACH_ROWS)) * width + col + (over + REACH_COLS)] = block
+    for r in range(rows):
         for c in range(cols):
-            over = c - col
-            cols_5 = (col_5 + 4 * over >= 0) & (col_5 + 4 * over < WIDE[5] + 3)
-            cols_6 = (col_6 + 2 * over >= 0) & (col_6 + 2 * over < WIDE[6] + 3)
-            block = jnp.zeros((8, LANES), f32)
-            for (patch, _), down, rows_5, rows_6 in zip(sources, downs, held_5, held_6):
-                away = jnp.bitwise_and(-(2 * PITCH_5 * down + 4 * over), LANES - 1)
-                block = block + jnp.where(rows_5 & cols_5, pltpu.roll(patch, away, 1), 0.0)
-                away = jnp.bitwise_and(-(PITCH_6 * down + 2 * over), LANES - 1)
-                block = block + jnp.where(rows_6 & cols_6, pltpu.roll(patch, away, 1), 0.0)
-            patches[chip * cols + c] = block
+            patches[r * cols + c] = slots[(r + REACH_ROWS) * width + c + REACH_COLS]
 
 
 def tables_kernel(after, inner, tile, top):
@@ -270,36 +273,29 @@
     top[...] = jnp.concatenate([weights, weights], 0)
 
 
-def fine_kernel(
-    s0, scale, x1, x2, x3, x4, got_a, got_b, side_a, side_b, inner, tile,
-    b0, b1, b2, b3, t4,
-    t1, t2, t3, left, right, across, spread,
-):
-    row_odd = lax.axis_index("core") == 1
-    col_odd = jnp.bitwise_and(lax.axis_index("tx"), 1) == 1
-    left[...] = jnp.where(col_odd, side_a[0:6], side_b[0:6]).reshape(STRIP, LANES)
-    right[...] = jnp.where(col_odd, side_b[0:6], side_a[0:6]).reshape(STRIP, LANES)
-
-    totals = (None, t1, t2, t3, t4)
-    parts = (None, x1, x2, x3, x4)
+def add_side(totals, parts, strip, on_left, held):
+    held[...] = strip[...].reshape(STRIP, LANES)
     for level in range(1, 5):
         count, wide, at = ROWS[level], WIDE[level], STRIP_AT[level]
         lane = iota((count, LANES), 1)
-        from_left = left[at : at + count, :]
-        from_right = right[at : at + count, :]
-        if level == 1:
-            both = jnp.where(lane < HALF, from_left, pltpu.roll(from_right, HALF, 1))
-            ends = jnp.bitwise_and(lane, HALF - 1) < 3
+        start = 0 if level == 1 else HALF
+        rim = held[at : at + count, :]
+        rim = jnp.where((lane >= start) & (lane < start + 3 * PLANES), rim, 0.0)
+        rim = jnp.where(on_left, rim, pltpu.roll(rim, wide, 1))
+        first = jnp.where(on_left, 0, wide)
+        inside = (lane >= first) & (lane < first + 3)
         for p in range(PLANES):
+            away = -(start + 3 * p) % LANES
             place = plane_of(level, p)
-            if level == 1:
-                rim = jnp.where(ends, pltpu.roll(both, LANES - 3 * p, 1) if p else both, 0.0)
-            else:
-                first = pltpu.roll(from_left, HALF - 3 * p, 1)
-                last = pltpu.roll(from_right, HALF + wide - 3 * p, 1)
-                last = jnp.where((lane >= wide) & (lane < wide + 3), last, 0.0)
-                rim = jnp.where(lane < 3, first, last)
-            totals[level][place, :] = parts[level][place, :] + rim
+            part = jnp.where(inside, pltpu.roll(rim, away, 1) if away else rim, 0.0)
+            totals[level][place, :] = parts[level][place, :] + part
+
+
+def rims_kernel(x1, x2, x3, x4, got_a, got_b, side, t1, t2, t3, t4, held):
+    row_odd = lax.axis_index("core") == 1
+    col_odd = jnp.bitwise_and(lax.axis_index("tx"), 1) == 1
+    totals = (None, t1, t2, t3, t4)
+    add_side(totals, (None, x1, x2, x3, x4), side, col_odd, held)
     rims_a, rims_b = got_a[0 : 2 * SLOTS], got_b[0 : 2 * SLOTS]
     below = jnp.where(row_odd, rims_a, rims_b).reshape(SLOTS, PLANES, LANES)
     above = jnp.where(row_odd, rims_b, rims_a).reshape(SLOTS, PLANES, LANES)
@@ -308,6 +304,16 @@
             values = rim[slot]
             values = pltpu.roll(values, LANES - lane, 1) if lane else values
             totals[level][line_of(level, at[level] + line), :] += values
+
+
+def fine_kernel(
+    s0, scale, x1, x2, x3, x4, side, inner, tile,
+    b0, b1, b2, b3, t4,
+    t1, t2, t3, held, across, spread,
+):
+    col_odd = jnp.bitwise_and(lax.axis_index("tx"), 1) == 1
+    totals = (None, t1, t2, t3, t4)
+    add_side(totals, (None, x1, x2, x3, x4), side, jnp.logical_not(col_odd), held)
 
     for level in (3, 2, 1):
         source, count, out = totals[level + 1], ROWS[level + 1], (None, b1, b2, b3)[level]
@@ -341,7 +347,7 @@
 ):
     row, col = place_of(CORES)
     total = patches[0]
-    for k in range(1, rows // CORES * cols):
+    for k in range(1, rows * cols):
         total = total + patches[k]
     lane = iota((PLANES, LANES), 1)
     total = jnp.concatenate([total, pltpu.roll(total, HALF, 1)], 0)
@@ -428,19 +434,20 @@
     images = images.reshape(INNER, ROWS[0], LANES)
     pinned = [pltpu.with_memory_space_constraint(x, pltpu.HBM) for x in (images, gains, labels)]
     levels = [floats(PLANES * ROWS[level], LANES) for level in range(1, 5)]
-    s0, scale, x1, x2, x3, x4, send_a, send_b, strip_a, strip_b = pl.pallas_call(
+    s0, scale, x1, x2, x3, x4, send_a, send_b, strip_a, strip_b, patch = pl.pallas_call(
         lambda *refs: partial_kernel(rows, cols, *refs),
         out_shape=[
             floats(PLANES, 88, LANES),
             floats(INNER, 8, LANES),
             *levels,
-            floats(RIMS + 1, 8, LANES),
+            floats(RIMS, 8, LANES),
             floats(RIMS, 8, LANES),
             floats(6, 8, LANES),
             floats(6, 8, LANES),
+            floats(8, LANES),
         ],
         in_specs=[HBM] * 3,
-        out_specs=[VMEM] * 10,
+        out_specs=[VMEM] * 11,
         scratch_shapes=[
             scratch(PLANES, 56, LANES),
             scratch(PLANES, 40, LANES),
@@ -455,13 +462,22 @@
             scratch(2, STRIP, LANES),
             scratch(RIMS, 8, LANES),
             scratch(RIMS, 8, LANES),
-            pltpu.SemaphoreType.DMA((INNER + 2,)),
+            pltpu.SemaphoreType.DMA((EXPOSURES + 2,)),
         ],
         compiler_params=PARAMS,
         name="partial_levels",
     )(*pinned)
+    got_b = lax.ppermute(send_b, ("chip", "core"), swaps(rows, 1))
+    patches, send_a = pl.pallas_call(
+        lambda *refs: coarse_kernel(rows, cols, *refs),
+        out_shape=[floats(rows * cols, 8, LANES), floats(RIMS, 8, LANES)],
+        in_specs=[VMEM] * 2,
+        out_specs=[VMEM] * 2,
+        scratch_shapes=[scratch((rows + 2 * REACH_ROWS) * (cols + 2 * REACH_COLS), 8, LANES)],
+        compiler_params=PARAMS,
+        name="coarse_patches",
+    )(patch, send_a)
     got_a = lax.ppermute(send_a, "core", swaps(CORES, 0))
-    got_b = lax.ppermute(send_b, ("chip", "core"), swaps(rows, 1))
     inner, tile, top = pl.pallas_call(
         tables_kernel,
         out_shape=[halves(2 * LANES, LANES)] * 3,
@@ -470,16 +486,8 @@
         compiler_params=PARAMS,
         name="expand_tables",
     )(strip_a)
-    patches = pl.pallas_call(
-        lambda *refs: coarse_kernel(rows, cols, *refs),
-        out_shape=floats(chips * cols, 8, LANES),
-        in_specs=[VMEM] * 2,
-        out_specs=VMEM,
-        compiler_params=PARAMS,
-        name="coarse_patches",
-    )(send_a, got_a)
     odd = lax.axis_index("core") == 1
-    rims_a, rims_b = got_a[2 * SLOTS : RIMS], got_b[2 * SLOTS :]
+    rims_a, rims_b = got_a[2 * SLOTS :], got_b[2 * SLOTS :]
     below, above = jnp.where(odd, rims_a, rims_b), jnp.where(odd, rims_b, rims_a)
     strips = []
     for k, strip in enumerate((strip_a, strip_b)):
@@ -488,26 +496,34 @@
         rims = [low[0:1], none, high[0:1], low[1:2], high[1:2], low[2:3] + high[2:3]]
         strips.append(strip + jnp.concatenate(rims, 0))
     strips, inner, tile, top, _ = lax.optimization_barrier((strips, inner, tile, top, patches))
-    patches = lax.all_to_all(patches, ("chip", "tx"), 0, 0, tiled=True)
+    patches = lax.all_to_all(patches, ("chip", "core", "tx"), 0, 0, tiled=True)
     side_a = lax.ppermute(strips[0], "tx", swaps(cols, 0))
     side_b = lax.ppermute(strips[1], "tx", swaps(cols, 1))
+    x1, x2, x3, x4 = pl.pallas_call(
+        rims_kernel,
+        out_shape=levels,
+        in_specs=[VMEM] * 7,
+        out_specs=[VMEM] * 4,
+        scratch_shapes=[scratch(STRIP, LANES)],
+        compiler_params=PARAMS,
+        name="add_rims",
+    )(x1, x2, x3, x4, got_a, got_b, side_a)
     b0, b1, b2, b3, t4 = pl.pallas_call(
         fine_kernel,
         out_shape=[floats(BANDS, ROWS[level], LANES) for level in range(4)] + [levels[3]],
-        in_specs=[VMEM] * 12,
+        in_specs=[VMEM] * 9,
         out_specs=[VMEM] * 5,
         scratch_shapes=[
             scratch(PLANES * ROWS[1], LANES),
             scratch(PLANES * ROWS[2], LANES),
             scratch(PLANES * ROWS[3], LANES),
             scratch(STRIP, LANES),
-            scratch(STRIP, LANES),
             scratch(INNER, ROWS[1], LANES),
             scratch(INNER, ROWS[0], LANES),
         ],
         compiler_params=PARAMS,
         name="fine_laplacians",
-    )(s0, scale, x1, x2, x3, x4, got_a, got_b, side_a, side_b, inner, tile)
+    )(s0, scale, x1, x2, x3, x4, side_b, inner, tile)
     return pl.pallas_call(
         lambda *refs: collapse_kernel(rows, cols, *refs),
         out_shape=floats(BANDS, ROWS[0], LANES),

time: 28.2 us -> 27.6 us (0.979)
  the two profiles are of different devices: /device:TPU:16 before, /device:TPU:400 now
where the time goes in v5:
time: 27.6 us; the launch traced here: 27.3 us
  starting transfers between devices  17.5 us (63%)
  Pallas kernels  6.34 us (23%)
  waiting for transfers between devices  3.24 us (12%)
    all_to_all x1, starting transfers between devices, shards(): patches = lax.all_to_all(patches, ('chip', 'core', 'tx'), 0, 0, tiled=True)  7.14 us
    ppermute x1, starting transfers between devices, shards(): got_a = lax.ppermute(send_a, 'core', swaps(CORES, 0))  4.74 us
    ppermute x1, starting transfers between devices, shards(): side_a = lax.ppermute(strips[0], 'tx', swaps(cols, 0))  3.08 us
    pallas_call x1, Pallas kernels, shards(): pl.pallas_call(lambda *refs: partial_kernel(rows, cols, *refs), out_shape...  2.55 us
    ppermute x1, waiting for transfers between devices, shards(): side_b = lax.ppermute(strips[1], 'tx', swaps(cols, 1))  2.44 us
    ppermute x1, starting transfers between devices, shards(): side_b = lax.ppermute(strips[1], 'tx', swaps(cols, 1))  1.92 us
    pallas_call x1, Pallas kernels, shards(): pl.pallas_call(lambda *refs: collapse_kernel(rows, cols, *refs), out_shap...  1.73 us
    ppermute x1, waiting for transfers between devices, shards(): side_a = lax.ppermute(strips[0], 'tx', swaps(cols, 0))  0.79 us
  transfers between devices with their start and end apart: 5, of which 2 were waited for; matrix products, arithmetic and copies ran while one was open for 0% of the time, Pallas kernels for 8%

profile of v5, /device:TPU:400, one launch (start us, length us, event | category | flops | bytes accessed | tf_op | source)
XLA Modules:
  0.0 27.3 jit_solution(13662618991332984458)
XLA Ops:
  0.0 2.6 %partial_levels.1 = (f32[16,88,128]{2,1,0:T(8,128)S(1)}, f32[12,8,128]{2,1,0:T(8,128)S(1)}, f32[640,128]{1,0:T(8,128)S(1)}, f32[384,128]{1,0:T(8,128)S(1)}, f32[...) custom-call(f32[12,64,128]{2,1,0:T(8,128)} %bitcast.1, ...), custom_call_target="tpu_custom_call" | custom-call | tf_op jit(solution)/shard_map/partial_levels/pallas_call | solution.py:437
  2.6 0.7 %collective-permute-start.1 = (f32[12,8,128]{2,1,0:T(8,128)S(1)}, f32[12,8,128]{2,1,0:T(8,128)S(1)}, u32[]{:S(2)}, u32[]{:S(2)}) collective-permute-start(f32[12,8,128]{2,1,0:T(8,128)S(1)} %get-tuple-element.45), channel_id=1, source_target_pairs={{4,8},{8,4},{12,16},{16,12},{20,24},{24,20},{5,9},{9,5},{13,17},{1... | collective-permute-start | bytes 147464 | tf_op jit(solution)/shard_map/ppermute | solution.py:470
  3.2 0.8 %coarse_patches.1 = (f32[32,8,128]{2,1,0:T(8,128)}, f32[12,8,128]{2,1,0:T(8,128)S(1)}) custom-call(f32[8,128]{1,0:T(8,128)S(1)} %get-tuple-element.35.refs_0_, f32[12,8,128]{2,1,0:T(8,128)S(1)} %get-tuple-element.36.refs_1_), custom_call_target="tpu_custom_call" | custom-call | tf_op jit(solution)/shard_map/coarse_patches/pallas_call | solution.py:471
  4.0 4.7 %collective-permute-start = (f32[12,8,128]{2,1,0:T(8,128)S(1)}, f32[12,8,128]{2,1,0:T(8,128)S(1)}, u32[]{:S(2)}, u32[]{:S(2)}) collective-permute-start(f32[12,8,128]{2,1,0:T(8,128)S(1)} %get-tuple-element.44), channel_id=1, source_target_pairs={{0,4},{4,0},{1,5},{5,1},{2,6},{6,2},{3,7},{7,3},{8,12},{12,8},{9,1... | collective-permute-start | bytes 147464 | tf_op jit(solution)/shard_map/ppermute | solution.py:480
  8.7 7.1 %all-to-all-start = ((f32[32,8,128]{2,1,0:T(8,128)}), f32[32,8,128]{2,1,0:T(8,128)S(1)}, u32[]{:S(2)}, u32[]{:S(2)}) async-start(f32[32,8,128]{2,1,0:T(8,128)} %get-tuple-element.37), calls=%async_computation | async-start | bytes 262144 | tf_op jit(solution)/shard_map/all_to_all | solution.py:499
  15.9 0.1 expand_tables.1
  16.0 0.0 collective-permute-done.1.got_b
  16.0 0.0 collective-permute-done.got_a
  16.1 3.1 %collective-permute-start.2 = (f32[6,8,128]{2,1,0:T(8,128)S(1)}, f32[6,8,128]{2,1,0:T(8,128)S(1)}, u32[]{:S(2)}, u32[]{:S(2)}) collective-permute-start(f32[6,8,128]{2,1,0:T(8,128)S(1)} %add.13), channel_id=1, source_target_pairs={{0,1},{1,0},{2,3},{3,2},{4,5},{5,4},{6,7},{7,6},{8,9},{9,8},{10,11... | collective-permute-start | bytes 73736 | tf_op jit(solution)/shard_map/ppermute | solution.py:500
  19.2 1.9 %collective-permute-start.3 = (f32[6,8,128]{2,1,0:T(8,128)S(1)}, f32[6,8,128]{2,1,0:T(8,128)S(1)}, u32[]{:S(2)}, u32[]{:S(2)}) collective-permute-start(f32[6,8,128]{2,1,0:T(8,128)S(1)} %add.15), channel_id=1, source_target_pairs={{1,2},{2,1},{5,6},{6,5},{9,10},{10,9},{13,14},{14,13},{17,18},{18,... | collective-permute-start | bytes 73736 | tf_op jit(solution)/shard_map/ppermute | solution.py:501
  21.1 0.8 %collective-permute-done.2.side = f32[6,8,128]{2,1,0:T(8,128)S(1)} collective-permute-done((f32[6,8,128]{2,1,0:T(8,128)S(1)}, f32[6,8,128]{2,1,0:T(8,128)S(1)}, u32[]{:S(2)}, u32[]{:S(2)}) %collective-permute-start.2) | collective-permute-done | bytes 24608 | tf_op jit(solution)/shard_map/ppermute | solution.py:500
  21.9 0.5 %add_rims.1 = (f32[640,128]{1,0:T(8,128)S(1)}, f32[384,128]{1,0:T(8,128)S(1)}, f32[256,128]{1,0:T(8,128)S(1)}, f32[128,128]{1,0:T(8,128)S(1)}) custom-call(f32[640,128]{1,0:T(8,128)S(1)} %get-tuple-element.40.x1, f32[384,128]{1,0:T(8,128)S(1)} %get-tuple-element.41.x2, f32[256,128]{1,0:T(8,128)S(1)} %get-tuple-element.42.x3, ...), custom_call_target="tpu_custom_call" | custom-call | tf_op jit(solution)/shard_map/add_rims/pallas_call | solution.py:502
  22.5 2.4 %collective-permute-done.3.side = f32[6,8,128]{2,1,0:T(8,128)S(1)} collective-permute-done((f32[6,8,128]{2,1,0:T(8,128)S(1)}, f32[6,8,128]{2,1,0:T(8,128)S(1)}, u32[]{:S(2)}, u32[]{:S(2)}) %collective-permute-start.3) | collective-permute-done | bytes 24608 | tf_op jit(solution)/shard_map/ppermute | solution.py:501
  24.9 0.7 %fine_laplacians.1 = (f32[3,64,128]{2,1,0:T(8,128)S(1)}, f32[3,40,128]{2,1,0:T(8,128)S(1)}, f32[3,24,128]{2,1,0:T(8,128)S(1)}, f32[3,16,128]{2,1,0:T(8,128)S(1)}, f32[128,128]{1,0:T(8,128)S(1)}) custom-call(f32[16,88,128]{2,1,0:T(8,128)S(1)} %get-tuple-element.38.s0, f32[12,8,128]{2,1,0:T(8,128)S(1)} %get-tuple-element.39.scale, ...), custom_call_target="tpu_custom_call" | custom-call | tf_op jit(solution)/shard_map/fine_laplacians/pallas_call | solution.py:511
  25.6 0.0 all-to-all-done.refs_0_
  25.6 1.7 %collapse.1 = f32[3,64,128]{2,1,0:T(8,128)} custom-call(f32[32,8,128]{2,1,0:T(8,128)S(1)} %all-to-all-done.refs_0_, f32[3,64,128]{2,1,0:T(8,128)S(1)} %get-tuple-element.59.refs_1_, f32[3,40,128]{2,1,0:T(8,128)S(1)} %get-tuple-element.60.refs_2_, f32[3,24,128]{2,1,0:T(8,128)S(1)} %get-tuple-element.61.refs_3_, f32[3,16,128]{2,1,0:T(8,128)S(1)} %get-tuple-element.62.refs_4_, ...), custom_call_target="tpu_custom_call" | custom-call | tf_op jit(solution)/shard_map/collapse/pallas_call | solution.py:527
  (9 shorter events, 0.0 us)
Async XLA Ops:
  2.6 13.4 %collective-permute-start.1 = (f32[12,8,128]{2,1,0:T(8,128)S(1)}, f32[12,8,128]{2,1,0:T(8,128)S(1)}, u32[]{:S(2)}, u32[]{:S(2)}) collective-permute-start(f32[12,8,128]{2,1,0:T(8,128)S(1)} %get-tuple-element.45), channel_id=1, source_target_pairs={{4,8},{8,4},{12,16},{16,12},{20,24},{24,20},{5,9},{9,5},{13,17},{1... | collective-permute-start | bytes 147464 | tf_op jit(solution)/shard_map/ppermute | solution.py:470
  4.0 12.0 %collective-permute-start = (f32[12,8,128]{2,1,0:T(8,128)S(1)}, f32[12,8,128]{2,1,0:T(8,128)S(1)}, u32[]{:S(2)}, u32[]{:S(2)}) collective-permute-start(f32[12,8,128]{2,1,0:T(8,128)S(1)} %get-tuple-element.44), channel_id=1, source_target_pairs={{0,4},{4,0},{1,5},{5,1},{2,6},{6,2},{3,7},{7,3},{8,12},{12,8},{9,1... | collective-permute-start | bytes 147464 | tf_op jit(solution)/shard_map/ppermute | solution.py:480
  8.7 16.9 %all-to-all-start = ((f32[32,8,128]{2,1,0:T(8,128)}), f32[32,8,128]{2,1,0:T(8,128)S(1)}, u32[]{:S(2)}, u32[]{:S(2)}) async-start(f32[32,8,128]{2,1,0:T(8,128)} %get-tuple-element.37), calls=%async_computation | async-start | bytes 262144 | tf_op jit(solution)/shard_map/all_to_all | solution.py:499
  16.1 5.8 %collective-permute-start.2 = (f32[6,8,128]{2,1,0:T(8,128)S(1)}, f32[6,8,128]{2,1,0:T(8,128)S(1)}, u32[]{:S(2)}, u32[]{:S(2)}) collective-permute-start(f32[6,8,128]{2,1,0:T(8,128)S(1)} %add.13), channel_id=1, source_target_pairs={{0,1},{1,0},{2,3},{3,2},{4,5},{5,4},{6,7},{7,6},{8,9},{9,8},{10,11... | collective-permute-start | bytes 73736 | tf_op jit(solution)/shard_map/ppermute | solution.py:500
  19.2 5.7 %collective-permute-start.3 = (f32[6,8,128]{2,1,0:T(8,128)S(1)}, f32[6,8,128]{2,1,0:T(8,128)S(1)}, u32[]{:S(2)}, u32[]{:S(2)}) collective-permute-start(f32[6,8,128]{2,1,0:T(8,128)S(1)} %add.15), channel_id=1, source_target_pairs={{1,2},{2,1},{5,6},{6,5},{9,10},{10,9},{13,14},{14,13},{17,18},{18,... | collective-permute-start | bytes 73736 | tf_op jit(solution)/shard_map/ppermute | solution.py:501

commit v6 on v5

--- a/solution.py
+++ b/solution.py
@@ -117,8 +117,8 @@
 
 def partial_kernel(
     rows, cols, images, gains, labels,
-    s0, scale, x1, x2, x3, x4, send_a, send_b, strip_a, strip_b, patch_out,
-    s1, s2, s3, s4, s5, y5, y6, label, gain, first_part, other_part, low, high, done,
+    s0, scale, x1, x2, x3, x4, send_a, send_b, strip_a, strip_b, patches,
+    s1, s2, s3, s4, s5, y5, y6, label, gain, first_part, other_part, low, high, slots, done, sent,
 ):
     row, col = place_of(CORES)
     copies = [
@@ -132,6 +132,7 @@
         copy.start()
     s0[:, 0:8, :] = jnp.zeros((PLANES, 8, LANES), f32)
     s0[:, 72:88, :] = jnp.zeros((PLANES, 16, LANES), f32)
+    slots[...] = jnp.zeros(slots.shape, f32)
     for store in (s1, s2, s3, s4, s5):
         depth = store.shape[1]
         store[:, 0:8, :] = jnp.zeros((PLANES, 8, LANES), f32)
@@ -181,7 +182,25 @@
     for k in range(SIDE[6] + 3):
         patch = patch + pltpu.roll(y6[line_of(6, k), :], AT_6 + PITCH_6 * k, 1)
     patch = patch[0:8, :] + pltpu.roll(patch[8:16, :], HALF, 1)
-    patch_out[...] = patch
+    width = cols + 2 * REACH_COLS
+    (is_5, row_5, col_5), (is_6, row_6, col_6) = patch_places((8, LANES), 1)
+    for down in range(-REACH_ROWS, REACH_ROWS + 1):
+        for over in range(-REACH_COLS, REACH_COLS + 1):
+            along, aside = row_6 + down, col_6 + 2 * over
+            held = is_6 & (along >= 0) & (along < SIDE[6] + 3) & (aside >= 0) & (aside < WIDE[6] + 3)
+            away = -(PITCH_6 * down + 2 * over) % LANES
+            block = jnp.where(held, pltpu.roll(patch, away, 1) if away else patch, 0.0)
+            if abs(down) < REACH_ROWS and abs(over) < REACH_COLS:
+                along, aside = row_5 + 2 * down, col_5 + 4 * over
+                held = is_5 & (along >= 0) & (along < SIDE[5] + 3) & (aside >= 0) & (aside < WIDE[5] + 3)
+                away = -(2 * PITCH_5 * down + 4 * over) % LANES
+                block = jnp.where(held, pltpu.roll(patch, away, 1) if away else patch, block)
+            slots[(row + (down + REACH_ROWS)) * width + col + (over + REACH_COLS)] = block
+    sends = []
+    for r in range(rows):
+        source = slots.at[pl.ds((r + REACH_ROWS) * width + REACH_COLS, cols)]
+        sends.append(pltpu.make_async_copy(source, patches.at[pl.ds(r * cols, cols)], sent.at[r]))
+        sends[r].start()
 
     levels = (None, x1, x2, x3, x4)
     odd = jnp.bitwise_and(col, 1) == 1
@@ -236,33 +255,12 @@
     upward = jnp.where(row == rows - 1, 0.0, high[...])
     send_a[...] = jnp.where(odd, downward, upward)
     send_b[...] = jnp.where(odd, upward, downward)
-
-
-def coarse_kernel(rows, cols, patch, rims, patches, send, slots):
-    row, col = place_of(CORES)
+    for copy in sends:
+        copy.wait()
+
+
+def tables_kernel(rims, inner, tile, top, send):
     send[...] = rims[...]
-    slots[...] = jnp.zeros(slots.shape, f32)
-    width = cols + 2 * REACH_COLS
-    (is_5, row_5, col_5), (is_6, row_6, col_6) = patch_places((8, LANES), 1)
-    values = patch[...]
-    for down in range(-REACH_ROWS, REACH_ROWS + 1):
-        for over in range(-REACH_COLS, REACH_COLS + 1):
-            along, aside = row_6 + down, col_6 + 2 * over
-            held = is_6 & (along >= 0) & (along < SIDE[6] + 3) & (aside >= 0) & (aside < WIDE[6] + 3)
-            away = -(PITCH_6 * down + 2 * over) % LANES
-            block = jnp.where(held, pltpu.roll(values, away, 1) if away else values, 0.0)
-            if abs(down) < REACH_ROWS and abs(over) < REACH_COLS:
-                along, aside = row_5 + 2 * down, col_5 + 4 * over
-                held = is_5 & (along >= 0) & (along < SIDE[5] + 3) & (aside >= 0) & (aside < WIDE[5] + 3)
-                away = -(2 * PITCH_5 * down + 4 * over) % LANES
-                block = jnp.where(held, pltpu.roll(values, away, 1) if away else values, block)
-            slots[(row + (down + REACH_ROWS)) * width + col + (over + REACH_COLS)] = block
-    for r in range(rows):
-        for c in range(cols):
-            patches[r * cols + c] = slots[(r + REACH_ROWS) * width + c + REACH_COLS]
-
-
-def tables_kernel(after, inner, tile, top):
     inner[...] = expand_weights(1)
     tile[...] = expand_weights(0)
     _, (is_6, row_6, col_6) = patch_places((LANES, LANES), 0)
@@ -434,7 +432,7 @@
     images = images.reshape(INNER, ROWS[0], LANES)
     pinned = [pltpu.with_memory_space_constraint(x, pltpu.HBM) for x in (images, gains, labels)]
     levels = [floats(PLANES * ROWS[level], LANES) for level in range(1, 5)]
-    s0, scale, x1, x2, x3, x4, send_a, send_b, strip_a, strip_b, patch = pl.pallas_call(
+    s0, scale, x1, x2, x3, x4, send_a, send_b, strip_a, strip_b, patches = pl.pallas_call(
         lambda *refs: partial_kernel(rows, cols, *refs),
         out_shape=[
             floats(PLANES, 88, LANES),
@@ -444,10 +442,10 @@
             floats(RIMS, 8, LANES),
             floats(6, 8, LANES),
             floats(6, 8, LANES),
-            floats(8, LANES),
+            floats(rows * cols, 8, LANES),
         ],
         in_specs=[HBM] * 3,
-        out_specs=[VMEM] * 11,
+        out_specs=[VMEM] * 10 + [HBM],
         scratch_shapes=[
             scratch(PLANES, 56, LANES),
             scratch(PLANES, 40, LANES),
@@ -462,30 +460,23 @@
             scratch(2, STRIP, LANES),
             scratch(RIMS, 8, LANES),
             scratch(RIMS, 8, LANES),
+            scratch((rows + 2 * REACH_ROWS) * (cols + 2 * REACH_COLS), 8, LANES),
             pltpu.SemaphoreType.DMA((EXPOSURES + 2,)),
+            pltpu.SemaphoreType.DMA((rows,)),
         ],
         compiler_params=PARAMS,
         name="partial_levels",
     )(*pinned)
     got_b = lax.ppermute(send_b, ("chip", "core"), swaps(rows, 1))
-    patches, send_a = pl.pallas_call(
-        lambda *refs: coarse_kernel(rows, cols, *refs),
-        out_shape=[floats(rows * cols, 8, LANES), floats(RIMS, 8, LANES)],
-        in_specs=[VMEM] * 2,
-        out_specs=[VMEM] * 2,
-        scratch_shapes=[scratch((rows + 2 * REACH_ROWS) * (cols + 2 * REACH_COLS), 8, LANES)],
-        compiler_params=PARAMS,
-        name="coarse_patches",
-    )(patch, send_a)
-    got_a = lax.ppermute(send_a, "core", swaps(CORES, 0))
-    inner, tile, top = pl.pallas_call(
+    inner, tile, top, send_a = pl.pallas_call(
         tables_kernel,
-        out_shape=[halves(2 * LANES, LANES)] * 3,
+        out_shape=[halves(2 * LANES, LANES)] * 3 + [floats(RIMS, 8, LANES)],
         in_specs=[VMEM],
-        out_specs=[VMEM] * 3,
+        out_specs=[VMEM] * 4,
         compiler_params=PARAMS,
         name="expand_tables",
-    )(strip_a)
+    )(send_a)
+    got_a = lax.ppermute(send_a, "core", swaps(CORES, 0))
     odd = lax.axis_index("core") == 1
     rims_a, rims_b = got_a[2 * SLOTS :], got_b[2 * SLOTS :]
     below, above = jnp.where(odd, rims_a, rims_b), jnp.where(odd, rims_b, rims_a)
@@ -495,7 +486,6 @@
         none = jnp.zeros((1, 8, LANES), f32)
         rims = [low[0:1], none, high[0:1], low[1:2], high[1:2], low[2:3] + high[2:3]]
         strips.append(strip + jnp.concatenate(rims, 0))
-    strips, inner, tile, top, _ = lax.optimization_barrier((strips, inner, tile, top, patches))
     patches = lax.all_to_all(patches, ("chip", "core", "tx"), 0, 0, tiled=True)
     side_a = lax.ppermute(strips[0], "tx", swaps(cols, 0))
     side_b = lax.ppermute(strips[1], "tx", swaps(cols, 1))

time: 27.6 us -> 27.7 us (level)
  the two profiles are of different devices: /device:TPU:400 before, /device:TPU:336 now
where the time goes in v6:
time: 27.7 us; the launch traced here: 27.4 us
  starting transfers between devices  17.6 us (64%)
  Pallas kernels  6.39 us (23%)
  waiting for transfers between devices  3.24 us (12%)
    all_to_all x1, starting transfers between devices, shards(): patches = lax.all_to_all(patches, ('chip', 'core', 'tx'), 0, 0, tiled=True)  7.14 us
    ppermute x1, starting transfers between devices, shards(): got_a = lax.ppermute(send_a, 'core', swaps(CORES, 0))  4.76 us
    pallas_call x1, Pallas kernels, shards(): pl.pallas_call(lambda *refs: partial_kernel(rows, cols, *refs), out_shape...  3.36 us
    ppermute x1, starting transfers between devices, shards(): side_a = lax.ppermute(strips[0], 'tx', swaps(cols, 0))  3.08 us
    ppermute x1, waiting for transfers between devices, shards(): side_b = lax.ppermute(strips[1], 'tx', swaps(cols, 1))  2.5 us
    ppermute x1, starting transfers between devices, shards(): side_b = lax.ppermute(strips[1], 'tx', swaps(cols, 1))  1.92 us
    pallas_call x1, Pallas kernels, shards(): pl.pallas_call(lambda *refs: collapse_kernel(rows, cols, *refs), out_shap...  1.73 us
    ppermute x1, waiting for transfers between devices, shards(): side_a = lax.ppermute(strips[0], 'tx', swaps(cols, 0))  0.74 us
  transfers between devices with their start and end apart: 5, of which 2 were waited for; matrix products, arithmetic and copies ran while one was open for 0% of the time, Pallas kernels for 5%

profile of v6, /device:TPU:336, one launch (start us, length us, event | category | flops | bytes accessed | tf_op | source)
XLA Modules:
  0.0 27.4 jit_solution(1398164832577000940)
XLA Ops:
  0.0 3.4 %partial_levels.1 = (f32[16,88,128]{2,1,0:T(8,128)S(1)}, f32[12,8,128]{2,1,0:T(8,128)S(1)}, f32[640,128]{1,0:T(8,128)S(1)}, f32[384,128]{1,0:T(8,128)S(1)}, f32[...) custom-call(f32[12,64,128]{2,1,0:T(8,128)} %bitcast.1, ...), custom_call_target="tpu_custom_call" | custom-call | tf_op jit(solution)/shard_map/partial_levels/pallas_call | solution.py:435
  3.4 0.7 %collective-permute-start.1 = (f32[12,8,128]{2,1,0:T(8,128)S(1)}, f32[12,8,128]{2,1,0:T(8,128)S(1)}, u32[]{:S(2)}, u32[]{:S(2)}) collective-permute-start(f32[12,8,128]{2,1,0:T(8,128)S(1)} %get-tuple-element.38), channel_id=1, source_target_pairs={{4,8},{8,4},{12,16},{16,12},{20,24},{24,20},{5,9},{9,5},{13,17},{1... | collective-permute-start | bytes 147464 | tf_op jit(solution)/shard_map/ppermute | solution.py:470
  4.0 0.1 expand_tables.1
  4.1 4.8 %collective-permute-start = (f32[12,8,128]{2,1,0:T(8,128)S(1)}, f32[12,8,128]{2,1,0:T(8,128)S(1)}, u32[]{:S(2)}, u32[]{:S(2)}) collective-permute-start(f32[12,8,128]{2,1,0:T(8,128)S(1)} %get-tuple-element.37), channel_id=1, source_target_pairs={{0,4},{4,0},{1,5},{5,1},{2,6},{6,2},{3,7},{7,3},{8,12},{12,8},{9,1... | collective-permute-start | bytes 147464 | tf_op jit(solution)/shard_map/ppermute | solution.py:479
  8.9 7.1 %all-to-all-start = ((f32[32,8,128]{2,1,0:T(8,128)}), f32[32,8,128]{2,1,0:T(8,128)S(1)}, u32[]{:S(2)}, u32[]{:S(2)}) async-start(f32[32,8,128]{2,1,0:T(8,128)} %get-tuple-element.29), calls=%async_computation | async-start | bytes 262144 | tf_op jit(solution)/shard_map/all_to_all | solution.py:489
  16.1 0.0 collective-permute-done.1.got_b
  16.1 0.0 collective-permute-done.got_a
  16.2 3.1 %collective-permute-start.2 = (f32[6,8,128]{2,1,0:T(8,128)S(1)}, f32[6,8,128]{2,1,0:T(8,128)S(1)}, u32[]{:S(2)}, u32[]{:S(2)}) collective-permute-start(f32[6,8,128]{2,1,0:T(8,128)S(1)} %add.13), channel_id=1, source_target_pairs={{0,1},{1,0},{2,3},{3,2},{4,5},{5,4},{6,7},{7,6},{8,9},{9,8},{10,11... | collective-permute-start | bytes 73736 | tf_op jit(solution)/shard_map/ppermute | solution.py:490
  19.3 1.9 %collective-permute-start.3 = (f32[6,8,128]{2,1,0:T(8,128)S(1)}, f32[6,8,128]{2,1,0:T(8,128)S(1)}, u32[]{:S(2)}, u32[]{:S(2)}) collective-permute-start(f32[6,8,128]{2,1,0:T(8,128)S(1)} %add.15), channel_id=1, source_target_pairs={{1,2},{2,1},{5,6},{6,5},{9,10},{10,9},{13,14},{14,13},{17,18},{18,... | collective-permute-start | bytes 73736 | tf_op jit(solution)/shard_map/ppermute | solution.py:491
  21.2 0.7 %collective-permute-done.2.side = f32[6,8,128]{2,1,0:T(8,128)S(1)} collective-permute-done((f32[6,8,128]{2,1,0:T(8,128)S(1)}, f32[6,8,128]{2,1,0:T(8,128)S(1)}, u32[]{:S(2)}, u32[]{:S(2)}) %collective-permute-start.2) | collective-permute-done | bytes 24608 | tf_op jit(solution)/shard_map/ppermute | solution.py:490
  21.9 0.5 %add_rims.1 = (f32[640,128]{1,0:T(8,128)S(1)}, f32[384,128]{1,0:T(8,128)S(1)}, f32[256,128]{1,0:T(8,128)S(1)}, f32[128,128]{1,0:T(8,128)S(1)}) custom-call(f32[640,128]{1,0:T(8,128)S(1)} %get-tuple-element.32.x1, f32[384,128]{1,0:T(8,128)S(1)} %get-tuple-element.33.x2, f32[256,128]{1,0:T(8,128)S(1)} %get-tuple-element.34.x3, ...), custom_call_target="tpu_custom_call" | custom-call | tf_op jit(solution)/shard_map/add_rims/pallas_call | solution.py:492
  22.5 2.5 %collective-permute-done.3.side = f32[6,8,128]{2,1,0:T(8,128)S(1)} collective-permute-done((f32[6,8,128]{2,1,0:T(8,128)S(1)}, f32[6,8,128]{2,1,0:T(8,128)S(1)}, u32[]{:S(2)}, u32[]{:S(2)}) %collective-permute-start.3) | collective-permute-done | bytes 24608 | tf_op jit(solution)/shard_map/ppermute | solution.py:491
  25.0 0.7 %fine_laplacians.1 = (f32[3,64,128]{2,1,0:T(8,128)S(1)}, f32[3,40,128]{2,1,0:T(8,128)S(1)}, f32[3,24,128]{2,1,0:T(8,128)S(1)}, f32[3,16,128]{2,1,0:T(8,128)S(1)}, f32[128,128]{1,0:T(8,128)S(1)}) custom-call(f32[16,88,128]{2,1,0:T(8,128)S(1)} %get-tuple-element.30.s0, f32[12,8,128]{2,1,0:T(8,128)S(1)} %get-tuple-element.31.scale, ...), custom_call_target="tpu_custom_call" | custom-call | tf_op jit(solution)/shard_map/fine_laplacians/pallas_call | solution.py:501
  25.7 0.0 all-to-all-done.refs_0_
  25.7 1.7 %collapse.1 = f32[3,64,128]{2,1,0:T(8,128)} custom-call(f32[32,8,128]{2,1,0:T(8,128)S(1)} %all-to-all-done.refs_0_, f32[3,64,128]{2,1,0:T(8,128)S(1)} %get-tuple-element.47.refs_1_, f32[3,40,128]{2,1,0:T(8,128)S(1)} %get-tuple-element.48.refs_2_, f32[3,24,128]{2,1,0:T(8,128)S(1)} %get-tuple-element.49.refs_3_, f32[3,16,128]{2,1,0:T(8,128)S(1)} %get-tuple-element.50.refs_4_, ...), custom_call_target="tpu_custom_call" | custom-call | tf_op jit(solution)/shard_map/collapse/pallas_call | solution.py:517
  (9 shorter events, 0.0 us)
Async XLA Ops:
  3.4 12.7 %collective-permute-start.1 = (f32[12,8,128]{2,1,0:T(8,128)S(1)}, f32[12,8,128]{2,1,0:T(8,128)S(1)}, u32[]{:S(2)}, u32[]{:S(2)}) collective-permute-start(f32[12,8,128]{2,1,0:T(8,128)S(1)} %get-tuple-element.38), channel_id=1, source_target_pairs={{4,8},{8,4},{12,16},{16,12},{20,24},{24,20},{5,9},{9,5},{13,17},{1... | collective-permute-start | bytes 147464 | tf_op jit(solution)/shard_map/ppermute | solution.py:470
  4.1 11.9 %collective-permute-start = (f32[12,8,128]{2,1,0:T(8,128)S(1)}, f32[12,8,128]{2,1,0:T(8,128)S(1)}, u32[]{:S(2)}, u32[]{:S(2)}) collective-permute-start(f32[12,8,128]{2,1,0:T(8,128)S(1)} %get-tuple-element.37), channel_id=1, source_target_pairs={{0,4},{4,0},{1,5},{5,1},{2,6},{6,2},{3,7},{7,3},{8,12},{12,8},{9,1... | collective-permute-start | bytes 147464 | tf_op jit(solution)/shard_map/ppermute | solution.py:479
  8.9 16.8 %all-to-all-start = ((f32[32,8,128]{2,1,0:T(8,128)}), f32[32,8,128]{2,1,0:T(8,128)S(1)}, u32[]{:S(2)}, u32[]{:S(2)}) async-start(f32[32,8,128]{2,1,0:T(8,128)} %get-tuple-element.29), calls=%async_computation | async-start | bytes 262144 | tf_op jit(solution)/shard_map/all_to_all | solution.py:489
  16.2 5.8 %collective-permute-start.2 = (f32[6,8,128]{2,1,0:T(8,128)S(1)}, f32[6,8,128]{2,1,0:T(8,128)S(1)}, u32[]{:S(2)}, u32[]{:S(2)}) collective-permute-start(f32[6,8,128]{2,1,0:T(8,128)S(1)} %add.13), channel_id=1, source_target_pairs={{0,1},{1,0},{2,3},{3,2},{4,5},{5,4},{6,7},{7,6},{8,9},{9,8},{10,11... | collective-permute-start | bytes 73736 | tf_op jit(solution)/shard_map/ppermute | solution.py:490
  19.3 5.7 %collective-permute-start.3 = (f32[6,8,128]{2,1,0:T(8,128)S(1)}, f32[6,8,128]{2,1,0:T(8,128)S(1)}, u32[]{:S(2)}, u32[]{:S(2)}) collective-permute-start(f32[6,8,128]{2,1,0:T(8,128)S(1)} %add.15), channel_id=1, source_target_pairs={{1,2},{2,1},{5,6},{6,5},{9,10},{10,9},{13,14},{14,13},{17,18},{18,... | collective-permute-start | bytes 73736 | tf_op jit(solution)/shard_map/ppermute | solution.py:491

commit v7 on v6

--- a/solution.py
+++ b/solution.py
@@ -66,6 +66,12 @@
     high = values.astype(bf16)
     low = (values - high.astype(f32)).astype(bf16)
     return jnp.dot(jnp.concatenate([high, low], 1), weights, preferred_element_type=f32)
+
+
+def split_dot_2(values, weights):
+    high = values.astype(bf16)
+    low = (values - high.astype(f32)).astype(bf16)
+    return jnp.dot(jnp.concatenate([high, low, high], 1), weights, preferred_element_type=f32)
 
 
 def in_slab(level, row, col, rows, cols):
@@ -289,7 +295,37 @@
             totals[level][place, :] = parts[level][place, :] + part
 
 
-def rims_kernel(x1, x2, x3, x4, got_a, got_b, side, t1, t2, t3, t4, held):
+def rims_kernel(
+    cols, x1, x2, x3, x4, got_a, got_b, side, inner, tile, s0, scale,
+    t1, t2, t3, t4, wide_2, wide_3, wide_4, chosen, held,
+):
+    col = lax.axis_index("tx")
+    step = inner[0:LANES, :].astype(f32)
+
+    def masked(level):
+        across = iota((LANES, LANES), 1)
+        first, last = 1 - WIDE[level] * col, 1 + WIDE[level] * (cols - col)
+        return jnp.where((across >= first) & (across < last), step, 0.0).astype(bf16)
+
+    def halved(weights):
+        high = weights.astype(bf16)
+        return high, (weights - high.astype(f32)).astype(bf16)
+
+    weights = jnp.dot(masked(1), tile[0:LANES, :], preferred_element_type=f32).astype(bf16)
+    wide_2[...] = jnp.concatenate([weights, weights], 0)
+    high, low = halved(jnp.dot(masked(2), weights, preferred_element_type=f32))
+    wide_3[...] = jnp.concatenate([high, high, low], 0)
+    both = jnp.concatenate([masked(3), masked(3)], 1)
+    weights = jnp.dot(both, jnp.concatenate([high, low], 0), preferred_element_type=f32)
+    high, low = halved(weights)
+    wide_4[...] = jnp.concatenate([high, high, low], 0)
+    for b in range(BANDS):
+        total = jnp.zeros((ROWS[0], LANES), f32)
+        for e in range(EXPOSURES):
+            p = e * BANDS + b
+            total = total + s0[INNER + e, 8:72, :] * (s0[p, 8:72, :] * scale[p, 0:1, :])
+        chosen[b] = total
+
     row_odd = lax.axis_index("core") == 1
     col_odd = jnp.bitwise_and(lax.axis_index("tx"), 1) == 1
     totals = (None, t1, t2, t3, t4)
@@ -305,7 +341,7 @@
 
 
 def fine_kernel(
-    s0, scale, x1, x2, x3, x4, side, inner, tile,
+    s0, chosen, x1, x2, x3, x4, side, inner, tile, wide_2, wide_3,
     b0, b1, b2, b3, t4,
     t1, t2, t3, held, across, spread,
 ):
@@ -321,26 +357,31 @@
             spread[:, 0 : ROWS[3], :] = jnp.zeros((INNER, ROWS[3], LANES), f32)
         expand_rows(across, spread, PAIRS[level])
         here = totals[level]
+        bands = []
         for b in range(BANDS):
             total = jnp.zeros((ROWS[level], LANES), f32)
             for e in range(EXPOSURES):
                 p = e * BANDS + b
                 laplace = here[plane_of(level, p), :] - spread[p, 0 : ROWS[level], :]
                 total = total + here[plane_of(level, INNER + e), :] * laplace
-            out[b] = total
+            bands.append(total)
+        bands = jnp.concatenate(bands + [jnp.zeros((ROWS[level], LANES), f32)], 0)
+        if level == 3:
+            bands = split_dot_2(bands, wide_3[...])
+        else:
+            bands = split_dot(bands, wide_2[...] if level == 2 else tile[...])
+        out[...] = bands[0 : BANDS * ROWS[level]].reshape(BANDS, ROWS[level], LANES)
     across[...] = split_dot(t1[0 : INNER * ROWS[1], :], tile[...]).reshape(INNER, ROWS[1], LANES)
     expand_rows_tile(across, spread, PAIRS[0])
     for b in range(BANDS):
-        total = jnp.zeros((ROWS[0], LANES), f32)
+        total = chosen[b]
         for e in range(EXPOSURES):
-            p = e * BANDS + b
-            laplace = s0[p, 8:72, :] * scale[p, 0:1, :] - spread[p]
-            total = total + s0[INNER + e, 8:72, :] * laplace
+            total = total - s0[INNER + e, 8:72, :] * spread[e * BANDS + b]
         b0[b] = total
 
 
 def collapse_kernel(
-    rows, cols, patches, b0, b1, b2, b3, t4, inner, tile, top_weights, out,
+    rows, cols, patches, b0, b1, b2, b3, t4, inner, wide_4, top_weights, out,
     v5, window, c4, c3, c2, c1, across, spread,
 ):
     row, col = place_of(CORES)
@@ -387,20 +428,18 @@
         c4[b] = jnp.where(inside, total, 0.0)
     c4[BANDS] = jnp.zeros((8, LANES), f32)
 
+    wide = split_dot_2(c4[...].reshape(EXPOSURES * ROWS[4], LANES), wide_4[...])
+    c4[...] = wide.reshape(EXPOSURES, ROWS[4], LANES)
+    spread[0:BANDS, 0 : ROWS[3], :] = jnp.zeros((BANDS, ROWS[3], LANES), f32)
     for level, source, target, band in ((3, c4, c3, b3), (2, c3, c2, b2), (1, c2, c1, b1)):
-        count, depth = ROWS[level + 1], ROWS[level]
-        wide = split_dot(source[...].reshape(EXPOSURES * count, LANES), inner[...])
-        across[0:EXPOSURES, 0:count, :] = wide.reshape(EXPOSURES, count, LANES)
-        if level == 3:
-            spread[0:BANDS, 0:depth, :] = jnp.zeros((BANDS, depth, LANES), f32)
-        expand_rows(across.at[0:BANDS], spread.at[0:BANDS], PAIRS[level])
-        inside = in_slab(level, row, col, rows, cols)
+        depth = ROWS[level]
+        expand_rows(source.at[0:BANDS], spread.at[0:BANDS], PAIRS[level])
+        along = iota((depth, LANES), 0)
+        first, last = 1 - SIDE[level] * row, 1 + SIDE[level] * (rows - row)
+        inside = (along >= first) & (along < last)
         for b in range(BANDS):
             target[b] = jnp.where(inside, band[b] + spread[b, 0:depth, :], 0.0)
-        target[BANDS] = jnp.zeros((depth, LANES), f32)
-    wide = split_dot(c1[...].reshape(EXPOSURES * ROWS[1], LANES), tile[...])
-    across[0:EXPOSURES] = wide.reshape(EXPOSURES, ROWS[1], LANES)
-    expand_rows_tile(across.at[0:BANDS], spread.at[0:BANDS], PAIRS[0])
+    expand_rows_tile(c1, spread.at[0:BANDS], PAIRS[0])
     out[...] = b0[...] + spread[0:BANDS]
 
 
@@ -489,19 +528,21 @@
     patches = lax.all_to_all(patches, ("chip", "core", "tx"), 0, 0, tiled=True)
     side_a = lax.ppermute(strips[0], "tx", swaps(cols, 0))
     side_b = lax.ppermute(strips[1], "tx", swaps(cols, 1))
-    x1, x2, x3, x4 = pl.pallas_call(
-        rims_kernel,
-        out_shape=levels,
-        in_specs=[VMEM] * 7,
-        out_specs=[VMEM] * 4,
+    x1, x2, x3, x4, wide_2, wide_3, wide_4, chosen = pl.pallas_call(
+        lambda *refs: rims_kernel(cols, *refs),
+        out_shape=levels
+        + [halves(2 * LANES, LANES), halves(3 * LANES, LANES), halves(3 * LANES, LANES)]
+        + [floats(BANDS, ROWS[0], LANES)],
+        in_specs=[VMEM] * 11,
+        out_specs=[VMEM] * 8,
         scratch_shapes=[scratch(STRIP, LANES)],
         compiler_params=PARAMS,
         name="add_rims",
-    )(x1, x2, x3, x4, got_a, got_b, side_a)
+    )(x1, x2, x3, x4, got_a, got_b, side_a, inner, tile, s0, scale)
     b0, b1, b2, b3, t4 = pl.pallas_call(
         fine_kernel,
         out_shape=[floats(BANDS, ROWS[level], LANES) for level in range(4)] + [levels[3]],
-        in_specs=[VMEM] * 9,
+        in_specs=[VMEM] * 11,
         out_specs=[VMEM] * 5,
         scratch_shapes=[
             scratch(PLANES * ROWS[1], LANES),
@@ -513,7 +554,7 @@
         ],
         compiler_params=PARAMS,
         name="fine_laplacians",
-    )(s0, scale, x1, x2, x3, x4, side_b, inner, tile)
+    )(s0, chosen, x1, x2, x3, x4, side_b, inner, tile, wide_2, wide_3)
     return pl.pallas_call(
         lambda *refs: collapse_kernel(rows, cols, *refs),
         out_shape=floats(BANDS, ROWS[0], LANES),
@@ -523,15 +564,15 @@
             scratch(PLANES, LANES),
             scratch(PLANES * 8, LANES),
             scratch(EXPOSURES, ROWS[4], LANES),
-            scratch(EXPOSURES, ROWS[3], LANES),
-            scratch(EXPOSURES, ROWS[2], LANES),
-            scratch(EXPOSURES, ROWS[1], LANES),
-            scratch(PLANES, ROWS[1], LANES),
+            scratch(BANDS, ROWS[3], LANES),
+            scratch(BANDS, ROWS[2], LANES),
+            scratch(BANDS, ROWS[1], LANES),
+            scratch(PLANES, ROWS[4], LANES),
             scratch(PLANES, ROWS[0], LANES),
         ],
         compiler_params=PARAMS,
         name="collapse",
-    )(patches, b0, b1, b2, b3, t4, inner, tile, top)
+    )(patches, b0, b1, b2, b3, t4, inner, wide_4, top)
 
 
 def solution(mesh):

time: 27.7 us -> 27.8 us (level)
  the two profiles are of different devices: /device:TPU:336 before, /device:TPU:400 now
where the time goes in v7:
time: 27.8 us; the launch traced here: 27.5 us
  starting transfers between devices  17.6 us (63%)
  Pallas kernels  6.53 us (23%)
  waiting for transfers between devices  3.23 us (12%)
    all_to_all x1, starting transfers between devices, shards(): patches = lax.all_to_all(patches, ('chip', 'core', 'tx'), 0, 0, tiled=True)  7.14 us
    ppermute x1, starting transfers between devices, shards(): got_a = lax.ppermute(send_a, 'core', swaps(CORES, 0))  4.76 us
    pallas_call x1, Pallas kernels, shards(): pl.pallas_call(lambda *refs: partial_kernel(rows, cols, *refs), out_shape...  3.37 us
    ppermute x1, starting transfers between devices, shards(): side_a = lax.ppermute(strips[0], 'tx', swaps(cols, 0))  3.08 us
    ppermute x1, waiting for transfers between devices, shards(): side_b = lax.ppermute(strips[1], 'tx', swaps(cols, 1))  2.49 us
    ppermute x1, starting transfers between devices, shards(): side_b = lax.ppermute(strips[1], 'tx', swaps(cols, 1))  1.92 us
    pallas_call x1, Pallas kernels, shards(): pl.pallas_call(lambda *refs: collapse_kernel(rows, cols, *refs), out_shap...  1.36 us
    pallas_call x1, Pallas kernels, shards(): pl.pallas_call(fine_kernel, out_shape=[floats(BANDS, ROWS[level], LANES)...  1.16 us
  transfers between devices with their start and end apart: 5, of which 2 were waited for; matrix products, arithmetic and copies ran while one was open for 0% of the time, Pallas kernels for 7%

profile of v7, /device:TPU:400, one launch (start us, length us, event | category | flops | bytes accessed | tf_op | source)
XLA Modules:
  0.0 27.5 jit_solution(12876478013334566868)
XLA Ops:
  0.0 3.4 %partial_levels.1 = (f32[16,88,128]{2,1,0:T(8,128)S(1)}, f32[12,8,128]{2,1,0:T(8,128)S(1)}, f32[640,128]{1,0:T(8,128)S(1)}, f32[384,128]{1,0:T(8,128)S(1)}, f32[...) custom-call(f32[12,64,128]{2,1,0:T(8,128)} %bitcast.1, ...), custom_call_target="tpu_custom_call" | custom-call | tf_op jit(solution)/shard_map/partial_levels/pallas_call | solution.py:474
  3.4 0.7 %collective-permute-start.1 = (f32[12,8,128]{2,1,0:T(8,128)S(1)}, f32[12,8,128]{2,1,0:T(8,128)S(1)}, u32[]{:S(2)}, u32[]{:S(2)}) collective-permute-start(f32[12,8,128]{2,1,0:T(8,128)S(1)} %get-tuple-element.41), channel_id=1, source_target_pairs={{4,8},{8,4},{12,16},{16,12},{20,24},{24,20},{5,9},{9,5},{13,17},{1... | collective-permute-start | bytes 147464 | tf_op jit(solution)/shard_map/ppermute | solution.py:509
  4.0 0.1 expand_tables.1
  4.1 4.8 %collective-permute-start = (f32[12,8,128]{2,1,0:T(8,128)S(1)}, f32[12,8,128]{2,1,0:T(8,128)S(1)}, u32[]{:S(2)}, u32[]{:S(2)}) collective-permute-start(f32[12,8,128]{2,1,0:T(8,128)S(1)} %get-tuple-element.40), channel_id=1, source_target_pairs={{0,4},{4,0},{1,5},{5,1},{2,6},{6,2},{3,7},{7,3},{8,12},{12,8},{9,1... | collective-permute-start | bytes 147464 | tf_op jit(solution)/shard_map/ppermute | solution.py:518
  8.9 7.1 %all-to-all-start = ((f32[32,8,128]{2,1,0:T(8,128)}), f32[32,8,128]{2,1,0:T(8,128)S(1)}, u32[]{:S(2)}, u32[]{:S(2)}) async-start(f32[32,8,128]{2,1,0:T(8,128)} %get-tuple-element.33), calls=%async_computation | async-start | bytes 262144 | tf_op jit(solution)/shard_map/all_to_all | solution.py:528
  16.1 0.0 collective-permute-done.1.refs_5_
  16.1 0.0 collective-permute-done.refs_4_
  16.2 3.1 %collective-permute-start.2 = (f32[6,8,128]{2,1,0:T(8,128)S(1)}, f32[6,8,128]{2,1,0:T(8,128)S(1)}, u32[]{:S(2)}, u32[]{:S(2)}) collective-permute-start(f32[6,8,128]{2,1,0:T(8,128)S(1)} %add.13), channel_id=1, source_target_pairs={{0,1},{1,0},{2,3},{3,2},{4,5},{5,4},{6,7},{7,6},{8,9},{9,8},{10,11... | collective-permute-start | bytes 73736 | tf_op jit(solution)/shard_map/ppermute | solution.py:529
  19.3 1.9 %collective-permute-start.3 = (f32[6,8,128]{2,1,0:T(8,128)S(1)}, f32[6,8,128]{2,1,0:T(8,128)S(1)}, u32[]{:S(2)}, u32[]{:S(2)}) collective-permute-start(f32[6,8,128]{2,1,0:T(8,128)S(1)} %add.15), channel_id=1, source_target_pairs={{1,2},{2,1},{5,6},{6,5},{9,10},{10,9},{13,14},{14,13},{17,18},{18,... | collective-permute-start | bytes 73736 | tf_op jit(solution)/shard_map/ppermute | solution.py:530
  21.2 0.7 %collective-permute-done.2.refs_6_ = f32[6,8,128]{2,1,0:T(8,128)S(1)} collective-permute-done((f32[6,8,128]{2,1,0:T(8,128)S(1)}, f32[6,8,128]{2,1,0:T(8,128)S(1)}, u32[]{:S(2)}, u32[]{:S(2)}) %collective-permute-start.2) | collective-permute-done | bytes 24608 | tf_op jit(solution)/shard_map/ppermute | solution.py:529
  21.9 0.6 %add_rims.1 = (f32[640,128]{1,0:T(8,128)S(1)}, f32[384,128]{1,0:T(8,128)S(1)}, f32[256,128]{1,0:T(8,128)S(1)}, f32[128,128]{1,0:T(8,128)S(1)}, bf16[256,128]{1,0...) custom-call(f32[640,128]{1,0:T(8,128)S(1)} %get-tuple-element.35.refs_0_, ...), custom_call_target="tpu_custom_call" | custom-call | tf_op jit(solution)/shard_map/add_rims/pallas_call | solution.py:531
  22.5 2.5 %collective-permute-done.3.side = f32[6,8,128]{2,1,0:T(8,128)S(1)} collective-permute-done((f32[6,8,128]{2,1,0:T(8,128)S(1)}, f32[6,8,128]{2,1,0:T(8,128)S(1)}, u32[]{:S(2)}, u32[]{:S(2)}) %collective-permute-start.3) | collective-permute-done | bytes 24608 | tf_op jit(solution)/shard_map/ppermute | solution.py:530
  25.0 1.2 %fine_laplacians.1 = (f32[3,64,128]{2,1,0:T(8,128)S(1)}, f32[3,40,128]{2,1,0:T(8,128)S(1)}, f32[3,24,128]{2,1,0:T(8,128)S(1)}, f32[3,16,128]{2,1,0:T(8,128)S(1)}, f32[128,128]{1,0:T(8,128)S(1)}) custom-call(f32[16,88,128]{2,1,0:T(8,128)S(1)} %get-tuple-element.34.refs_9_.s0, f32[3,64,128]{2,1,0:T(8,128)S(1)} %get-tuple-element.46.chosen, ...), custom_call_target="tpu_custom_call" | custom-call | tf_op jit(solution)/shard_map/fine_laplacians/pallas_call | solution.py:542
  26.2 0.0 all-to-all-done.refs_0_
  26.2 1.4 %collapse.1 = f32[3,64,128]{2,1,0:T(8,128)} custom-call(f32[32,8,128]{2,1,0:T(8,128)S(1)} %all-to-all-done.refs_0_, f32[3,64,128]{2,1,0:T(8,128)S(1)} %get-tuple-element.54.refs_1_, f32[3,40,128]{2,1,0:T(8,128)S(1)} %get-tuple-element.55.refs_2_, f32[3,24,128]{2,1,0:T(8,128)S(1)} %get-tuple-element.56.refs_3_, f32[3,16,128]{2,1,0:T(8,128)S(1)} %get-tuple-element.57.refs_4_, ...), custom_call_target="tpu_custom_call" | custom-call | tf_op jit(solution)/shard_map/collapse/pallas_call | solution.py:558
  (9 shorter events, 0.0 us)
Async XLA Ops:
  3.4 12.7 %collective-permute-start.1 = (f32[12,8,128]{2,1,0:T(8,128)S(1)}, f32[12,8,128]{2,1,0:T(8,128)S(1)}, u32[]{:S(2)}, u32[]{:S(2)}) collective-permute-start(f32[12,8,128]{2,1,0:T(8,128)S(1)} %get-tuple-element.41), channel_id=1, source_target_pairs={{4,8},{8,4},{12,16},{16,12},{20,24},{24,20},{5,9},{9,5},{13,17},{1... | collective-permute-start | bytes 147464 | tf_op jit(solution)/shard_map/ppermute | solution.py:509
  4.1 11.9 %collective-permute-start = (f32[12,8,128]{2,1,0:T(8,128)S(1)}, f32[12,8,128]{2,1,0:T(8,128)S(1)}, u32[]{:S(2)}, u32[]{:S(2)}) collective-permute-start(f32[12,8,128]{2,1,0:T(8,128)S(1)} %get-tuple-element.40), channel_id=1, source_target_pairs={{0,4},{4,0},{1,5},{5,1},{2,6},{6,2},{3,7},{7,3},{8,12},{12,8},{9,1... | collective-permute-start | bytes 147464 | tf_op jit(solution)/shard_map/ppermute | solution.py:518
  8.9 17.3 %all-to-all-start = ((f32[32,8,128]{2,1,0:T(8,128)}), f32[32,8,128]{2,1,0:T(8,128)S(1)}, u32[]{:S(2)}, u32[]{:S(2)}) async-start(f32[32,8,128]{2,1,0:T(8,128)} %get-tuple-element.33), calls=%async_computation | async-start | bytes 262144 | tf_op jit(solution)/shard_map/all_to_all | solution.py:528
  16.2 5.8 %collective-permute-start.2 = (f32[6,8,128]{2,1,0:T(8,128)S(1)}, f32[6,8,128]{2,1,0:T(8,128)S(1)}, u32[]{:S(2)}, u32[]{:S(2)}) collective-permute-start(f32[6,8,128]{2,1,0:T(8,128)S(1)} %add.13), channel_id=1, source_target_pairs={{0,1},{1,0},{2,3},{3,2},{4,5},{5,4},{6,7},{7,6},{8,9},{9,8},{10,11... | collective-permute-start | bytes 73736 | tf_op jit(solution)/shard_map/ppermute | solution.py:529
  19.3 5.7 %collective-permute-start.3 = (f32[6,8,128]{2,1,0:T(8,128)S(1)}, f32[6,8,128]{2,1,0:T(8,128)S(1)}, u32[]{:S(2)}, u32[]{:S(2)}) collective-permute-start(f32[6,8,128]{2,1,0:T(8,128)S(1)} %add.15), channel_id=1, source_target_pairs={{1,2},{2,1},{5,6},{6,5},{9,10},{10,9},{13,14},{14,13},{17,18},{18,... | collective-permute-start | bytes 73736 | tf_op jit(solution)/shard_map/ppermute | solution.py:530

commit v8 on v7

--- a/solution.py
+++ b/solution.py
@@ -124,7 +124,7 @@
 def partial_kernel(
     rows, cols, images, gains, labels,
     s0, scale, x1, x2, x3, x4, send_a, send_b, strip_a, strip_b, patches,
-    s1, s2, s3, s4, s5, y5, y6, label, gain, first_part, other_part, low, high, slots, done, sent,
+    s1, s2, s3, s4, s5, y5, y6, across, label, gain, first_part, other_part, low, high, slots, done, sent,
 ):
     row, col = place_of(CORES)
     copies = [
@@ -145,41 +145,37 @@
         store[:, depth - 8 : depth, :] = jnp.zeros((PLANES, 8, LANES), f32)
     edge_weights, weights = reduce_weights(4), reduce_weights(3)
 
-    def reduce(source, level, first, planes, scales, weights):
-        count, held, sums = ROWS[level], len(planes), []
-        for p in planes:
-            tap = [source[p, pl.ds(first + k, count, stride=2), :] for k in range(5)]
-            total = tap[2] * 0.375 + (tap[1] + tap[3]) * 0.25 + (tap[0] + tap[4]) * 0.0625
-            sums.append(total if scales is None else total * scales[p])
-        result = split_dot(jnp.concatenate(sums, 0), weights).reshape(held, count, LANES)
-        return jnp.where(in_slab(level, row, col, rows, cols)[None], result, 0.0)
-
-    def finish(level, planes, result, store, out):
-        count, held = ROWS[level], len(planes)
-        if out is not None:
-            out[pl.ds(planes[0] * count, held * count), :] = result.reshape(held * count, LANES)
+    def reduce_rows(source, level, first, p, scale=None):
+        count = ROWS[level]
+        tap = [source[p, pl.ds(first + k, count, stride=2), :] for k in range(5)]
+        total = tap[2] * 0.375 + (tap[1] + tap[3]) * 0.25 + (tap[0] + tap[4]) * 0.0625
+        across[plane_of(level, p), :] = total if scale is None else total * scale
+
+    def reduce_columns(level, weights, store, out):
+        count = ROWS[level]
+        result = split_dot(across[0 : PLANES * count, :], weights).reshape(PLANES, count, LANES)
+        result = jnp.where(in_slab(level, row, col, rows, cols)[None], result, 0.0)
+        out[...] = result.reshape(PLANES * count, LANES)
         if store is not None:
-            store[planes[0] : planes[0] + held, 8 : 8 + count, :] = result
+            store[:, 8 : 8 + count, :] = result
 
     copies[0].wait()
     for e in range(EXPOSURES):
         s0[INNER + e, 8:72, :] = jnp.where(label[...] == e, 1.0, 0.0)
-    planes = range(INNER, PLANES)
-    finish(1, planes, reduce(s0, 1, 4, planes, None, edge_weights), s1, x1)
+        reduce_rows(s0, 1, 4, INNER + e)
     copies[1].wait()
     for p in range(INNER):
         scale[p] = jnp.full((8, LANES), gain[p // BANDS, p % BANDS], f32)
     for e in range(EXPOSURES):
-        planes = range(e * BANDS, (e + 1) * BANDS)
-        scales = {e * BANDS + b: gain[e, b] for b in range(BANDS)}
         copies[2 + e].wait()
-        finish(1, planes, reduce(s0, 1, 4, planes, scales, edge_weights), s1, x1)
+        for b in range(BANDS):
+            reduce_rows(s0, 1, 4, e * BANDS + b, gain[e, b])
+    reduce_columns(1, edge_weights, s1, x1)
     stores = ((2, s1, s2, x2), (3, s2, s3, x3), (4, s3, s4, x4), (5, s4, s5, y5), (6, s5, None, y6))
     for level, source, store, out in stores:
-        held = {2: 4, 3: 8}.get(level, PLANES)
-        for at in range(0, PLANES, held):
-            planes = range(at, at + held)
-            finish(level, planes, reduce(source, level, 5, planes, None, weights), store, out)
+        for p in range(PLANES):
+            reduce_rows(source, level, 5, p)
+        reduce_columns(level, weights, store, out)
 
     patch = jnp.zeros((PLANES, LANES), f32)
     for k in range(SIDE[5] + 3):
@@ -297,7 +293,7 @@
 
 def rims_kernel(
     cols, x1, x2, x3, x4, got_a, got_b, side, inner, tile, s0, scale,
-    t1, t2, t3, t4, wide_2, wide_3, wide_4, chosen, held,
+    t1, t2, t3, t4, wide, wide_4, chosen, held,
 ):
     col = lax.axis_index("tx")
     step = inner[0:LANES, :].astype(f32)
@@ -311,10 +307,10 @@
         high = weights.astype(bf16)
         return high, (weights - high.astype(f32)).astype(bf16)
 
-    weights = jnp.dot(masked(1), tile[0:LANES, :], preferred_element_type=f32).astype(bf16)
-    wide_2[...] = jnp.concatenate([weights, weights], 0)
-    high, low = halved(jnp.dot(masked(2), weights, preferred_element_type=f32))
-    wide_3[...] = jnp.concatenate([high, high, low], 0)
+    second = jnp.dot(masked(1), tile[0:LANES, :], preferred_element_type=f32).astype(bf16)
+    high, low = halved(jnp.dot(masked(2), second, preferred_element_type=f32))
+    weights = jnp.concatenate([high, second, tile[0:LANES, :], low], 1)
+    wide[...] = jnp.concatenate([weights, weights], 0)
     both = jnp.concatenate([masked(3), masked(3)], 1)
     weights = jnp.dot(both, jnp.concatenate([high, low], 0), preferred_element_type=f32)
     high, low = halved(weights)
@@ -341,42 +337,50 @@
 
 
 def fine_kernel(
-    s0, chosen, x1, x2, x3, x4, side, inner, tile, wide_2, wide_3,
+    s0, chosen, x1, x2, x3, x4, side, inner, tile, wide,
     b0, b1, b2, b3, t4,
-    t1, t2, t3, held, across, spread,
+    t1, t2, t3, held, u1, u2, u3, u4, d0, d1, d2, d3, bands,
 ):
     col_odd = jnp.bitwise_and(lax.axis_index("tx"), 1) == 1
     totals = (None, t1, t2, t3, t4)
     add_side(totals, (None, x1, x2, x3, x4), side, jnp.logical_not(col_odd), held)
 
-    for level in (3, 2, 1):
-        source, count, out = totals[level + 1], ROWS[level + 1], (None, b1, b2, b3)[level]
-        wide = split_dot(source[0 : INNER * count, :], inner[...])
-        across[:, 0:count, :] = wide.reshape(INNER, count, LANES)
-        if level == 3:
-            spread[:, 0 : ROWS[3], :] = jnp.zeros((INNER, ROWS[3], LANES), f32)
-        expand_rows(across, spread, PAIRS[level])
+    values = [totals[level][0 : INNER * ROWS[level], :] for level in (4, 3, 2)]
+    values = split_dot(jnp.concatenate(values, 0), inner[...])
+    at = 0
+    for level, store in ((4, u4), (3, u3), (2, u2)):
+        count = INNER * ROWS[level]
+        store[...] = values[at : at + count, :].reshape(INNER, ROWS[level], LANES)
+        at += count
+    values = split_dot(t1[0 : INNER * ROWS[1], :], tile[...])
+    u1[...] = values.reshape(INNER, ROWS[1], LANES)
+    d3[...] = jnp.zeros((INNER, ROWS[3], LANES), f32)
+    at = 0
+    for level, source, spread in ((3, u4, d3), (2, u3, d2), (1, u2, d1)):
+        expand_rows(source, spread, PAIRS[level])
         here = totals[level]
-        bands = []
         for b in range(BANDS):
             total = jnp.zeros((ROWS[level], LANES), f32)
             for e in range(EXPOSURES):
                 p = e * BANDS + b
-                laplace = here[plane_of(level, p), :] - spread[p, 0 : ROWS[level], :]
+                laplace = here[plane_of(level, p), :] - spread[p]
                 total = total + here[plane_of(level, INNER + e), :] * laplace
-            bands.append(total)
-        bands = jnp.concatenate(bands + [jnp.zeros((ROWS[level], LANES), f32)], 0)
+            bands[at : at + ROWS[level], :] = total
+            at += ROWS[level]
+    values = split_dot(bands[...], wide[...])
+    at = 0
+    for k, level, out in ((0, 3, b3), (1, 2, b2), (2, 1, b1)):
+        count = BANDS * ROWS[level]
+        part = values[at : at + count, k * LANES : (k + 1) * LANES]
         if level == 3:
-            bands = split_dot_2(bands, wide_3[...])
-        else:
-            bands = split_dot(bands, wide_2[...] if level == 2 else tile[...])
-        out[...] = bands[0 : BANDS * ROWS[level]].reshape(BANDS, ROWS[level], LANES)
-    across[...] = split_dot(t1[0 : INNER * ROWS[1], :], tile[...]).reshape(INNER, ROWS[1], LANES)
-    expand_rows_tile(across, spread, PAIRS[0])
+            part = part + values[at : at + count, 3 * LANES :]
+        out[...] = part.reshape(BANDS, ROWS[level], LANES)
+        at += count
+    expand_rows_tile(u1, d0, PAIRS[0])
     for b in range(BANDS):
         total = chosen[b]
         for e in range(EXPOSURES):
-            total = total - s0[INNER + e, 8:72, :] * spread[e * BANDS + b]
+            total = total - s0[INNER + e, 8:72, :] * d0[e * BANDS + b]
         b0[b] = total
 
 
@@ -493,6 +497,7 @@
             scratch(PLANES, 24, LANES),
             scratch(PLANES * 8, LANES),
             scratch(PLANES * 8, LANES),
+            scratch(PLANES * ROWS[1], LANES),
             pltpu.VMEM((ROWS[0], LANES), jnp.int32),
             pltpu.SMEM((EXPOSURES, BANDS), f32),
             scratch(2, ROWS[1], LANES),
@@ -528,13 +533,13 @@
     patches = lax.all_to_all(patches, ("chip", "core", "tx"), 0, 0, tiled=True)
     side_a = lax.ppermute(strips[0], "tx", swaps(cols, 0))
     side_b = lax.ppermute(strips[1], "tx", swaps(cols, 1))
-    x1, x2, x3, x4, wide_2, wide_3, wide_4, chosen = pl.pallas_call(
+    x1, x2, x3, x4, wide, wide_4, chosen = pl.pallas_call(
         lambda *refs: rims_kernel(cols, *refs),
         out_shape=levels
-        + [halves(2 * LANES, LANES), halves(3 * LANES, LANES), halves(3 * LANES, LANES)]
+        + [halves(2 * LANES, 4 * LANES), halves(3 * LANES, LANES)]
         + [floats(BANDS, ROWS[0], LANES)],
         in_specs=[VMEM] * 11,
-        out_specs=[VMEM] * 8,
+        out_specs=[VMEM] * 7,
         scratch_shapes=[scratch(STRIP, LANES)],
         compiler_params=PARAMS,
         name="add_rims",
@@ -542,19 +547,19 @@
     b0, b1, b2, b3, t4 = pl.pallas_call(
         fine_kernel,
         out_shape=[floats(BANDS, ROWS[level], LANES) for level in range(4)] + [levels[3]],
-        in_specs=[VMEM] * 11,
+        in_specs=[VMEM] * 10,
         out_specs=[VMEM] * 5,
         scratch_shapes=[
             scratch(PLANES * ROWS[1], LANES),
             scratch(PLANES * ROWS[2], LANES),
             scratch(PLANES * ROWS[3], LANES),
             scratch(STRIP, LANES),
-            scratch(INNER, ROWS[1], LANES),
-            scratch(INNER, ROWS[0], LANES),
+            *[scratch(INNER, ROWS[level], LANES) for level in (1, 2, 3, 4, 0, 1, 2, 3)],
+            scratch(BANDS * (ROWS[1] + ROWS[2] + ROWS[3]), LANES),
         ],
         compiler_params=PARAMS,
         name="fine_laplacians",
-    )(s0, chosen, x1, x2, x3, x4, side_b, inner, tile, wide_2, wide_3)
+    )(s0, chosen, x1, x2, x3, x4, side_b, inner, tile, wide)
     return pl.pallas_call(
         lambda *refs: collapse_kernel(rows, cols, *refs),
         out_shape=floats(BANDS, ROWS[0], LANES),

time: 27.8 us -> 27.2 us (0.978)
  the two profiles are of different devices: /device:TPU:400 before, /device:TPU:368 now
where the time goes in v8:
time: 27.2 us; the launch traced here: 26.9 us
  starting transfers between devices  17.6 us (65%)
  Pallas kernels  5.91 us (22%)
  waiting for transfers between devices  3.23 us (12%)
    all_to_all x1, starting transfers between devices, shards(): patches = lax.all_to_all(patches, ('chip', 'core', 'tx'), 0, 0, tiled=True)  7.14 us
    ppermute x1, starting transfers between devices, shards(): got_a = lax.ppermute(send_a, 'core', swaps(CORES, 0))  4.76 us
    pallas_call x1, Pallas kernels, shards(): pl.pallas_call(lambda *refs: partial_kernel(rows, cols, *refs), out_shape...  3.16 us
    ppermute x1, starting transfers between devices, shards(): side_a = lax.ppermute(strips[0], 'tx', swaps(cols, 0))  3.08 us
    ppermute x1, waiting for transfers between devices, shards(): side_b = lax.ppermute(strips[1], 'tx', swaps(cols, 1))  2.48 us
    ppermute x1, starting transfers between devices, shards(): side_b = lax.ppermute(strips[1], 'tx', swaps(cols, 1))  1.92 us
    pallas_call x1, Pallas kernels, shards(): pl.pallas_call(lambda *refs: collapse_kernel(rows, cols, *refs), out_shap...  1.36 us
    pallas_call x1, Pallas kernels, shards(): pl.pallas_call(fine_kernel, out_shape=[floats(BANDS, ROWS[level], LANES)...  0.74 us
  transfers between devices with their start and end apart: 5, of which 2 were waited for; matrix products, arithmetic and copies ran while one was open for 0% of the time, Pallas kernels for 5%

profile of v8, /device:TPU:368, one launch (start us, length us, event | category | flops | bytes accessed | tf_op | source)
XLA Modules:
  0.0 26.9 jit_solution(4367952455978724479)
XLA Ops:
  0.0 3.2 %partial_levels.1 = (f32[16,88,128]{2,1,0:T(8,128)S(1)}, f32[12,8,128]{2,1,0:T(8,128)S(1)}, f32[640,128]{1,0:T(8,128)S(1)}, f32[384,128]{1,0:T(8,128)S(1)}, f32[...) custom-call(f32[12,64,128]{2,1,0:T(8,128)} %bitcast.1, ...), custom_call_target="tpu_custom_call" | custom-call | tf_op jit(solution)/shard_map/partial_levels/pallas_call | solution.py:478
  3.2 0.7 %collective-permute-start.1 = (f32[12,8,128]{2,1,0:T(8,128)S(1)}, f32[12,8,128]{2,1,0:T(8,128)S(1)}, u32[]{:S(2)}, u32[]{:S(2)}) collective-permute-start(f32[12,8,128]{2,1,0:T(8,128)S(1)} %get-tuple-element.40), channel_id=1, source_target_pairs={{4,8},{8,4},{12,16},{16,12},{20,24},{24,20},{5,9},{9,5},{13,17},{1... | collective-permute-start | bytes 147464 | tf_op jit(solution)/shard_map/ppermute | solution.py:514
  3.8 0.1 expand_tables.1
  3.9 4.8 %collective-permute-start = (f32[12,8,128]{2,1,0:T(8,128)S(1)}, f32[12,8,128]{2,1,0:T(8,128)S(1)}, u32[]{:S(2)}, u32[]{:S(2)}) collective-permute-start(f32[12,8,128]{2,1,0:T(8,128)S(1)} %get-tuple-element.39), channel_id=1, source_target_pairs={{0,4},{4,0},{1,5},{5,1},{2,6},{6,2},{3,7},{7,3},{8,12},{12,8},{9,1... | collective-permute-start | bytes 147464 | tf_op jit(solution)/shard_map/ppermute | solution.py:523
  8.7 7.1 %all-to-all-start = ((f32[32,8,128]{2,1,0:T(8,128)}), f32[32,8,128]{2,1,0:T(8,128)S(1)}, u32[]{:S(2)}, u32[]{:S(2)}) async-start(f32[32,8,128]{2,1,0:T(8,128)} %get-tuple-element.32), calls=%async_computation | async-start | bytes 262144 | tf_op jit(solution)/shard_map/all_to_all | solution.py:533
  15.8 0.0 collective-permute-done.1.refs_5_
  15.9 0.0 collective-permute-done.refs_4_
  16.0 3.1 %collective-permute-start.2 = (f32[6,8,128]{2,1,0:T(8,128)S(1)}, f32[6,8,128]{2,1,0:T(8,128)S(1)}, u32[]{:S(2)}, u32[]{:S(2)}) collective-permute-start(f32[6,8,128]{2,1,0:T(8,128)S(1)} %add.13), channel_id=1, source_target_pairs={{0,1},{1,0},{2,3},{3,2},{4,5},{5,4},{6,7},{7,6},{8,9},{9,8},{10,11... | collective-permute-start | bytes 73736 | tf_op jit(solution)/shard_map/ppermute | solution.py:534
  19.1 1.9 %collective-permute-start.3 = (f32[6,8,128]{2,1,0:T(8,128)S(1)}, f32[6,8,128]{2,1,0:T(8,128)S(1)}, u32[]{:S(2)}, u32[]{:S(2)}) collective-permute-start(f32[6,8,128]{2,1,0:T(8,128)S(1)} %add.15), channel_id=1, source_target_pairs={{1,2},{2,1},{5,6},{6,5},{9,10},{10,9},{13,14},{14,13},{17,18},{18,... | collective-permute-start | bytes 73736 | tf_op jit(solution)/shard_map/ppermute | solution.py:535
  21.0 0.7 %collective-permute-done.2.refs_6_ = f32[6,8,128]{2,1,0:T(8,128)S(1)} collective-permute-done((f32[6,8,128]{2,1,0:T(8,128)S(1)}, f32[6,8,128]{2,1,0:T(8,128)S(1)}, u32[]{:S(2)}, u32[]{:S(2)}) %collective-permute-start.2) | collective-permute-done | bytes 24608 | tf_op jit(solution)/shard_map/ppermute | solution.py:534
  21.7 0.6 %add_rims.1 = (f32[640,128]{1,0:T(8,128)S(1)}, f32[384,128]{1,0:T(8,128)S(1)}, f32[256,128]{1,0:T(8,128)S(1)}, f32[128,128]{1,0:T(8,128)S(1)}, bf16[256,512]{1,0...) custom-call(f32[640,128]{1,0:T(8,128)S(1)} %get-tuple-element.34.refs_0_, ...), custom_call_target="tpu_custom_call" | custom-call | tf_op jit(solution)/shard_map/add_rims/pallas_call | solution.py:536
  22.3 2.5 %collective-permute-done.3.side = f32[6,8,128]{2,1,0:T(8,128)S(1)} collective-permute-done((f32[6,8,128]{2,1,0:T(8,128)S(1)}, f32[6,8,128]{2,1,0:T(8,128)S(1)}, u32[]{:S(2)}, u32[]{:S(2)}) %collective-permute-start.3) | collective-permute-done | bytes 24608 | tf_op jit(solution)/shard_map/ppermute | solution.py:535
  24.8 0.7 %fine_laplacians.1 = (f32[3,64,128]{2,1,0:T(8,128)S(1)}, f32[3,40,128]{2,1,0:T(8,128)S(1)}, f32[3,24,128]{2,1,0:T(8,128)S(1)}, f32[3,16,128]{2,1,0:T(8,128)S(1)}, f32[128,128]{1,0:T(8,128)S(1)}) custom-call(f32[16,88,128]{2,1,0:T(8,128)S(1)} %get-tuple-element.33.refs_9_.s0, f32[3,64,128]{2,1,0:T(8,128)S(1)} %get-tuple-element.45.chosen, ...), custom_call_target="tpu_custom_call" | custom-call | tf_op jit(solution)/shard_map/fine_laplacians/pallas_call | solution.py:547
  25.5 0.0 all-to-all-done.refs_0_
  25.5 1.4 %collapse.1 = f32[3,64,128]{2,1,0:T(8,128)} custom-call(f32[32,8,128]{2,1,0:T(8,128)S(1)} %all-to-all-done.refs_0_, f32[3,64,128]{2,1,0:T(8,128)S(1)} %get-tuple-element.52.refs_1_, f32[3,40,128]{2,1,0:T(8,128)S(1)} %get-tuple-element.53.refs_2_, f32[3,24,128]{2,1,0:T(8,128)S(1)} %get-tuple-element.54.refs_3_, f32[3,16,128]{2,1,0:T(8,128)S(1)} %get-tuple-element.55.refs_4_, ...), custom_call_target="tpu_custom_call" | custom-call | tf_op jit(solution)/shard_map/collapse/pallas_call | solution.py:563
  (9 shorter events, 0.0 us)
Async XLA Ops:
  3.2 12.7 %collective-permute-start.1 = (f32[12,8,128]{2,1,0:T(8,128)S(1)}, f32[12,8,128]{2,1,0:T(8,128)S(1)}, u32[]{:S(2)}, u32[]{:S(2)}) collective-permute-start(f32[12,8,128]{2,1,0:T(8,128)S(1)} %get-tuple-element.40), channel_id=1, source_target_pairs={{4,8},{8,4},{12,16},{16,12},{20,24},{24,20},{5,9},{9,5},{13,17},{1... | collective-permute-start | bytes 147464 | tf_op jit(solution)/shard_map/ppermute | solution.py:514
  3.9 11.9 %collective-permute-start = (f32[12,8,128]{2,1,0:T(8,128)S(1)}, f32[12,8,128]{2,1,0:T(8,128)S(1)}, u32[]{:S(2)}, u32[]{:S(2)}) collective-permute-start(f32[12,8,128]{2,1,0:T(8,128)S(1)} %get-tuple-element.39), channel_id=1, source_target_pairs={{0,4},{4,0},{1,5},{5,1},{2,6},{6,2},{3,7},{7,3},{8,12},{12,8},{9,1... | collective-permute-start | bytes 147464 | tf_op jit(solution)/shard_map/ppermute | solution.py:523
  8.7 16.8 %all-to-all-start = ((f32[32,8,128]{2,1,0:T(8,128)}), f32[32,8,128]{2,1,0:T(8,128)S(1)}, u32[]{:S(2)}, u32[]{:S(2)}) async-start(f32[32,8,128]{2,1,0:T(8,128)} %get-tuple-element.32), calls=%async_computation | async-start | bytes 262144 | tf_op jit(solution)/shard_map/all_to_all | solution.py:533
  16.0 5.8 %collective-permute-start.2 = (f32[6,8,128]{2,1,0:T(8,128)S(1)}, f32[6,8,128]{2,1,0:T(8,128)S(1)}, u32[]{:S(2)}, u32[]{:S(2)}) collective-permute-start(f32[6,8,128]{2,1,0:T(8,128)S(1)} %add.13), channel_id=1, source_target_pairs={{0,1},{1,0},{2,3},{3,2},{4,5},{5,4},{6,7},{7,6},{8,9},{9,8},{10,11... | collective-permute-start | bytes 73736 | tf_op jit(solution)/shard_map/ppermute | solution.py:534
  19.1 5.7 %collective-permute-start.3 = (f32[6,8,128]{2,1,0:T(8,128)S(1)}, f32[6,8,128]{2,1,0:T(8,128)S(1)}, u32[]{:S(2)}, u32[]{:S(2)}) collective-permute-start(f32[6,8,128]{2,1,0:T(8,128)S(1)} %add.15), channel_id=1, source_target_pairs={{1,2},{2,1},{5,6},{6,5},{9,10},{10,9},{13,14},{14,13},{17,18},{18,... | collective-permute-start | bytes 73736 | tf_op jit(solution)/shard_map/ppermute | solution.py:535

commit v9 on v8

--- a/solution.py
+++ b/solution.py
@@ -66,12 +66,6 @@
     high = values.astype(bf16)
     low = (values - high.astype(f32)).astype(bf16)
     return jnp.dot(jnp.concatenate([high, low], 1), weights, preferred_element_type=f32)
-
-
-def split_dot_2(values, weights):
-    high = values.astype(bf16)
-    low = (values - high.astype(f32)).astype(bf16)
-    return jnp.dot(jnp.concatenate([high, low, high], 1), weights, preferred_element_type=f32)
 
 
 def in_slab(level, row, col, rows, cols):
@@ -293,7 +287,7 @@
 
 def rims_kernel(
     cols, x1, x2, x3, x4, got_a, got_b, side, inner, tile, s0, scale,
-    t1, t2, t3, t4, wide, wide_4, chosen, held,
+    t1, t2, t3, t4, wide, chosen, held,
 ):
     col = lax.axis_index("tx")
     step = inner[0:LANES, :].astype(f32)
@@ -309,12 +303,11 @@
 
     second = jnp.dot(masked(1), tile[0:LANES, :], preferred_element_type=f32).astype(bf16)
     high, low = halved(jnp.dot(masked(2), second, preferred_element_type=f32))
-    weights = jnp.concatenate([high, second, tile[0:LANES, :], low], 1)
+    both = jnp.concatenate([masked(3), masked(3)], 1)
+    fourth = jnp.dot(both, jnp.concatenate([high, low], 0), preferred_element_type=f32)
+    high_4, low_4 = halved(fourth)
+    weights = jnp.concatenate([high_4, high, second, tile[0:LANES, :], low_4, low], 1)
     wide[...] = jnp.concatenate([weights, weights], 0)
-    both = jnp.concatenate([masked(3), masked(3)], 1)
-    weights = jnp.dot(both, jnp.concatenate([high, low], 0), preferred_element_type=f32)
-    high, low = halved(weights)
-    wide_4[...] = jnp.concatenate([high, high, low], 0)
     for b in range(BANDS):
         total = jnp.zeros((ROWS[0], LANES), f32)
         for e in range(EXPOSURES):
@@ -336,12 +329,12 @@
             totals[level][line_of(level, at[level] + line), :] += values
 
 
-def fine_kernel(
-    s0, chosen, x1, x2, x3, x4, side, inner, tile, wide,
-    b0, b1, b2, b3, t4,
-    t1, t2, t3, held, u1, u2, u3, u4, d0, d1, d2, d3, bands,
+def finish_kernel(
+    rows, cols, s0, chosen, x1, x2, x3, x4, side, inner, tile, wide, coarse, out,
+    t1, t2, t3, t4, held, u1, u2, u3, u4, d0, d1, d2, d3, bands, c4, c3, c2, c1, spread,
 ):
-    col_odd = jnp.bitwise_and(lax.axis_index("tx"), 1) == 1
+    row, col = place_of(CORES)
+    col_odd = jnp.bitwise_and(col, 1) == 1
     totals = (None, t1, t2, t3, t4)
     add_side(totals, (None, x1, x2, x3, x4), side, jnp.logical_not(col_odd), held)
 
@@ -355,39 +348,59 @@
     values = split_dot(t1[0 : INNER * ROWS[1], :], tile[...])
     u1[...] = values.reshape(INNER, ROWS[1], LANES)
     d3[...] = jnp.zeros((INNER, ROWS[3], LANES), f32)
-    at = 0
-    for level, source, spread in ((3, u4, d3), (2, u3, d2), (1, u2, d1)):
-        expand_rows(source, spread, PAIRS[level])
+    inside = in_slab(4, row, col, rows, cols)
+    for b in range(BANDS):
+        total = coarse[INNER + b]
+        for e in range(EXPOSURES):
+            p = e * BANDS + b
+            laplace = t4[plane_of(4, p), :] - coarse[p]
+            total = total + t4[plane_of(4, INNER + e), :] * laplace
+        bands[b * ROWS[4] : (b + 1) * ROWS[4], :] = jnp.where(inside, total, 0.0)
+    bands[BANDS * ROWS[4] : PLANES // 4 * ROWS[4], :] = jnp.zeros((ROWS[4], LANES), f32)
+    at = PLANES // 4 * ROWS[4]
+    for level, source, spread_out in ((3, u4, d3), (2, u3, d2), (1, u2, d1)):
+        expand_rows(source, spread_out, PAIRS[level])
         here = totals[level]
         for b in range(BANDS):
             total = jnp.zeros((ROWS[level], LANES), f32)
             for e in range(EXPOSURES):
                 p = e * BANDS + b
-                laplace = here[plane_of(level, p), :] - spread[p]
+                laplace = here[plane_of(level, p), :] - spread_out[p]
                 total = total + here[plane_of(level, INNER + e), :] * laplace
             bands[at : at + ROWS[level], :] = total
             at += ROWS[level]
     values = split_dot(bands[...], wide[...])
-    at = 0
-    for k, level, out in ((0, 3, b3), (1, 2, b2), (2, 1, b1)):
+    at, parts = 0, {}
+    for k, level in enumerate((4, 3, 2, 1)):
         count = BANDS * ROWS[level]
         part = values[at : at + count, k * LANES : (k + 1) * LANES]
-        if level == 3:
-            part = part + values[at : at + count, 3 * LANES :]
-        out[...] = part.reshape(BANDS, ROWS[level], LANES)
-        at += count
+        if k < 2:
+            part = part + values[at : at + count, (k + 4) * LANES : (k + 5) * LANES]
+        parts[level] = part.reshape(BANDS, ROWS[level], LANES)
+        at += PLANES // 4 * ROWS[4] if level == 4 else count
+    c4[...] = parts[4]
+    for level, store in ((3, c3), (2, c2), (1, c1)):
+        store[...] = parts[level]
     expand_rows_tile(u1, d0, PAIRS[0])
     for b in range(BANDS):
         total = chosen[b]
         for e in range(EXPOSURES):
             total = total - s0[INNER + e, 8:72, :] * d0[e * BANDS + b]
-        b0[b] = total
-
-
-def collapse_kernel(
-    rows, cols, patches, b0, b1, b2, b3, t4, inner, wide_4, top_weights, out,
-    v5, window, c4, c3, c2, c1, across, spread,
-):
+        out[b] = total
+    spread[:, 0 : ROWS[3], :] = jnp.zeros((BANDS, ROWS[3], LANES), f32)
+    for level, source, target in ((3, c4, c3), (2, c3, c2), (1, c2, c1)):
+        depth = ROWS[level]
+        expand_rows(source, spread, PAIRS[level])
+        along = iota((depth, LANES), 0)
+        first, last = 1 - SIDE[level] * row, 1 + SIDE[level] * (rows - row)
+        inside = (along >= first) & (along < last)
+        for b in range(BANDS):
+            target[b] = jnp.where(inside, target[b] + spread[b, 0:depth, :], 0.0)
+    expand_rows_tile(c1, spread, PAIRS[0])
+    out[...] = out[...] + spread[...]
+
+
+def coarse_kernel(rows, cols, patches, inner, top_weights, spread, v5, window, across):
     row, col = place_of(CORES)
     total = patches[0]
     for k in range(1, rows * cols):
@@ -422,29 +435,6 @@
 
     across[:, 0:8, :] = split_dot(window[...], inner[...]).reshape(PLANES, 8, LANES)
     expand_rows(across, spread, PAIRS[4])
-    inside = in_slab(4, row, col, rows, cols)
-    for b in range(BANDS):
-        total = spread[INNER + b, 0:8, :]
-        for e in range(EXPOSURES):
-            p = e * BANDS + b
-            laplace = t4[plane_of(4, p), :] - spread[p, 0:8, :]
-            total = total + t4[plane_of(4, INNER + e), :] * laplace
-        c4[b] = jnp.where(inside, total, 0.0)
-    c4[BANDS] = jnp.zeros((8, LANES), f32)
-
-    wide = split_dot_2(c4[...].reshape(EXPOSURES * ROWS[4], LANES), wide_4[...])
-    c4[...] = wide.reshape(EXPOSURES, ROWS[4], LANES)
-    spread[0:BANDS, 0 : ROWS[3], :] = jnp.zeros((BANDS, ROWS[3], LANES), f32)
-    for level, source, target, band in ((3, c4, c3, b3), (2, c3, c2, b2), (1, c2, c1, b1)):
-        depth = ROWS[level]
-        expand_rows(source.at[0:BANDS], spread.at[0:BANDS], PAIRS[level])
-        along = iota((depth, LANES), 0)
-        first, last = 1 - SIDE[level] * row, 1 + SIDE[level] * (rows - row)
-        inside = (along >= first) & (along < last)
-        for b in range(BANDS):
-            target[b] = jnp.where(inside, band[b] + spread[b, 0:depth, :], 0.0)
-    expand_rows_tile(c1, spread.at[0:BANDS], PAIRS[0])
-    out[...] = b0[...] + spread[0:BANDS]
 
 
 VMEM = pl.BlockSpec(memory_space=pltpu.VMEM)
@@ -533,51 +523,46 @@
     patches = lax.all_to_all(patches, ("chip", "core", "tx"), 0, 0, tiled=True)
     side_a = lax.ppermute(strips[0], "tx", swaps(cols, 0))
     side_b = lax.ppermute(strips[1], "tx", swaps(cols, 1))
-    x1, x2, x3, x4, wide, wide_4, chosen = pl.pallas_call(
+    x1, x2, x3, x4, wide, chosen = pl.pallas_call(
         lambda *refs: rims_kernel(cols, *refs),
         out_shape=levels
-        + [halves(2 * LANES, 4 * LANES), halves(3 * LANES, LANES)]
+        + [halves(2 * LANES, 6 * LANES)]
         + [floats(BANDS, ROWS[0], LANES)],
         in_specs=[VMEM] * 11,
-        out_specs=[VMEM] * 7,
+        out_specs=[VMEM] * 6,
         scratch_shapes=[scratch(STRIP, LANES)],
         compiler_params=PARAMS,
         name="add_rims",
     )(x1, x2, x3, x4, got_a, got_b, side_a, inner, tile, s0, scale)
-    b0, b1, b2, b3, t4 = pl.pallas_call(
-        fine_kernel,
-        out_shape=[floats(BANDS, ROWS[level], LANES) for level in range(4)] + [levels[3]],
-        in_specs=[VMEM] * 10,
-        out_specs=[VMEM] * 5,
-        scratch_shapes=[
-            scratch(PLANES * ROWS[1], LANES),
-            scratch(PLANES * ROWS[2], LANES),
-            scratch(PLANES * ROWS[3], LANES),
-            scratch(STRIP, LANES),
-            *[scratch(INNER, ROWS[level], LANES) for level in (1, 2, 3, 4, 0, 1, 2, 3)],
-            scratch(BANDS * (ROWS[1] + ROWS[2] + ROWS[3]), LANES),
-        ],
-        compiler_params=PARAMS,
-        name="fine_laplacians",
-    )(s0, chosen, x1, x2, x3, x4, side_b, inner, tile, wide)
-    return pl.pallas_call(
-        lambda *refs: collapse_kernel(rows, cols, *refs),
-        out_shape=floats(BANDS, ROWS[0], LANES),
-        in_specs=[VMEM] * 9,
+    coarse = pl.pallas_call(
+        lambda *refs: coarse_kernel(rows, cols, *refs),
+        out_shape=floats(PLANES, ROWS[4], LANES),
+        in_specs=[VMEM] * 3,
         out_specs=VMEM,
         scratch_shapes=[
             scratch(PLANES, LANES),
             scratch(PLANES * 8, LANES),
-            scratch(EXPOSURES, ROWS[4], LANES),
-            scratch(BANDS, ROWS[3], LANES),
-            scratch(BANDS, ROWS[2], LANES),
-            scratch(BANDS, ROWS[1], LANES),
-            scratch(PLANES, ROWS[4], LANES),
-            scratch(PLANES, ROWS[0], LANES),
+            scratch(PLANES, 8, LANES),
         ],
         compiler_params=PARAMS,
-        name="collapse",
-    )(patches, b0, b1, b2, b3, t4, inner, wide_4, top)
+        name="coarse_levels",
+    )(patches, inner, top)
+    return pl.pallas_call(
+        lambda *refs: finish_kernel(rows, cols, *refs),
+        out_shape=floats(BANDS, ROWS[0], LANES),
+        in_specs=[VMEM] * 11,
+        out_specs=VMEM,
+        scratch_shapes=[
+            *[scratch(PLANES * ROWS[level], LANES) for level in (1, 2, 3, 4)],
+            scratch(STRIP, LANES),
+            *[scratch(INNER, ROWS[level], LANES) for level in (1, 2, 3, 4, 0, 1, 2, 3)],
+            scratch(PLANES // 4 * ROWS[4] + BANDS * (ROWS[1] + ROWS[2] + ROWS[3]), LANES),
+            *[scratch(BANDS, ROWS[level], LANES) for level in (4, 3, 2, 1)],
+            scratch(BANDS, ROWS[0], LANES),
+        ],
+        compiler_params=PARAMS,
+        name="finish",
+    )(s0, chosen, x1, x2, x3, x4, side_b, inner, tile, wide, coarse)
 
 
 def solution(mesh):

time: 27.2 us -> 26.8 us (0.985)
  the two profiles are of different devices: /device:TPU:368 before, /device:TPU:1 now
where the time goes in v9:
time: 26.8 us; the launch traced here: 26.5 us
  starting transfers between devices  17.7 us (66%)
  Pallas kernels  5.75 us (21%)
  waiting for transfers between devices  2.9 us (11%)
    ppermute x1, starting transfers between devices, shards(): got_a = lax.ppermute(send_a, 'core', swaps(CORES, 0))  4.94 us
    ppermute x1, starting transfers between devices, shards(): got_b = lax.ppermute(send_b, ('chip', 'core'), swaps(rows, 1))  4.51 us
    all_to_all x1, starting transfers between devices, shards(): patches = lax.all_to_all(patches, ('chip', 'core', 'tx'), 0, 0, tiled=True)  4.28 us
    ppermute x1, starting transfers between devices, shards(): side_a = lax.ppermute(strips[0], 'tx', swaps(cols, 0))  3.29 us
    pallas_call x1, Pallas kernels, shards(): pl.pallas_call(lambda *refs: partial_kernel(rows, cols, *refs), out_shape...  3.16 us
    all_to_all x1, waiting for transfers between devices, shards(): patches = lax.all_to_all(patches, ('chip', 'core', 'tx'), 0, 0, tiled=True)  1.73 us
    pallas_call x1, Pallas kernels, shards(): pl.pallas_call(lambda *refs: finish_kernel(rows, cols, *refs), out_shape=...  1.46 us
    ppermute x1, waiting for transfers between devices, shards(): side_a = lax.ppermute(strips[0], 'tx', swaps(cols, 0))  1.16 us
  transfers between devices with their start and end apart: 5, of which 2 were waited for; matrix products, arithmetic and copies ran while one was open for 0% of the time, Pallas kernels for 4%

profile of v9, /device:TPU:1, one launch (start us, length us, event | category | flops | bytes accessed | tf_op | source)
XLA Modules:
  0.0 26.5 jit_solution(6373379508140991972)
XLA Ops:
  0.0 3.2 %partial_levels.1 = (f32[16,88,128]{2,1,0:T(8,128)S(1)}, f32[12,8,128]{2,1,0:T(8,128)S(1)}, f32[640,128]{1,0:T(8,128)S(1)}, f32[384,128]{1,0:T(8,128)S(1)}, f32[...) custom-call(f32[12,64,128]{2,1,0:T(8,128)} %bitcast.1, ...), custom_call_target="tpu_custom_call" | custom-call | tf_op jit(solution)/shard_map/partial_levels/pallas_call | solution.py:468
  3.2 4.5 %collective-permute-start.1 = (f32[12,8,128]{2,1,0:T(8,128)S(1)}, f32[12,8,128]{2,1,0:T(8,128)S(1)}, u32[]{:S(2)}, u32[]{:S(2)}) collective-permute-start(f32[12,8,128]{2,1,0:T(8,128)S(1)} %get-tuple-element.33), channel_id=1, source_target_pairs={{4,8},{8,4},{12,16},{16,12},{20,24},{24,20},{5,9},{9,5},{13,17},{1... | collective-permute-start | bytes 147464 | tf_op jit(solution)/shard_map/ppermute | solution.py:504
  7.7 0.1 expand_tables.1
  7.8 4.9 %collective-permute-start = (f32[12,8,128]{2,1,0:T(8,128)S(1)}, f32[12,8,128]{2,1,0:T(8,128)S(1)}, u32[]{:S(2)}, u32[]{:S(2)}) collective-permute-start(f32[12,8,128]{2,1,0:T(8,128)S(1)} %get-tuple-element.32), channel_id=1, source_target_pairs={{0,4},{4,0},{1,5},{5,1},{2,6},{6,2},{3,7},{7,3},{8,12},{12,8},{9,1... | collective-permute-start | bytes 147464 | tf_op jit(solution)/shard_map/ppermute | solution.py:513
  12.7 4.3 %all-to-all-start = ((f32[32,8,128]{2,1,0:T(8,128)}), f32[32,8,128]{2,1,0:T(8,128)S(1)}, u32[]{:S(2)}, u32[]{:S(2)}) async-start(f32[32,8,128]{2,1,0:T(8,128)} %get-tuple-element.45), calls=%async_computation | async-start | bytes 262144 | tf_op jit(solution)/shard_map/all_to_all | solution.py:523
  17.0 0.0 collective-permute-done.1.refs_5_
  17.0 0.0 collective-permute-done.refs_4_
  17.1 3.3 %collective-permute-start.2 = (f32[6,8,128]{2,1,0:T(8,128)S(1)}, f32[6,8,128]{2,1,0:T(8,128)S(1)}, u32[]{:S(2)}, u32[]{:S(2)}) collective-permute-start(f32[6,8,128]{2,1,0:T(8,128)S(1)} %add.13), channel_id=1, source_target_pairs={{0,1},{1,0},{2,3},{3,2},{4,5},{5,4},{6,7},{7,6},{8,9},{9,8},{10,11... | collective-permute-start | bytes 73736 | tf_op jit(solution)/shard_map/ppermute | solution.py:524
  20.5 0.7 %collective-permute-start.3 = (f32[6,8,128]{2,1,0:T(8,128)S(1)}, f32[6,8,128]{2,1,0:T(8,128)S(1)}, u32[]{:S(2)}, u32[]{:S(2)}) collective-permute-start(f32[6,8,128]{2,1,0:T(8,128)S(1)} %add.15), channel_id=1, source_target_pairs={{1,2},{2,1},{5,6},{6,5},{9,10},{10,9},{13,14},{14,13},{17,18},{18,... | collective-permute-start | bytes 73736 | tf_op jit(solution)/shard_map/ppermute | solution.py:525
  21.1 1.2 %collective-permute-done.2.refs_6_ = f32[6,8,128]{2,1,0:T(8,128)S(1)} collective-permute-done((f32[6,8,128]{2,1,0:T(8,128)S(1)}, f32[6,8,128]{2,1,0:T(8,128)S(1)}, u32[]{:S(2)}, u32[]{:S(2)}) %collective-permute-start.2) | collective-permute-done | bytes 24608 | tf_op jit(solution)/shard_map/ppermute | solution.py:524
  22.3 0.6 %add_rims.1 = (f32[640,128]{1,0:T(8,128)S(1)}, f32[384,128]{1,0:T(8,128)S(1)}, f32[256,128]{1,0:T(8,128)S(1)}, f32[128,128]{1,0:T(8,128)S(1)}, bf16[256,768]{1,0:T(8,128)(2,1)S(1)}, /*index=5*/f32[3,64,128]{2,1,0:T(8,128)S(1)}) custom-call(f32[640,128]{1,0:T(8,128)S(1)} %get-tuple-element.27.refs_0_, f32[384,128]{1,0:T(8,128)S(1)} %get-tuple-element.28.refs_1_, ...), custom_call_target="tpu_custom_call" | custom-call | tf_op jit(solution)/shard_map/add_rims/pallas_call | solution.py:526
  22.9 1.7 %all-to-all-done.refs_0_ = f32[32,8,128]{2,1,0:T(8,128)S(1)} async-done(((f32[32,8,128]{2,1,0:T(8,128)}), f32[32,8,128]{2,1,0:T(8,128)S(1)}, u32[]{:S(2)}, u32[]{:S(2)}) %all-to-all-start) | async-done | bytes 131104 | tf_op jit(solution)/shard_map/all_to_all | solution.py:523
  24.6 0.5 %coarse_levels.1.refs_10_ = f32[16,8,128]{2,1,0:T(8,128)S(1)} custom-call(f32[32,8,128]{2,1,0:T(8,128)S(1)} %all-to-all-done.refs_0_, bf16[256,128]{1,0:T(8,128)(2,1)S(1)} %get-tuple-element.35.refs_7_.refs_1_, bf16[256,128]{1,0:T(8,128)(2,1)S(1)} %get-tuple-element.46.refs_2_), custom_call_target="tpu_custom_call" | custom-call | tf_op jit(solution)/shard_map/coarse_levels/pallas_call | solution.py:537
  25.1 0.0 collective-permute-done.3.refs_6_
  25.1 1.5 %finish.1 = f32[3,64,128]{2,1,0:T(8,128)} custom-call(f32[16,88,128]{2,1,0:T(8,128)S(1)} %get-tuple-element.26.refs_9_.refs_0_, f32[3,64,128]{2,1,0:T(8,128)S(1)} %get-tuple-element.38.refs_1_, f32[640,128]{1,0:T(8,128)S(1)} %get-tuple-element.39.refs_2_, f32[384,128]{1,0:T(8,128)S(1)} %get-tuple-element.40.refs_3_, ...), custom_call_target="tpu_custom_call" | custom-call | tf_op jit(solution)/shard_map/finish/pallas_call | solution.py:550
  (9 shorter events, 0.0 us)
Async XLA Ops:
  3.2 13.9 %collective-permute-start.1 = (f32[12,8,128]{2,1,0:T(8,128)S(1)}, f32[12,8,128]{2,1,0:T(8,128)S(1)}, u32[]{:S(2)}, u32[]{:S(2)}) collective-permute-start(f32[12,8,128]{2,1,0:T(8,128)S(1)} %get-tuple-element.33), channel_id=1, source_target_pairs={{4,8},{8,4},{12,16},{16,12},{20,24},{24,20},{5,9},{9,5},{13,17},{1... | collective-permute-start | bytes 147464 | tf_op jit(solution)/shard_map/ppermute | solution.py:504
  7.8 9.3 %collective-permute-start = (f32[12,8,128]{2,1,0:T(8,128)S(1)}, f32[12,8,128]{2,1,0:T(8,128)S(1)}, u32[]{:S(2)}, u32[]{:S(2)}) collective-permute-start(f32[12,8,128]{2,1,0:T(8,128)S(1)} %get-tuple-element.32), channel_id=1, source_target_pairs={{0,4},{4,0},{1,5},{5,1},{2,6},{6,2},{3,7},{7,3},{8,12},{12,8},{9,1... | collective-permute-start | bytes 147464 | tf_op jit(solution)/shard_map/ppermute | solution.py:513
  12.7 11.9 %all-to-all-start = ((f32[32,8,128]{2,1,0:T(8,128)}), f32[32,8,128]{2,1,0:T(8,128)S(1)}, u32[]{:S(2)}, u32[]{:S(2)}) async-start(f32[32,8,128]{2,1,0:T(8,128)} %get-tuple-element.45), calls=%async_computation | async-start | bytes 262144 | tf_op jit(solution)/shard_map/all_to_all | solution.py:523
  17.1 5.1 %collective-permute-start.2 = (f32[6,8,128]{2,1,0:T(8,128)S(1)}, f32[6,8,128]{2,1,0:T(8,128)S(1)}, u32[]{:S(2)}, u32[]{:S(2)}) collective-permute-start(f32[6,8,128]{2,1,0:T(8,128)S(1)} %add.13), channel_id=1, source_target_pairs={{0,1},{1,0},{2,3},{3,2},{4,5},{5,4},{6,7},{7,6},{8,9},{9,8},{10,11... | collective-permute-start | bytes 73736 | tf_op jit(solution)/shard_map/ppermute | solution.py:524
  20.5 4.6 %collective-permute-start.3 = (f32[6,8,128]{2,1,0:T(8,128)S(1)}, f32[6,8,128]{2,1,0:T(8,128)S(1)}, u32[]{:S(2)}, u32[]{:S(2)}) collective-permute-start(f32[6,8,128]{2,1,0:T(8,128)S(1)} %add.15), channel_id=1, source_target_pairs={{1,2},{2,1},{5,6},{6,5},{9,10},{10,9},{13,14},{14,13},{17,18},{18,... | collective-permute-start | bytes 73736 | tf_op jit(solution)/shard_map/ppermute | solution.py:525

commit v10 on v9

--- a/solution.py
+++ b/solution.py
@@ -180,15 +180,19 @@
     patch = patch[0:8, :] + pltpu.roll(patch[8:16, :], HALF, 1)
     width = cols + 2 * REACH_COLS
     (is_5, row_5, col_5), (is_6, row_6, col_6) = patch_places((8, LANES), 1)
+    downs = range(-REACH_ROWS, REACH_ROWS + 1)
+    overs = range(-REACH_COLS, REACH_COLS + 1)
+    rows_5 = {k: is_5 & (row_5 >= -2 * k) & (row_5 < SIDE[5] + 3 - 2 * k) for k in downs}
+    rows_6 = {k: is_6 & (row_6 >= -k) & (row_6 < SIDE[6] + 3 - k) for k in downs}
+    cols_5 = {k: (col_5 >= -4 * k) & (col_5 < WIDE[5] + 3 - 4 * k) for k in overs}
+    cols_6 = {k: (col_6 >= -2 * k) & (col_6 < WIDE[6] + 3 - 2 * k) for k in overs}
     for down in range(-REACH_ROWS, REACH_ROWS + 1):
         for over in range(-REACH_COLS, REACH_COLS + 1):
-            along, aside = row_6 + down, col_6 + 2 * over
-            held = is_6 & (along >= 0) & (along < SIDE[6] + 3) & (aside >= 0) & (aside < WIDE[6] + 3)
+            held = rows_6[down] & cols_6[over]
             away = -(PITCH_6 * down + 2 * over) % LANES
             block = jnp.where(held, pltpu.roll(patch, away, 1) if away else patch, 0.0)
             if abs(down) < REACH_ROWS and abs(over) < REACH_COLS:
-                along, aside = row_5 + 2 * down, col_5 + 4 * over
-                held = is_5 & (along >= 0) & (along < SIDE[5] + 3) & (aside >= 0) & (aside < WIDE[5] + 3)
+                held = rows_5[down] & cols_5[over]
                 away = -(2 * PITCH_5 * down + 4 * over) % LANES
                 block = jnp.where(held, pltpu.roll(patch, away, 1) if away else patch, block)
             slots[(row + (down + REACH_ROWS)) * width + col + (over + REACH_COLS)] = block

time: 26.8 us -> 26.8 us (level)
  no operation moved by 1% of the time
where the time goes in v10:
time: 26.8 us; the launch traced here: 26.5 us
  starting transfers between devices  17.7 us (66%)
  Pallas kernels  5.75 us (21%)
  waiting for transfers between devices  2.9 us (11%)
    ppermute x1, starting transfers between devices, shards(): got_a = lax.ppermute(send_a, 'core', swaps(CORES, 0))  4.94 us
    ppermute x1, starting transfers between devices, shards(): got_b = lax.ppermute(send_b, ('chip', 'core'), swaps(rows, 1))  4.51 us
    all_to_all x1, starting transfers between devices, shards(): patches = lax.all_to_all(patches, ('chip', 'core', 'tx'), 0, 0, tiled=True)  4.28 us
    ppermute x1, starting transfers between devices, shards(): side_a = lax.ppermute(strips[0], 'tx', swaps(cols, 0))  3.29 us
    pallas_call x1, Pallas kernels, shards(): pl.pallas_call(lambda *refs: partial_kernel(rows, cols, *refs), out_shape...  3.16 us
    all_to_all x1, waiting for transfers between devices, shards(): patches = lax.all_to_all(patches, ('chip', 'core', 'tx'), 0, 0, tiled=True)  1.73 us
    pallas_call x1, Pallas kernels, shards(): pl.pallas_call(lambda *refs: finish_kernel(rows, cols, *refs), out_shape=...  1.46 us
    ppermute x1, waiting for transfers between devices, shards(): side_a = lax.ppermute(strips[0], 'tx', swaps(cols, 0))  1.16 us
  transfers between devices with their start and end apart: 5, of which 2 were waited for; matrix products, arithmetic and copies ran while one was open for 0% of the time, Pallas kernels for 4%

profile of v10, /device:TPU:1, one launch (start us, length us, event | category | flops | bytes accessed | tf_op | source)
XLA Modules:
  0.0 26.5 jit_solution(9291781430377744931)
XLA Ops:
  0.0 3.2 %partial_levels.1 = (f32[16,88,128]{2,1,0:T(8,128)S(1)}, f32[12,8,128]{2,1,0:T(8,128)S(1)}, f32[640,128]{1,0:T(8,128)S(1)}, f32[384,128]{1,0:T(8,128)S(1)}, f32[...) custom-call(f32[12,64,128]{2,1,0:T(8,128)} %bitcast.1, ...), custom_call_target="tpu_custom_call" | custom-call | tf_op jit(solution)/shard_map/partial_levels/pallas_call | solution.py:472
  3.2 4.5 %collective-permute-start.1 = (f32[12,8,128]{2,1,0:T(8,128)S(1)}, f32[12,8,128]{2,1,0:T(8,128)S(1)}, u32[]{:S(2)}, u32[]{:S(2)}) collective-permute-start(f32[12,8,128]{2,1,0:T(8,128)S(1)} %get-tuple-element.33), channel_id=1, source_target_pairs={{4,8},{8,4},{12,16},{16,12},{20,24},{24,20},{5,9},{9,5},{13,17},{1... | collective-permute-start | bytes 147464 | tf_op jit(solution)/shard_map/ppermute | solution.py:508
  7.7 0.1 expand_tables.1
  7.8 4.9 %collective-permute-start = (f32[12,8,128]{2,1,0:T(8,128)S(1)}, f32[12,8,128]{2,1,0:T(8,128)S(1)}, u32[]{:S(2)}, u32[]{:S(2)}) collective-permute-start(f32[12,8,128]{2,1,0:T(8,128)S(1)} %get-tuple-element.32), channel_id=1, source_target_pairs={{0,4},{4,0},{1,5},{5,1},{2,6},{6,2},{3,7},{7,3},{8,12},{12,8},{9,1... | collective-permute-start | bytes 147464 | tf_op jit(solution)/shard_map/ppermute | solution.py:517
  12.7 4.3 %all-to-all-start = ((f32[32,8,128]{2,1,0:T(8,128)}), f32[32,8,128]{2,1,0:T(8,128)S(1)}, u32[]{:S(2)}, u32[]{:S(2)}) async-start(f32[32,8,128]{2,1,0:T(8,128)} %get-tuple-element.45), calls=%async_computation | async-start | bytes 262144 | tf_op jit(solution)/shard_map/all_to_all | solution.py:527
  17.0 0.0 collective-permute-done.1.refs_5_
  17.0 0.0 collective-permute-done.refs_4_
  17.1 3.3 %collective-permute-start.2 = (f32[6,8,128]{2,1,0:T(8,128)S(1)}, f32[6,8,128]{2,1,0:T(8,128)S(1)}, u32[]{:S(2)}, u32[]{:S(2)}) collective-permute-start(f32[6,8,128]{2,1,0:T(8,128)S(1)} %add.13), channel_id=1, source_target_pairs={{0,1},{1,0},{2,3},{3,2},{4,5},{5,4},{6,7},{7,6},{8,9},{9,8},{10,11... | collective-permute-start | bytes 73736 | tf_op jit(solution)/shard_map/ppermute | solution.py:528
  20.5 0.7 %collective-permute-start.3 = (f32[6,8,128]{2,1,0:T(8,128)S(1)}, f32[6,8,128]{2,1,0:T(8,128)S(1)}, u32[]{:S(2)}, u32[]{:S(2)}) collective-permute-start(f32[6,8,128]{2,1,0:T(8,128)S(1)} %add.15), channel_id=1, source_target_pairs={{1,2},{2,1},{5,6},{6,5},{9,10},{10,9},{13,14},{14,13},{17,18},{18,... | collective-permute-start | bytes 73736 | tf_op jit(solution)/shard_map/ppermute | solution.py:529
  21.1 1.2 %collective-permute-done.2.refs_6_ = f32[6,8,128]{2,1,0:T(8,128)S(1)} collective-permute-done((f32[6,8,128]{2,1,0:T(8,128)S(1)}, f32[6,8,128]{2,1,0:T(8,128)S(1)}, u32[]{:S(2)}, u32[]{:S(2)}) %collective-permute-start.2) | collective-permute-done | bytes 24608 | tf_op jit(solution)/shard_map/ppermute | solution.py:528
  22.3 0.6 %add_rims.1 = (f32[640,128]{1,0:T(8,128)S(1)}, f32[384,128]{1,0:T(8,128)S(1)}, f32[256,128]{1,0:T(8,128)S(1)}, f32[128,128]{1,0:T(8,128)S(1)}, bf16[256,768]{1,0:T(8,128)(2,1)S(1)}, /*index=5*/f32[3,64,128]{2,1,0:T(8,128)S(1)}) custom-call(f32[640,128]{1,0:T(8,128)S(1)} %get-tuple-element.27.refs_0_, f32[384,128]{1,0:T(8,128)S(1)} %get-tuple-element.28.refs_1_, ...), custom_call_target="tpu_custom_call" | custom-call | tf_op jit(solution)/shard_map/add_rims/pallas_call | solution.py:530
  22.9 1.7 %all-to-all-done.refs_0_ = f32[32,8,128]{2,1,0:T(8,128)S(1)} async-done(((f32[32,8,128]{2,1,0:T(8,128)}), f32[32,8,128]{2,1,0:T(8,128)S(1)}, u32[]{:S(2)}, u32[]{:S(2)}) %all-to-all-start) | async-done | bytes 131104 | tf_op jit(solution)/shard_map/all_to_all | solution.py:527
  24.6 0.5 %coarse_levels.1.refs_10_ = f32[16,8,128]{2,1,0:T(8,128)S(1)} custom-call(f32[32,8,128]{2,1,0:T(8,128)S(1)} %all-to-all-done.refs_0_, bf16[256,128]{1,0:T(8,128)(2,1)S(1)} %get-tuple-element.35.refs_7_.refs_1_, bf16[256,128]{1,0:T(8,128)(2,1)S(1)} %get-tuple-element.46.refs_2_), custom_call_target="tpu_custom_call" | custom-call | tf_op jit(solution)/shard_map/coarse_levels/pallas_call | solution.py:541
  25.1 0.0 collective-permute-done.3.refs_6_
  25.1 1.5 %finish.1 = f32[3,64,128]{2,1,0:T(8,128)} custom-call(f32[16,88,128]{2,1,0:T(8,128)S(1)} %get-tuple-element.26.refs_9_.refs_0_, f32[3,64,128]{2,1,0:T(8,128)S(1)} %get-tuple-element.38.refs_1_, f32[640,128]{1,0:T(8,128)S(1)} %get-tuple-element.39.refs_2_, f32[384,128]{1,0:T(8,128)S(1)} %get-tuple-element.40.refs_3_, ...), custom_call_target="tpu_custom_call" | custom-call | tf_op jit(solution)/shard_map/finish/pallas_call | solution.py:554
  (9 shorter events, 0.0 us)
Async XLA Ops:
  3.2 13.9 %collective-permute-start.1 = (f32[12,8,128]{2,1,0:T(8,128)S(1)}, f32[12,8,128]{2,1,0:T(8,128)S(1)}, u32[]{:S(2)}, u32[]{:S(2)}) collective-permute-start(f32[12,8,128]{2,1,0:T(8,128)S(1)} %get-tuple-element.33), channel_id=1, source_target_pairs={{4,8},{8,4},{12,16},{16,12},{20,24},{24,20},{5,9},{9,5},{13,17},{1... | collective-permute-start | bytes 147464 | tf_op jit(solution)/shard_map/ppermute | solution.py:508
  7.8 9.3 %collective-permute-start = (f32[12,8,128]{2,1,0:T(8,128)S(1)}, f32[12,8,128]{2,1,0:T(8,128)S(1)}, u32[]{:S(2)}, u32[]{:S(2)}) collective-permute-start(f32[12,8,128]{2,1,0:T(8,128)S(1)} %get-tuple-element.32), channel_id=1, source_target_pairs={{0,4},{4,0},{1,5},{5,1},{2,6},{6,2},{3,7},{7,3},{8,12},{12,8},{9,1... | collective-permute-start | bytes 147464 | tf_op jit(solution)/shard_map/ppermute | solution.py:517
  12.7 11.9 %all-to-all-start = ((f32[32,8,128]{2,1,0:T(8,128)}), f32[32,8,128]{2,1,0:T(8,128)S(1)}, u32[]{:S(2)}, u32[]{:S(2)}) async-start(f32[32,8,128]{2,1,0:T(8,128)} %get-tuple-element.45), calls=%async_computation | async-start | bytes 262144 | tf_op jit(solution)/shard_map/all_to_all | solution.py:527
  17.1 5.1 %collective-permute-start.2 = (f32[6,8,128]{2,1,0:T(8,128)S(1)}, f32[6,8,128]{2,1,0:T(8,128)S(1)}, u32[]{:S(2)}, u32[]{:S(2)}) collective-permute-start(f32[6,8,128]{2,1,0:T(8,128)S(1)} %add.13), channel_id=1, source_target_pairs={{0,1},{1,0},{2,3},{3,2},{4,5},{5,4},{6,7},{7,6},{8,9},{9,8},{10,11... | collective-permute-start | bytes 73736 | tf_op jit(solution)/shard_map/ppermute | solution.py:528
  20.5 4.6 %collective-permute-start.3 = (f32[6,8,128]{2,1,0:T(8,128)S(1)}, f32[6,8,128]{2,1,0:T(8,128)S(1)}, u32[]{:S(2)}, u32[]{:S(2)}) collective-permute-start(f32[6,8,128]{2,1,0:T(8,128)S(1)} %add.15), channel_id=1, source_target_pairs={{1,2},{2,1},{5,6},{6,5},{9,10},{10,9},{13,14},{14,13},{17,18},{18,... | collective-permute-start | bytes 73736 | tf_op jit(solution)/shard_map/ppermute | solution.py:529
